TPU v7x, 128 devices: a whole 4x4x4 slice. The times are simulated.
128 devices in a mesh: by: 8 (over x, core), bx: 16 (over y, z).
Axes of the slice: x: 4, y: 4, z: 4, core: 2. Of those that a mesh axis runs over, the one named last changes fastest.
Arguments:
- tracer_one: float32 [18, 512, 4096], P(None, 'by', 'bx'), may hold values from -6 to 6
- tracer_two: float32 [18, 512, 4096], P(None, 'by', 'bx'), may hold values from -6 to 6
- east_flow: bfloat16 [18, 512, 4096], P(None, 'by', 'bx'), may hold values from -0.3984375 to 0.3984375
- north_flow: bfloat16 [18, 512, 4096], P(None, 'by', 'bx'), may hold values from -0.3984375 to 0.3984375
- depth_levels: int32 [512, 4096], P('by', 'bx'), may hold values from 0 to 18
- side_mix: float32 [18], replicated, may hold values from 0.02 to 0.2
- vert_mix: float32 [18], replicated, may hold values from 0.01 to 0.3
- thickness: float32 [18], replicated, may hold values from 0.1 to 0.4
- corner_depth: float32 [512, 4096], P('by', 'bx'), may hold values from 0.5 to 4
- diagonal: float32 [512, 4096], P('by', 'bx'), may hold values from 0.05 to 0.5
Outputs:
- new_one: float32 [18, 512, 4096], P(None, 'by', 'bx')
- new_two: float32 [18, 512, 4096], P(None, 'by', 'bx')
- surface: float32 [512, 4096], P('by', 'bx')
All inputs are finite; a program needn't handle non-finite values.
Results may differ from a plain program's by a relative error of at most 0.0003.
Values may be sent and summed in bfloat16 or wider, within the bound.
No kernel may reach another device: no remote copies, remote signals or barrier semaphores. Data moves between devices by JAX's collectives and lax.ppermute only.
A program may use at most 192 MiB of HBM per device.

v0:
```python
import jax
import jax.numpy as jnp
from jax import lax
from jax.sharding import PartitionSpec as P

ITERS = 3


def padded_2(shard, sides, width, wrap):
    for axis, dim in sides:
        peers, length = (lax.axis_size(axis), shard.shape[dim])
        up = [(i, (i + 1) % peers) for i in range(peers if wrap else peers - 1)]
        down = [(j, i) for i, j in up]
        last = lax.slice_in_dim(shard, length - width, length, axis=dim)
        first = lax.slice_in_dim(shard, 0, width, axis=dim)
        before = lax.ppermute(last, axis, up)
        after = lax.ppermute(first, axis, down)
        shard = jnp.concatenate([before, shard, after], axis=dim)
    return shard


def horizontal(tracer_pad, east_cols, north_rows, wet_pad, side):
    left = tracer_pad[..., 1:-1, :-1]
    right = tracer_pad[..., 1:-1, 1:]
    face_east = wet_pad[..., 1:-1, :-1] * wet_pad[..., 1:-1, 1:]
    east = (east_cols * 0.5 * (left + right) - side * (right - left)) * face_east
    lower = tracer_pad[..., :-1, 1:-1]
    upper = tracer_pad[..., 1:, 1:-1]
    face_north = wet_pad[..., :-1, 1:-1] * wet_pad[..., 1:, 1:-1]
    north = (north_rows * 0.5 * (lower + upper) - side * (upper - lower)) * face_north
    return -(east[..., 1:] - east[..., :-1]) - (north[..., 1:, :] - north[..., :-1, :])


def vertical(tracers, wet, vert_mix):
    falling = vert_mix[:-1, None, None] * (tracers[:, 1:] - tracers[:, :-1]) * wet[1:]
    zeros = jnp.zeros_like(tracers[:, :1])
    padded = jnp.concatenate([zeros, falling, zeros], axis=1)
    return padded[:, 1:] - padded[:, :-1]


def corner_operator(extended, depth_ext, field, diagonal):
    cell_a = extended[:-1, :-1]
    cell_b = extended[:-1, 1:]
    cell_c = extended[1:, :-1]
    cell_d = extended[1:, 1:]
    grad_x = 0.5 * (cell_b + cell_d - (cell_a + cell_c))
    grad_y = 0.5 * (cell_c + cell_d - (cell_a + cell_b))
    flux_x = depth_ext * grad_x
    flux_y = depth_ext * grad_y
    plus = flux_x + flux_y
    minus = flux_x - flux_y
    return (
        diagonal * field
        - 0.5 * plus[1:, 1:]
        + 0.5 * minus[1:, :-1]
        - 0.5 * minus[:-1, 1:]
        + 0.5 * plus[:-1, :-1]
    )


def chron_gear(forcing, operate, totals):
    surface = jnp.zeros_like(forcing)
    residual = forcing
    image = operate(residual)
    norm_now, product = totals(residual * residual, residual * image)
    alpha = norm_now / product
    direction, along = (residual, image)
    for step in range(ITERS):
        surface = surface + alpha * direction
        residual = residual - alpha * along
        if step + 1 < ITERS:
            image = operate(residual)
            norm_next, product = totals(residual * residual, residual * image)
            ratio = norm_next / norm_now
            alpha = norm_next / (product - ratio * norm_next / alpha)
            direction = residual + ratio * direction
            along = image + ratio * along
            norm_now = norm_next
    return surface


def device_totals(first, second):
    return lax.psum((jnp.sum(first), jnp.sum(second)), ("by", "bx"))


def block_rim(field):
    widened = padded_2(field, (("bx", 1),), 1, True)
    return padded_2(widened, (("by", 0),), 1, False)


def on_device(
    tracer_one,
    tracer_two,
    east_flow,
    north_flow,
    depth_levels,
    side_mix,
    vert_mix,
    thickness,
    corner_depth,
    diagonal,
):
    levels = lax.broadcasted_iota(jnp.int32, tracer_one.shape, 0)
    wet = (levels < depth_levels[None]).astype(jnp.float32)
    tracers = jnp.stack([tracer_one, tracer_two])
    side = side_mix[:, None, None]
    stacked = jnp.stack(
        [tracer_one, tracer_two, east_flow.astype(jnp.float32), north_flow.astype(jnp.float32), wet]
    )
    widened = padded_2(stacked, (("bx", 3),), 1, True)
    padded = padded_2(widened, (("by", 2),), 1, False)
    tracer_pad = padded[0:2]
    east_cols = padded[2][:, 1:-1, :-1]
    north_rows = padded[3][:, :-1, 1:-1]
    wet_pad = padded[4]
    change = horizontal(tracer_pad, east_cols, north_rows, wet_pad, side)
    updated = wet * (tracers + change + vertical(tracers, wet, vert_mix))
    forcing = jnp.sum(thickness[:, None, None] * (updated[0] - 0.5 * updated[1]), axis=0)
    depth = corner_depth * (depth_levels > 0).astype(jnp.float32)
    depth_ext = block_rim(depth)[:-1, :-1]

    def operate(field):
        return corner_operator(block_rim(field), depth_ext, field, diagonal)

    surface = chron_gear(forcing, operate, device_totals)
    return (updated[0], updated[1], surface)


def solution(mesh):
    return jax.shard_map(
        on_device,
        mesh=mesh,
        in_specs=(
            P(None, "by", "bx"),
            P(None, "by", "bx"),
            P(None, "by", "bx"),
            P(None, "by", "bx"),
            P("by", "bx"),
            P(),
            P(),
            P(),
            P("by", "bx"),
            P("by", "bx"),
        ),
        out_specs=(P(None, "by", "bx"), P(None, "by", "bx"), P("by", "bx")),
        check_vma=False,
    )
```

profile of v0, /device:TPU:1, one launch (start us, length us, event | category | flops | bytes accessed | tf_op | source)
XLA Modules:
  0.0 407.2 jit_solution(18150655062539320579)
XLA Ops:
  0.6 1.8 copy.23
  2.5 3.5 copy.22
  6.0 3.3 constant_dynamic-update-slice_fusion.1
  10.7 1.6 copy.25
  12.3 1.6 copy.21
  13.9 1.5 constant_dynamic-update-slice_fusion
  15.7 1.7 convert_dynamic-update-slice_fusion.1
  17.4 1.6 convert_dynamic-update-slice_fusion
  19.0 1.7 convert_dynamic-update-slice_fusion.2
  21.8 7.1 %collective-permute-start.1 = (f32[5,18,64,1]{2,3,1,0:T(1,128)S(1)}, f32[5,18,64,1]{2,3,1,0:T(1,128)S(1)}, u32[]{:S(2)}, u32[]{:S(2)}) collective-permute-start(f32[5,18,64,1]{2,3,1,0:T(1,128)S(1)} %get-tuple-element.39), channel_id=1, source_target_pairs={{1,0},{2,1},{3,2},{4,3},{5,4},{6,5},{7,6},{8,7},{9,8},{10,9},{11,1... | collective-permute-start | bytes 69128 | tf_op jit(solution)/shard_map/ppermute | solution.py:17
  30.8 4.9 %collective-permute-start.5 = (f32[64,1]{0,1:T(1,128)S(1)}, f32[64,1]{0,1:T(1,128)S(1)}, u32[]{:S(2)}, u32[]{:S(2)}) collective-permute-start(f32[64,1]{0,1:T(1,128)S(1)} %get-tuple-element.59), channel_id=1, source_target_pairs={{1,0},{2,1},{3,2},{4,3},{5,4},{6,5},{7,6},{8,7},{9,8},{10,9},{11,1... | collective-permute-start | bytes 776 | tf_op jit(solution)/shard_map/ppermute | solution.py:17
  36.8 1.7 slice.316
  39.0 5.5 %pad_maximum_fusion = f32[5,18,64,258]{2,3,1,0:T(8,128)S(1)} fusion(f32[5,18,64,1]{2,3,1,0:T(1,128)S(1)} %collective-permute-done.1, f32[5,18,64,256]{2,3,1,0:T(8,128)} %convert_dynamic-update-slice_fusion.2, f32[5,18,64,1]{2,3,1,0:T(1,128)S(1)} %collective-permute-done), kind=kLoop, calls=%fused_computation | loop fusion | flops 2972160 | bytes 11888640 | tf_op jit(solution)/shard_map/concatenate | solution.py:18
  44.5 9.4 %fusion.31 = (f32[5,18,1,258]{2,3,1,0:T(8,128)}, f32[5,18,1,258]{2,3,1,0:T(8,128)}) fusion(f32[5,18,64,258]{2,3,1,0:T(8,128)S(1)} %pad_maximum_fusion), kind=kLoop, calls=%fused_computation.108 | loop fusion | bytes 371520 | tf_op jit(solution)/shard_map/slice | solution.py:15
  53.9 8.2 %copy.27 = f32[5,18,1,258]{3,2,1,0:T(1,128)S(1)} copy(f32[5,18,1,258]{2,3,1,0:T(8,128)} %get-tuple-element.37) | data formatting | bytes 185760 | tf_op jit(solution)/shard_map/slice | solution.py:14
  62.1 4.5 %collective-permute-start.2 = (f32[5,18,1,258]{3,2,1,0:T(1,128)S(1)}, f32[5,18,1,258]{3,2,1,0:T(1,128)S(1)}, u32[]{:S(2)}, u32[]{:S(2)}) collective-permute-start(f32[5,18,1,258]{3,2,1,0:T(1,128)S(1)} %copy.27), channel_id=1, source_target_pairs={{0,16},{16,32},{32,48},{48,64},{64,80},{80,96},{96,112},{1,17},{17... | collective-permute-start | bytes 278648 | tf_op jit(solution)/shard_map/ppermute | solution.py:16
  66.6 8.2 %copy.28 = f32[5,18,1,258]{3,2,1,0:T(1,128)S(1)} copy(f32[5,18,1,258]{2,3,1,0:T(8,128)} %get-tuple-element.36) | data formatting | bytes 185760 | tf_op jit(solution)/shard_map/slice | solution.py:15
  74.8 2.1 collective-permute-start.3
  76.9 5.0 %fusion.8 = f32[2,17,64,256]{2,3,1,0:T(8,128)} fusion(f32[1,18,64,256]{2,3,1,0:T(8,128)} %bitcast.31, f32[1,18,64,256]{2,3,1,0:T(8,128)S(1)} %bitcast.29, f32[17,64,256]{1,2,0:T(8,128)} %slice.316, f32[17]{0:T(128)S(1)} %bitcast.33), kind=kLoop, calls=%fused_computation.26 | loop fusion | flops 2785280 | bytes 5701700 | tf_op jit(solution)/shard_map/mul | solution.py:35
  82.0 6.7 %copy.29 = f32[5,18,1,258]{2,3,1,0:T(8,128)} copy(f32[5,18,1,258]{3,2,1,0:T(1,128)S(1)} %collective-permute-done.2) | data formatting | bytes 185760 | tf_op jit(solution)/shard_map/ppermute | solution.py:16
  88.7 6.8 %copy.30 = f32[5,18,1,258]{2,3,1,0:T(8,128)} copy(f32[5,18,1,258]{3,2,1,0:T(1,128)S(1)} %collective-permute-done.3) | data formatting | bytes 185760 | tf_op jit(solution)/shard_map/ppermute | solution.py:17
  95.5 11.1 %maximum_bitcast_fusion.1 = (f32[18,66,258]{1,2,0:T(8,128)}, f32[18,66,258]{1,2,0:T(8,128)S(1)}, f32[18,66,258]{1,2,0:T(8,128)S(1)}) fusion(f32[5,18,1,258]{2,3,1,0:T(8,128)} %copy.30, f32[5,18,1,258]{2,3,1,0:T(8,128)} %copy.29, f32[5,18,64,1]{2,3,1,0:T(1,128)S(1)} %collective-permute-done.1, f32[5,18,64,256]{2,3,1,0:T(8,128)} %convert_dynamic-update-slice_fusion.2, ...), kind=kLoop, calls=%fused_computation.36 | loop fusion | flops 3678048 | bytes 9808128 | tf_op jit(solution)/shard_map/squeeze | solution.py:113
  106.7 3.2 slice_multiply_fusion.2
  110.2 8.1 %slice_multiply_fusion = (f32[18,64,257]{1,2,0:T(8,128)}, f32[18,64,257]{1,2,0:T(8,128)}) fusion(f32[18,66,258]{1,2,0:T(8,128)} %copy-done, f32[18,66,258]{1,2,0:T(8,128)} %get-tuple-element.33), kind=kLoop, calls=%fused_computation.33 | loop fusion | flops 592128 | bytes 5921280 | tf_op jit(solution)/shard_map/mul | solution.py:25
  118.3 7.9 %subtract_multiply_fusion.1 = f32[2,18,65,256]{2,3,1,0:T(8,128)} fusion(f32[5,18,64,1]{2,3,1,0:T(1,128)S(1)} %collective-permute-done.1, f32[5,18,64,256]{2,3,1,0:T(8,128)S(1)} %bitcast.26, f32[5,18,64,1]{2,3,1,0:T(1,128)S(1)} %collective-permute-done, f32[5,18,1,258]{2,3,1,0:T(8,128)S(1)} %bitcast.28, f32[5,18,1,258]{2,3,1,0:T(8,128)} %copy.30, ...), kind=kLoop, calls=%fused_computation.22 | loop fusion | flops 7188480 | bytes 10922472 | tf_op jit(solution)/shard_map/mul | solution.py:30
  126.2 5.1 %subtract_multiply_fusion = f32[2,18,64,257]{2,3,1,0:T(8,128)} fusion(f32[5,18,64,256]{2,3,1,0:T(8,128)S(1)} %bitcast.26, f32[5,18,64,1]{2,3,1,0:T(1,128)S(1)} %collective-permute-done, f32[5,18,64,1]{2,3,1,0:T(1,128)S(1)} %collective-permute-done.1, f32[18,64,257]{1,2,0:T(8,128)} %get-tuple-element.62, f32[18]{0:T(128)S(1)} %copy-done.8, ...), kind=kLoop, calls=%fused_computation.8 | loop fusion | flops 4737024 | bytes 10681416 | tf_op jit(solution)/shard_map/mul | solution.py:26
  131.3 13.1 %fusion.2 = f32[2,18,64,256]{2,3,1,0:T(8,128)S(1)} fusion(f32[1,18,64,256]{2,3,1,0:T(8,128)} %bitcast.30, f32[1,18,64,256]{2,3,1,0:T(8,128)} %bitcast.32, f32[2,18,65,256]{2,3,1,0:T(8,128)} %subtract_multiply_fusion.1, f32[2,18,64,257]{2,3,1,0:T(8,128)} %subtract_multiply_fusion, f32[2,17,64,256]{2,3,1,0:T(8,128)} %fusion.8, f32[18,64,256]{1,2,0:T(8,128)} %copy-done.3), kind=kLoop, calls=%fused_computation.11 | loop fusion | flops 5308416 | bytes 17563648 | tf_op jit(solution)/shard_map/mul | solution.py:117
  144.4 2.1 copy-done.1
  147.1 1.5 collective-permute-start.7
  149.5 3.4 collective-permute-done.7
  153.0 1.9 collective-permute-start.10
  155.0 4.8 %collective-permute-start.9 = (f32[1,258]{0,1:T(8,128)S(1)}, f32[1,258]{0,1:T(8,128)S(1)}, u32[]{:S(2)}, u32[]{:S(2)}) collective-permute-start(f32[1,258]{0,1:T(8,128)S(1)} %get-tuple-element.47), channel_id=1, source_target_pairs={{0,16},{16,32},{32,48},{48,64},{64,80},{80,96},{96,112},{1,17},{17... | collective-permute-start | bytes 3104 | tf_op jit(solution)/shard_map/ppermute | solution.py:16
  159.9 2.4 collective-permute-start.6
  162.5 1.8 collective-permute-done.6
  165.2 63.5 %all-reduce.4 = (f32[]{:T(128)}, f32[]{:T(128)}) all-reduce(f32[]{:T(128)} %get-tuple-element.14, f32[]{:T(128)} %get-tuple-element.13), channel_id=1, replica_groups=mesh['by'=8,'bx'=16] {'by','bx'}, use_global_device_ids=true, to_apply=%region_2.0 | all-reduce | flops 2 | bytes 16 | tf_op jit(solution)/shard_map/psum | solution.py:83
  230.0 2.4 collective-permute-start.12
  233.1 5.0 %collective-permute-done.11 = f32[64,1]{0,1:T(1,128)S(1)} collective-permute-done((f32[64,1]{0,1:T(1,128)S(1)}, f32[64,1]{0,1:T(1,128)S(1)}, u32[]{:S(2)}, u32[]{:S(2)}) %collective-permute-start.11) | collective-permute-done | bytes 288 | tf_op jit(solution)/shard_map/ppermute | solution.py:16
  238.2 4.0 collective-permute-start.14
  242.3 2.9 collective-permute-start.13
  248.2 62.1 %all-reduce.3 = (f32[]{:T(128)}, f32[]{:T(128)}) all-reduce(f32[]{:T(128)} %get-tuple-element.12, f32[]{:T(128)} %get-tuple-element.11), channel_id=1, replica_groups=mesh['by'=8,'bx'=16] {'by','bx'}, use_global_device_ids=true, to_apply=%region_6.0 | all-reduce | flops 2 | bytes 16 | tf_op jit(solution)/shard_map/psum | solution.py:83
  315.1 2.3 collective-permute-start.16
  318.1 5.0 %collective-permute-done.15 = f32[64,1]{0,1:T(1,128)S(1)} collective-permute-done((f32[64,1]{0,1:T(1,128)S(1)}, f32[64,1]{0,1:T(1,128)S(1)}, u32[]{:S(2)}, u32[]{:S(2)}) %collective-permute-start.15) | collective-permute-done | bytes 288 | tf_op jit(solution)/shard_map/ppermute | solution.py:16
  323.8 4.0 collective-permute-start.18
  327.9 2.9 collective-permute-start.17
  330.8 4.2 %slice_bitcast_fusion = (f32[18,64,256]{1,2,0:T(8,128)S(1)}, f32[18,64,256]{1,2,0:T(8,128)}) fusion(f32[2,18,64,256]{2,3,1,0:T(8,128)} %copy-done.1), kind=kLoop, calls=%fused_computation.37 | loop fusion | bytes 4718592 | tf_op jit(solution)/shard_map/squeeze | solution.py:126
  335.0 2.8 copy.38
  337.8 1.7 copy.39
  340.5 62.1 %all-reduce.2 = (f32[]{:T(128)}, f32[]{:T(128)}) all-reduce(f32[]{:T(128)} %get-tuple-element.10, f32[]{:T(128)} %get-tuple-element.9), channel_id=1, replica_groups=mesh['by'=8,'bx'=16] {'by','bx'}, use_global_device_ids=true, to_apply=%region_10.0 | all-reduce | flops 2 | bytes 16 | tf_op jit(solution)/shard_map/psum | solution.py:83
  (89 shorter events, 16.4 us)
Async XLA Ops:
  2.5 74.4 %copy-start.2 = (f32[18,64,256]{1,2,0:T(8,128)}, f32[18,64,256]{1,2,0:T(8,128)S(1)}, u32[]{:S(2)}) copy-start(f32[18,64,256]{1,2,0:T(8,128)S(1)} %copy.23) | copy-start | bytes 3538948
  2.5 6.9 %copy-start.6 = (bf16[18,64,256]{2,1,0:T(8,128)(2,1)S(1)}, bf16[18,64,256]{2,1,0:T(8,128)(2,1)}, u32[]{:S(2)}) copy-start(bf16[18,64,256]{2,1,0:T(8,128)(2,1)} %param.12) | copy-start | bytes 1769476
  13.9 1.7 copy-start.4
  15.7 3.3 copy-start.5
  21.8 16.7 %collective-permute-start.1 = (f32[5,18,64,1]{2,3,1,0:T(1,128)S(1)}, f32[5,18,64,1]{2,3,1,0:T(1,128)S(1)}, u32[]{:S(2)}, u32[]{:S(2)}) collective-permute-start(f32[5,18,64,1]{2,3,1,0:T(1,128)S(1)} %get-tuple-element.39), channel_id=1, source_target_pairs={{1,0},{2,1},{3,2},{4,3},{5,4},{6,5},{7,6},{8,7},{9,8},{10,9},{11,1... | collective-permute-start | bytes 69128 | tf_op jit(solution)/shard_map/ppermute | solution.py:17
  29.0 10.0 %collective-permute-start = (f32[5,18,64,1]{2,3,1,0:T(1,128)S(1)}, f32[5,18,64,1]{2,3,1,0:T(1,128)S(1)}, u32[]{:S(2)}, u32[]{:S(2)}) collective-permute-start(f32[5,18,64,1]{2,3,1,0:T(1,128)S(1)} %get-tuple-element.38), channel_id=1, source_target_pairs={{0,1},{1,2},{2,3},{3,4},{4,5},{5,6},{6,7},{7,8},{8,9},{9,10},{10,1... | collective-permute-start | bytes 69128 | tf_op jit(solution)/shard_map/ppermute | solution.py:16
  30.8 128.9 %collective-permute-start.5 = (f32[64,1]{0,1:T(1,128)S(1)}, f32[64,1]{0,1:T(1,128)S(1)}, u32[]{:S(2)}, u32[]{:S(2)}) collective-permute-start(f32[64,1]{0,1:T(1,128)S(1)} %get-tuple-element.59), channel_id=1, source_target_pairs={{1,0},{2,1},{3,2},{4,3},{5,4},{6,5},{7,6},{8,7},{9,8},{10,9},{11,1... | collective-permute-start | bytes 776 | tf_op jit(solution)/shard_map/ppermute | solution.py:17
  36.8 2.1 copy-start.3
  62.1 19.9 %collective-permute-start.2 = (f32[5,18,1,258]{3,2,1,0:T(1,128)S(1)}, f32[5,18,1,258]{3,2,1,0:T(1,128)S(1)}, u32[]{:S(2)}, u32[]{:S(2)}) collective-permute-start(f32[5,18,1,258]{3,2,1,0:T(1,128)S(1)} %copy.27), channel_id=1, source_target_pairs={{0,16},{16,32},{32,48},{48,64},{64,80},{80,96},{96,112},{1,17},{17... | collective-permute-start | bytes 278648 | tf_op jit(solution)/shard_map/ppermute | solution.py:16
  66.6 10.3 %copy-start.9 = (f32[18]{0:T(128)S(1)}, f32[18]{0:T(128)}, u32[]{:S(2)}) copy-start(f32[18]{0:T(128)} %param.16) | copy-start | bytes 220
  74.8 13.9 %collective-permute-start.3 = (f32[5,18,1,258]{3,2,1,0:T(1,128)S(1)}, f32[5,18,1,258]{3,2,1,0:T(1,128)S(1)}, u32[]{:S(2)}, u32[]{:S(2)}) collective-permute-start(f32[5,18,1,258]{3,2,1,0:T(1,128)S(1)} %copy.28), channel_id=1, source_target_pairs={{16,0},{32,16},{48,32},{64,48},{80,64},{96,80},{112,96},{17,1},{33... | collective-permute-start | bytes 278648 | tf_op jit(solution)/shard_map/ppermute | solution.py:17
  95.5 22.8 %slice-start.3 = ((s8[12165120]{0:T(1024)(128)(4,1)}), s8[4194304]{0:T(1024)(128)(4,1)S(1)}, s32[]{:S(2)}) async-start(s8[12165120]{0:T(1024)(128)(4,1)} %bitcast.27), calls=%async_computation.3 | async-start | bytes 8388608
  95.5 22.8 %slice-start.4 = ((s8[12165120]{0:T(1024)(128)(4,1)}), s8[4194304]{0:T(1024)(128)(4,1)S(1)}, s32[]{:S(2)}) async-start(s8[12165120]{0:T(1024)(128)(4,1)} %bitcast.27), calls=%async_computation.4 | async-start | bytes 8388608
  106.6 3.6 copy-start
  106.6 11.6 %slice-start = ((s8[11796480]{0:T(1024)(128)(4,1)}), s8[4194304]{0:T(1024)(128)(4,1)S(1)}, s32[]{:S(2)}) async-start(s8[11796480]{0:T(1024)(128)(4,1)} %bitcast.25), calls=%async_computation | async-start | bytes 8388608
  106.6 11.6 %slice-start.1 = ((s8[11796480]{0:T(1024)(128)(4,1)}), s8[4194304]{0:T(1024)(128)(4,1)S(1)}, s32[]{:S(2)}) async-start(s8[11796480]{0:T(1024)(128)(4,1)} %bitcast.25), calls=%async_computation.1 | async-start | bytes 8388608
  106.6 11.6 %slice-start.5 = ((s8[12165120]{0:T(1024)(128)(4,1)}), s8[3776512]{0:T(1024)(128)(4,1)S(1)}, s32[]{:S(2)}) async-start(s8[12165120]{0:T(1024)(128)(4,1)} %bitcast.27), calls=%async_computation.5 | async-start | bytes 7553024
  110.2 8.1 %slice-start.2 = ((s8[11796480]{0:T(1024)(128)(4,1)}), s8[3407872]{0:T(1024)(128)(4,1)S(1)}, s32[]{:S(2)}) async-start(s8[11796480]{0:T(1024)(128)(4,1)} %bitcast.25), calls=%async_computation.2 | async-start | bytes 6815744
  110.2 8.1 %copy-start.8 = (f32[18]{0:T(128)S(1)}, f32[18]{0:T(128)}, u32[]{:S(2)}) copy-start(f32[18]{0:T(128)} %param.15) | copy-start | bytes 220
  131.3 15.3 %copy-start.10 = (f32[18]{0:T(128)S(1)}, f32[18]{0:T(128)}, u32[]{:S(2)}) copy-start(f32[18]{0:T(128)} %param.17) | copy-start | bytes 220
  144.4 2.2 copy-start.1
  146.6 2.1 copy-start.7
  147.0 2.5 collective-permute-start.8
  147.1 5.8 %collective-permute-start.7 = (f32[64,1]{0,1:T(1,128)S(1)}, f32[64,1]{0,1:T(1,128)S(1)}, u32[]{:S(2)}, u32[]{:S(2)}) collective-permute-start(f32[64,1]{0,1:T(1,128)S(1)} %get-tuple-element.60), channel_id=1, source_target_pairs={{0,1},{1,2},{2,3},{3,4},{4,5},{5,6},{6,7},{7,8},{8,9},{9,10},{10,1... | collective-permute-start | bytes 776 | tf_op jit(solution)/shard_map/ppermute | solution.py:16
  148.6 11.2 %collective-permute-start.4 = (f32[64,1]{0,1:T(1,128)S(1)}, f32[64,1]{0,1:T(1,128)S(1)}, u32[]{:S(2)}, u32[]{:S(2)}) collective-permute-start(f32[64,1]{0,1:T(1,128)S(1)} %get-tuple-element.58), channel_id=1, source_target_pairs={{0,1},{1,2},{2,3},{3,4},{4,5},{5,6},{6,7},{7,8},{8,9},{9,10},{10,1... | collective-permute-start | bytes 776 | tf_op jit(solution)/shard_map/ppermute | solution.py:16
  153.0 9.3 %collective-permute-start.10 = (f32[1,258]{0,1:T(8,128)S(1)}, f32[1,258]{0,1:T(8,128)S(1)}, u32[]{:S(2)}, u32[]{:S(2)}) collective-permute-start(f32[1,258]{0,1:T(8,128)S(1)} %get-tuple-element.46), channel_id=1, source_target_pairs={{16,0},{32,16},{48,32},{64,48},{80,64},{96,80},{112,96},{17,1},{33... | collective-permute-start | bytes 3104 | tf_op jit(solution)/shard_map/ppermute | solution.py:17
  155.0 7.4 %collective-permute-start.9 = (f32[1,258]{0,1:T(8,128)S(1)}, f32[1,258]{0,1:T(8,128)S(1)}, u32[]{:S(2)}, u32[]{:S(2)}) collective-permute-start(f32[1,258]{0,1:T(8,128)S(1)} %get-tuple-element.47), channel_id=1, source_target_pairs={{0,16},{16,32},{32,48},{48,64},{64,80},{80,96},{96,112},{1,17},{17... | collective-permute-start | bytes 3104 | tf_op jit(solution)/shard_map/ppermute | solution.py:16
  159.9 4.4 %collective-permute-start.6 = (f32[1,258]{0,1:T(8,128)S(1)}, f32[1,258]{0,1:T(8,128)S(1)}, u32[]{:S(2)}, u32[]{:S(2)}) collective-permute-start(f32[1,258]{0,1:T(8,128)S(1)} %pad_maximum_fusion.17), channel_id=1, source_target_pairs={{0,16},{16,32},{32,48},{48,64},{64,80},{80,96},{96,112},{1,17},{17... | collective-permute-start | bytes 3104 | tf_op jit(solution)/shard_map/ppermute | solution.py:16
  230.0 3.1 collective-permute-start.12
  232.4 5.7 %collective-permute-start.11 = (f32[64,1]{0,1:T(1,128)S(1)}, f32[64,1]{0,1:T(1,128)S(1)}, u32[]{:S(2)}, u32[]{:S(2)}) collective-permute-start(f32[64,1]{0,1:T(1,128)S(1)} %get-tuple-element.56), channel_id=1, source_target_pairs={{0,1},{1,2},{2,3},{3,4},{4,5},{5,6},{6,7},{7,8},{8,9},{9,10},{10,1... | collective-permute-start | bytes 776 | tf_op jit(solution)/shard_map/ppermute | solution.py:16
  238.2 7.7 %collective-permute-start.14 = (f32[1,258]{0,1:T(8,128)S(1)}, f32[1,258]{0,1:T(8,128)S(1)}, u32[]{:S(2)}, u32[]{:S(2)}) collective-permute-start(f32[1,258]{0,1:T(8,128)S(1)} %get-tuple-element.44), channel_id=1, source_target_pairs={{16,0},{32,16},{48,32},{64,48},{80,64},{96,80},{112,96},{17,1},{33... | collective-permute-start | bytes 3104 | tf_op jit(solution)/shard_map/ppermute | solution.py:17
  242.3 4.9 %collective-permute-start.13 = (f32[1,258]{0,1:T(8,128)S(1)}, f32[1,258]{0,1:T(8,128)S(1)}, u32[]{:S(2)}, u32[]{:S(2)}) collective-permute-start(f32[1,258]{0,1:T(8,128)S(1)} %get-tuple-element.45), channel_id=1, source_target_pairs={{0,16},{16,32},{32,48},{48,64},{64,80},{80,96},{96,112},{1,17},{17... | collective-permute-start | bytes 3104 | tf_op jit(solution)/shard_map/ppermute | solution.py:16
  315.1 3.0 collective-permute-start.16
  317.4 5.7 %collective-permute-start.15 = (f32[64,1]{0,1:T(1,128)S(1)}, f32[64,1]{0,1:T(1,128)S(1)}, u32[]{:S(2)}, u32[]{:S(2)}) collective-permute-start(f32[64,1]{0,1:T(1,128)S(1)} %get-tuple-element.54), channel_id=1, source_target_pairs={{0,1},{1,2},{2,3},{3,4},{4,5},{5,6},{6,7},{7,8},{8,9},{9,10},{10,1... | collective-permute-start | bytes 776 | tf_op jit(solution)/shard_map/ppermute | solution.py:16
  323.8 15.7 %collective-permute-start.18 = (f32[1,258]{0,1:T(8,128)}, f32[1,258]{0,1:T(8,128)S(1)}, u32[]{:S(2)}, u32[]{:S(2)}) collective-permute-start(f32[1,258]{0,1:T(8,128)} %get-tuple-element.42), channel_id=1, source_target_pairs={{16,0},{32,16},{48,32},{64,48},{80,64},{96,80},{112,96},{17,1},{33... | collective-permute-start | bytes 3104 | tf_op jit(solution)/shard_map/ppermute | solution.py:17
  327.9 11.6 %collective-permute-start.17 = (f32[1,258]{0,1:T(8,128)S(1)}, f32[1,258]{0,1:T(8,128)S(1)}, u32[]{:S(2)}, u32[]{:S(2)}) collective-permute-start(f32[1,258]{0,1:T(8,128)S(1)} %get-tuple-element.43), channel_id=1, source_target_pairs={{0,16},{16,32},{32,48},{48,64},{64,80},{80,96},{96,112},{1,17},{17... | collective-permute-start | bytes 3104 | tf_op jit(solution)/shard_map/ppermute | solution.py:16
where the time goes:
time: 408 us; the launch traced here: 407 us
  blocking collectives  188 us (46%)
  local copies, waits for them, and re-layouts  71.5 us (18%)
  other arithmetic  69.9 us (17%)
  starting transfers between devices  47.9 us (12%)
  waiting for transfers between devices  19.4 us (5%)
  between operations  10.9 us (3%)
    psum x3, blocking collectives, device_totals(): return lax.psum((jnp.sum(first), jnp.sum(second)), ('by', 'bx'))  188 us
    ppermute x9, starting transfers between devices, padded_2(): after = lax.ppermute(first, axis, down)  28.8 us
    unnamed x46, local copies, waits for them, and re-layouts  24.2 us
    ppermute x10, starting transfers between devices, padded_2(): before = lax.ppermute(last, axis, up)  19.1 us
    slice x5, local copies, waits for them, and re-layouts, padded_2(): first = lax.slice_in_dim(shard, 0, width, axis=dim)  18.5 us
    ppermute x10, waiting for transfers between devices, padded_2(): before = lax.ppermute(last, axis, up)  16.4 us
    mul x1, other arithmetic, on_device(): updated = wet * (tracers + change + vertical(tracers, wet, vert_mix))  13.1 us
    squeeze x1, other arithmetic, on_device(): east_cols = padded[2][:, 1:-1, :-1]  11.1 us
  transfers between devices with their start and end apart: 19, of which 9 were waited for; matrix products, arithmetic and copies ran while one was open for 28% of the time, Pallas kernels for 0%

commit v1 on v0

v1 whole, which is shorter than its diff:
```python
import jax
import jax.numpy as jnp
from jax import lax
from jax.experimental import pallas as pl
from jax.experimental.pallas import tpu as pltpu
from jax.sharding import PartitionSpec as P

LEV = 18
GROUP = 3
SLOT = 24
ROWS, COLS = 64, 256
WIDE = COLS + 128
TALL = ROWS + 16
F32 = jnp.float32
VMEM = pl.BlockSpec(memory_space=pltpu.VMEM)
SMEM = pl.BlockSpec(memory_space=pltpu.SMEM)
HBM = pl.BlockSpec(memory_space=pl.ANY)
PARAMS = pltpu.CompilerParams(vmem_limit_bytes=48 * 1024 * 1024)


def iota(shape, axis):
    return lax.broadcasted_iota(jnp.int32, shape, axis)


def shape(*dims):
    return jax.ShapeDtypeStruct(dims, F32)


def pairs(size, odd, wrap):
    swaps = []
    for low in range(1 if odd else 0, size, 2):
        high = low + 1
        if high == size and not wrap:
            continue
        swaps += [(low, high % size), (high % size, low)]
    return swaps


def swap_both(first, second, axis, size, wrap):
    return (
        lax.ppermute(first, axis, pairs(size, False, wrap)),
        lax.ppermute(second, axis, pairs(size, True, wrap)),
    )


def by_side(axis, first, second):
    even = lax.axis_index(axis) % 2 == 0
    return jnp.where(even, first, second), jnp.where(even, second, first)


def load_groups(sources, targets, sems):
    def copy(array, group):
        part = pl.ds(group * GROUP, GROUP)
        return pltpu.make_async_copy(sources[array].at[part], targets[array].at[part], sems.at[array, group])

    return copy


def forcing_kernel(side, vert, thick, one_hbm, two_hbm, east_hbm, north_hbm, levels, corner, diag,
                   first_out, second_out, forcing_out, edge_rows,
                   one, two, east, north, east_sum, north_sum, column, right, left, sems):
    copy = load_groups((one_hbm, two_hbm, east_hbm, north_hbm), (one, two, east, north), sems)
    groups = LEV // GROUP
    for group in range(groups):
        for array in range(4):
            copy(array, group).start()
    deep = levels[...]
    at_row, at_col = iota((ROWS, COLS), 0), iota((ROWS, COLS), 1)
    lane = iota((ROWS, 128), 1)
    east_deep = jnp.where(at_col < COLS - 1, jnp.minimum(deep, pltpu.roll(deep, COLS - 1, 1)), 0)
    north_deep = jnp.where(at_row < ROWS - 1, jnp.minimum(deep, pltpu.roll(deep, ROWS - 1, 0)), 0)
    for total in (east_sum, north_sum, column, right, left, edge_rows):
        total[...] = jnp.zeros(total.shape, F32)

    def level(k):
        c_one, c_two = one[k], two[k]
        flow_e, flow_n = east[k].astype(F32), north[k].astype(F32)
        both = c_one - 0.5 * c_two
        weight, mix = thick[k], side[k]
        below, above = jnp.minimum(k + 1, LEV - 1), jnp.maximum(k - 1, 0)
        fall = (weight - thick[below]) * vert[k]
        fall_above = (thick[above] - weight) * vert[above]
        column[...] += both * jnp.where(
            deep > k + 1, weight + fall_above - fall, jnp.where(deep > k, weight + fall_above, 0.0))
        nxt = pltpu.roll(both, COLS - 1, 1)
        east_sum[...] += jnp.where(
            east_deep > k, (0.5 * weight) * (flow_e * (both + nxt)) - (weight * mix) * (nxt - both), 0.0)
        nxt = pltpu.roll(both, ROWS - 1, 0)
        north_sum[...] += jnp.where(
            north_deep > k, (0.5 * weight) * (flow_n * (both + nxt)) - (weight * mix) * (nxt - both), 0.0)
        packed = right[...]
        packed = jnp.where(lane == k, c_one[:, COLS - 1:], packed)
        packed = jnp.where(lane == k + LEV, c_two[:, COLS - 1:], packed)
        packed = jnp.where((lane == k + 2 * LEV) | (lane == k + 3 * LEV), flow_e[:, COLS - 1:], packed)
        right[...] = packed
        packed = left[...]
        packed = jnp.where(lane == k + 64, c_one[:, :1], packed)
        packed = jnp.where(lane == k + 64 + LEV, c_two[:, :1], packed)
        left[...] = packed
        edge_rows[pl.ds(k, 1), :] = c_one[:1]
        edge_rows[pl.ds(SLOT + k, 1), :] = c_two[:1]
        edge_rows[pl.ds(2 * SLOT + k, 1), :] = c_one[ROWS - 1:]
        edge_rows[pl.ds(3 * SLOT + k, 1), :] = c_two[ROWS - 1:]
        edge_rows[pl.ds(4 * SLOT + k, 1), :] = flow_n[ROWS - 1:]

    @pl.loop(0, groups)
    def _(group):
        for array in range(4):
            copy(array, group).wait()
        for step in range(GROUP):
            level(group * GROUP + step)

    e_sum, n_sum = east_sum[...], north_sum[...]
    forcing = column[...] - (e_sum - pltpu.roll(e_sum, 1, 1)) - (n_sum - pltpu.roll(n_sum, 1, 0))
    forcing_out[...] = forcing
    depth = jnp.where(deep > 0, corner[...], 0.0)
    fields = (forcing, depth, diag[...], deep.astype(F32))
    to_right, to_left = right[...], left[...]
    for i, field in enumerate(fields):
        tile = field[:, COLS - 128:]
        tile = pltpu.roll(tile, 128 - 2 * i, 1) if i else tile
        to_right = jnp.where((lane >= 126 - 2 * i) & (lane < 128 - 2 * i), tile, to_right)
        tile = field[:, :128]
        tile = pltpu.roll(tile, 3 * i, 1) if i else tile
        to_left = jnp.where((lane >= 3 * i) & (lane < 3 * i + 3), tile, to_left)
    rows_0 = edge_rows[0:SLOT] - 0.5 * edge_rows[SLOT:2 * SLOT]
    rows_1 = edge_rows[2 * SLOT:3 * SLOT] - 0.5 * edge_rows[3 * SLOT:4 * SLOT]
    rows_2 = edge_rows[4 * SLOT:5 * SLOT]
    lane = iota((SLOT, 128), 1)
    corner_right = corner_left = jnp.zeros((SLOT, 128), F32)
    for i, rows in enumerate((rows_0, rows_1, rows_2)):
        tile = rows[:, COLS - 128:]
        tile = pltpu.roll(tile, 128 - 2 * i, 1) if i else tile
        corner_right = jnp.where((lane >= 126 - 2 * i) & (lane < 128 - 2 * i), tile, corner_right)
        tile = rows[:, :128]
        tile = pltpu.roll(tile, 3 * i, 1) if i else tile
        corner_left = jnp.where((lane >= 3 * i) & (lane < 3 * i + 3), tile, corner_left)
    even = lax.axis_index("bx") % 2 == 0
    first_out[:ROWS] = jnp.where(even, to_right, to_left)
    second_out[:ROWS] = jnp.where(even, to_left, to_right)
    first_out[ROWS:] = jnp.where(even, corner_right, corner_left)
    second_out[ROWS:] = jnp.where(even, corner_left, corner_right)


def lane_tile(from_right, from_left, i):
    lane = iota(from_right.shape, 1)
    if i:
        from_right, from_left = pltpu.roll(from_right, 128 - 3 * i, 1), pltpu.roll(from_left, 2 * i, 1)
    return jnp.where(lane < 3, from_right, jnp.where(lane >= 126, from_left, 0.0))


def columns_kernel(side, thick, first, second, first_in, second_in, forcing, levels, corner, diag, edge_rows,
                   first_out, second_out, forcing_wide, depth_wide, diag_wide, flux_left, flux_right):
    own_right, own_left = by_side("bx", first[...], second[...])
    from_right, from_left = by_side("bx", first_in[...], second_in[...])
    deep = levels[...]
    deep_f = deep.astype(F32)
    lane = iota((ROWS, 128), 1)
    at = iota((8, 128), 1)
    mix, weight = jnp.zeros((8, 128), F32), jnp.zeros((8, 128), F32)
    for k in range(LEV):
        mix = jnp.where((at == k) | (at == k + LEV), side[k], mix)
        weight = jnp.where(at == k, thick[k], jnp.where(at == k + LEV, -0.5 * thick[k], weight))
    mix, weight = mix[:1], weight[:1]
    of_lane = jnp.where(at < LEV, at, jnp.where(at < 2 * LEV, at - LEV, 100))[:1].astype(F32)

    def face(west, east, flow, west_deep, east_deep):
        flux = 0.5 * flow * (west + east) - mix * (east - west)
        flux = jnp.where(of_lane < jnp.minimum(west_deep, east_deep), flux, 0.0)
        return flux, jnp.sum(flux * weight, axis=1, keepdims=True)

    own, seen = own_left[:ROWS], from_left[:ROWS]
    flux, west_sum = face(seen, pltpu.roll(own, 64, 1), pltpu.roll(seen, 128 - 2 * LEV, 1), seen[:, 121:122], deep_f[:, :1])
    flux_left[...] = flux
    own, seen = own_right[:ROWS], from_right[:ROWS]
    flux, east_sum = face(own, pltpu.roll(seen, 64, 1), pltpu.roll(own, 128 - 2 * LEV, 1), deep_f[:, COLS - 1:], seen[:, 9:10])
    flux_right[...] = flux

    mine = forcing[...]
    tiles = (
        mine[:, :128] + jnp.where(lane == 0, west_sum, 0.0),
        mine[:, 128:] - jnp.where(lane == 127, east_sum, 0.0),
        lane_tile(from_right[:ROWS], from_left[:ROWS], 0)
        + jnp.where(lane == 0, east_sum, jnp.where(lane == 127, -west_sum, 0.0)),
    )
    wide = jnp.concatenate(tiles, axis=1)
    forcing_wide[...] = wide
    depth = jnp.where(deep > 0, corner[...], 0.0)
    depth_w = jnp.concatenate([depth, lane_tile(from_right[:ROWS], from_left[:ROWS], 1)], axis=1)
    diag_w = jnp.concatenate([diag[...], lane_tile(from_right[:ROWS], from_left[:ROWS], 2)], axis=1)
    deep_w = jnp.concatenate([deep_f, lane_tile(from_right[:ROWS], from_left[:ROWS], 3)], axis=1)
    depth_wide[...] = depth_w
    diag_wide[...] = diag_w

    def rows(value, i):
        return jnp.concatenate([value, lane_tile(from_right[ROWS:], from_left[ROWS:], i)], axis=1)

    nothing = jnp.zeros((SLOT, 128), F32)
    two_0, two_1 = edge_rows[SLOT:2 * SLOT], edge_rows[3 * SLOT:4 * SLOT]
    both_0 = rows(edge_rows[0:SLOT] - 0.5 * two_0, 0)
    both_1 = rows(edge_rows[2 * SLOT:3 * SLOT] - 0.5 * two_1, 1)
    north_1 = rows(edge_rows[4 * SLOT:5 * SLOT], 2)
    even = lax.axis_index("by") % 2 == 0
    up = (both_1, jnp.concatenate([two_1, nothing], axis=1), north_1, jnp.concatenate(
        [wide[62:64], deep_w[63:64], depth_w[62:64], diag_w[63:64], jnp.zeros((2, WIDE), F32)], axis=0))
    down = (both_0, jnp.concatenate([two_0, nothing], axis=1), jnp.zeros((SLOT, WIDE), F32), jnp.concatenate(
        [wide[0:3], deep_w[0:1], depth_w[0:2], diag_w[0:2]], axis=0))
    for i in range(4):
        place = slice(i * SLOT, i * SLOT + (SLOT if i < 3 else 8))
        first_out[place] = jnp.where(even, up[i], down[i])
        second_out[place] = jnp.where(even, down[i], up[i])


def operate(field, half_depth, diag):
    east = pltpu.roll(field, WIDE - 1, 1)
    north = pltpu.roll(field, TALL - 1, 0)
    corner = pltpu.roll(north, WIDE - 1, 1)
    plus = half_depth * (corner - field)
    minus = half_depth * (east - north)
    return (diag * field - plus + pltpu.roll(minus, 1, 1)
            + pltpu.roll(pltpu.roll(plus, 1, 1) - minus, 1, 0)), plus, minus


def solver_kernel(side, thick, first, second, first_in, second_in, forcing, depth, diag,
                  zero_out, one_out, two_out, sums_out, flux_rows):
    own_up, own_down = by_side("by", first[...], second[...])
    above, beneath = by_side("by", first_in[...], second_in[...])
    level = iota((SLOT, WIDE), 0)
    mix, weight = jnp.zeros((SLOT, WIDE), F32), jnp.zeros((SLOT, WIDE), F32)
    for k in range(LEV):
        mix = jnp.where(level == k, side[k], mix)
        weight = jnp.where(level == k, thick[k], weight)
    level_f = level.astype(F32)

    def face(south, north, south_deep, north_deep, place):
        flow = south[2 * SLOT:3 * SLOT]
        wet = level_f < jnp.minimum(south_deep, north_deep)

        def flux(low, high):
            columns = low.shape[1]
            value = 0.5 * flow[:, :columns] * (low + high) - mix[:, :columns] * (high - low)
            return jnp.where(wet[:, :columns], value, 0.0)

        both = flux(south[:SLOT], north[:SLOT])
        two = flux(south[SLOT:2 * SLOT, :COLS], north[SLOT:2 * SLOT, :COLS])
        flux_rows[place * SLOT:(place + 1) * SLOT] = both[:, :COLS] + 0.5 * two
        flux_rows[(place + 1) * SLOT:(place + 2) * SLOT] = two
        return jnp.sum(both * weight, axis=0, keepdims=True)

    top = face(own_up, above, own_up[74:75], above[75:76], 0)
    bottom = face(beneath, own_down, beneath[74:75], own_down[75:76], 2)

    def blank(count):
        return jnp.zeros((count, WIDE), F32)

    own_row = iota((ROWS, WIDE), 0)
    mine = forcing[...] + jnp.where(own_row == 0, bottom, jnp.where(own_row == ROWS - 1, -top, 0.0))
    field = jnp.concatenate([
        jnp.concatenate([blank(6), beneath[72:73], beneath[73:74] - bottom], axis=0), mine,
        jnp.concatenate([above[72:73] + top, above[73:75], blank(5)], axis=0)], axis=0)
    half_depth = 0.5 * jnp.concatenate([
        jnp.concatenate([blank(6), beneath[75:77]], axis=0), depth[...],
        jnp.concatenate([above[76:78], blank(6)], axis=0)], axis=0)
    diag_all = jnp.concatenate([
        jnp.concatenate([blank(7), beneath[77:78]], axis=0), diag[...],
        jnp.concatenate([above[78:80], blank(6)], axis=0)], axis=0)
    last = lax.axis_index("by") == lax.axis_size("by") - 1
    inside = iota((TALL, WIDE), 0) < jnp.where(last, ROWS + 8, TALL)

    image, _, _ = operate(field, half_depth, diag_all)
    image = jnp.where(inside, image, 0.0)
    twice, _, _ = operate(image, half_depth, diag_all)
    twice = jnp.where(inside, twice, 0.0)
    _, plus, minus = operate(twice, half_depth, diag_all)
    east = pltpu.roll(twice, WIDE - 1, 1)
    north = pltpu.roll(twice, TALL - 1, 0)
    corner = pltpu.roll(north, WIDE - 1, 1)
    energy = diag_all * twice * twice + plus * (corner - twice) + minus * (east - north)

    def own(value):
        return value[8:8 + ROWS, :COLS]

    v_0, v_1, v_2 = own(field), own(image), own(twice)
    zero_out[...], one_out[...], two_out[...] = v_0, v_1, v_2
    lane = iota((128, 128), 1)
    sums = jnp.zeros((128, 128), F32)
    for i, product in enumerate((v_0 * v_0, v_0 * v_1, v_1 * v_1, v_1 * v_2, v_2 * v_2, own(energy))):
        sums = jnp.where(lane == i, jnp.sum(product, keepdims=True), sums)
    sums_out[...] = sums


def surface_kernel(sums, zero, one, two, surface):
    total = jnp.sum(sums[...], axis=0, keepdims=True)
    m = [total[:, i:i + 1] for i in range(6)]
    a_0 = m[0] / m[1]
    rr_1 = m[0] - 2.0 * a_0 * m[1] + a_0 * a_0 * m[2]
    rar_1 = m[1] - 2.0 * a_0 * m[2] + a_0 * a_0 * m[3]
    b_1 = rr_1 / m[0]
    a_1 = rr_1 / (rar_1 - b_1 * rr_1 / a_0)
    grow = 1.0 + b_1
    p_1 = -(a_0 + a_1 * grow)
    p_2 = a_1 * a_0
    rr_2 = m[0] + p_1 * p_1 * m[2] + p_2 * p_2 * m[4] + 2.0 * (p_1 * m[1] + p_2 * m[2] + p_1 * p_2 * m[3])
    rar_2 = m[1] + p_1 * p_1 * m[3] + p_2 * p_2 * m[5] + 2.0 * (p_1 * m[2] + p_2 * m[3] + p_1 * p_2 * m[4])
    b_2 = rr_2 / rr_1
    a_2 = rr_2 / (rar_2 - b_2 * rr_2 / a_1)
    w_0 = a_0 + a_1 * grow + a_2 * (1.0 + b_2 * grow)
    w_1 = -a_1 * a_0 + a_2 * (p_1 - b_2 * a_0)
    w_2 = a_2 * p_2
    surface[...] = w_0 * zero[...] + w_1 * one[...] + w_2 * two[...]


def tracers_kernel(side, vert, one_hbm, two_hbm, east_hbm, north_hbm, levels, flux_left, flux_right, flux_rows,
                   one_out, two_out, one, two, east, north, new_one, new_two, sems, out_sems):
    copy = load_groups((one_hbm, two_hbm, east_hbm, north_hbm), (one, two, east, north), sems)
    groups = LEV // GROUP
    for group in range(groups):
        for array in range(4):
            copy(array, group).start()

    def store(array, group):
        part = pl.ds(group * GROUP, GROUP)
        source, target = ((new_one, one_out), (new_two, two_out))[array]
        return pltpu.make_async_copy(source.at[part], target.at[part], out_sems.at[array, group])

    deep = levels[...]
    at_row, at_col = iota((ROWS, COLS), 0), iota((ROWS, COLS), 1)
    lane = iota((ROWS, 128), 1)
    east_deep = jnp.minimum(deep, pltpu.roll(deep, COLS - 1, 1))
    north_deep = jnp.minimum(deep, pltpu.roll(deep, ROWS - 1, 0))

    def level(k):
        flow_e, flow_n = 0.5 * east[k].astype(F32), 0.5 * north[k].astype(F32)
        mix = side[k]
        below, above = jnp.minimum(k + 1, LEV - 1), jnp.maximum(k - 1, 0)
        fall_w, fall_above_w = vert[k], vert[above]
        wet, wet_below = deep > k, deep > k + 1
        wet_east, wet_north = east_deep > k, north_deep > k
        for i, (source, target) in enumerate(((one, new_one), (two, new_two))):
            c = source[k]
            nxt = pltpu.roll(c, COLS - 1, 1)
            e = jnp.where(wet_east, flow_e * (c + nxt) - mix * (nxt - c), 0.0)
            seam = pltpu.roll(flux_right[...], 127 - k - i * LEV, 1)
            e = jnp.concatenate([e[:, :128], jnp.where(lane == 127, seam, e[:, 128:])], axis=1)
            e_west = pltpu.roll(e, 1, 1)
            seam = pltpu.roll(flux_left[...], (256 - k - i * LEV) % 128, 1)
            e_west = jnp.concatenate([jnp.where(lane == 0, seam, e_west[:, :128]), e_west[:, 128:]], axis=1)
            nxt = pltpu.roll(c, ROWS - 1, 0)
            n = jnp.where(wet_north, flow_n * (c + nxt) - mix * (nxt - c), 0.0)
            n = jnp.where(at_row == ROWS - 1, flux_rows[pl.ds(i * SLOT + k, 1), :], n)
            n_south = pltpu.roll(n, 1, 0)
            n_south = jnp.where(at_row == 0, flux_rows[pl.ds((2 + i) * SLOT + k, 1), :], n_south)
            fall = jnp.where(wet_below, fall_w * (source[below] - c), 0.0)
            fall_above = fall_above_w * (c - source[above])
            target[k] = jnp.where(wet, c - (e - e_west) - (n - n_south) + (fall - fall_above), 0.0)

    for array in range(4):
        copy(array, 0).wait()

    @pl.loop(0, groups)
    def _(group):
        @pl.when(group + 1 < groups)
        def _():
            for array in range(4):
                copy(array, group + 1).wait()

        for step in range(GROUP):
            level(group * GROUP + step)
        for array in range(2):
            store(array, group).start()

    for group in range(groups):
        for array in range(2):
            store(array, group).wait()


def level_scratch():
    block = (LEV, ROWS, COLS)
    return [pltpu.VMEM(block, F32), pltpu.VMEM(block, F32), pltpu.VMEM(block, jnp.bfloat16), pltpu.VMEM(block, jnp.bfloat16)]


def cost(flops, moved):
    return pl.CostEstimate(flops=flops, bytes_accessed=moved, transcendentals=0)


def on_device(tracer_one, tracer_two, east_flow, north_flow, depth_levels, side_mix, vert_mix, thickness,
              corner_depth, diagonal):
    n_by, n_bx = lax.axis_size("by"), lax.axis_size("bx")
    cells = LEV * ROWS * COLS
    plane = shape(ROWS, COLS)
    wide = shape(ROWS, WIDE)
    column_message, row_message = shape(ROWS + SLOT, 128), shape(3 * SLOT + 8, WIDE)
    flat = pltpu.VMEM((ROWS, COLS), F32)
    tile = pltpu.VMEM((ROWS, 128), F32)
    transfers = pltpu.SemaphoreType.DMA((4, LEV // GROUP))
    first, second, forcing, edge_rows = pl.pallas_call(
        forcing_kernel,
        out_shape=(column_message, column_message, plane, shape(5 * SLOT, COLS)),
        in_specs=[SMEM] * 3 + [HBM] * 4 + [VMEM] * 3,
        out_specs=(VMEM,) * 4,
        scratch_shapes=level_scratch() + [flat] * 3 + [tile] * 2 + [transfers],
        compiler_params=PARAMS, cost_estimate=cost(30 * cells, 12 * cells), name="forcing",
    )(side_mix, vert_mix, thickness, tracer_one, tracer_two, east_flow, north_flow, depth_levels, corner_depth, diagonal)
    first_in, second_in = swap_both(first, second, "bx", n_bx, True)
    row_first, row_second, forcing, depth, diag, flux_left, flux_right = pl.pallas_call(
        columns_kernel,
        out_shape=(row_message, row_message, wide, wide, wide, shape(ROWS, 128), shape(ROWS, 128)),
        in_specs=[SMEM] * 2 + [VMEM] * 9,
        out_specs=(VMEM,) * 7,
        compiler_params=PARAMS, cost_estimate=cost(10**6, 10**6), name="columns",
    )(side_mix, thickness, first, second, first_in, second_in, forcing, depth_levels, corner_depth, diagonal, edge_rows)
    row_first_in, row_second_in = swap_both(row_first, row_second, "by", n_by, False)
    zero, one, two, sums, flux_rows = pl.pallas_call(
        solver_kernel,
        out_shape=(plane, plane, plane, shape(128, 128), shape(4 * SLOT, COLS)),
        in_specs=[SMEM] * 2 + [VMEM] * 7,
        out_specs=(VMEM,) * 5,
        compiler_params=PARAMS, cost_estimate=cost(4 * 10**6, 10**6), name="solver",
    )(side_mix, thickness, row_first, row_second, row_first_in, row_second_in, forcing, depth, diag)
    new_one, new_two = pl.pallas_call(
        tracers_kernel,
        out_shape=(shape(LEV, ROWS, COLS),) * 2,
        in_specs=[SMEM] * 2 + [HBM] * 4 + [VMEM] * 4,
        out_specs=(HBM,) * 2,
        scratch_shapes=level_scratch() + [pltpu.VMEM((LEV, ROWS, COLS), F32)] * 2
        + [transfers, pltpu.SemaphoreType.DMA((2, LEV // GROUP))],
        compiler_params=PARAMS, cost_estimate=cost(60 * cells, 20 * cells), name="tracers",
    )(side_mix, vert_mix, tracer_one, tracer_two, east_flow, north_flow, depth_levels, flux_left, flux_right, flux_rows)
    sums = lax.all_to_all(sums[:n_by * n_bx], ("by", "bx"), 0, 0, tiled=True)
    surface = pl.pallas_call(
        surface_kernel, out_shape=plane, in_specs=[VMEM] * 4, out_specs=VMEM,
        compiler_params=PARAMS, cost_estimate=cost(10**5, 10**5), name="surface",
    )(sums, zero, one, two)
    return new_one, new_two, surface


def solution(mesh):
    block, field = P(None, "by", "bx"), P("by", "bx")
    return jax.shard_map(
        on_device, mesh=mesh,
        in_specs=(block, block, block, block, field, P(), P(), P(), field, field),
        out_specs=(block, block, field), check_vma=False,
    )
```

time: 408 us -> 68.5 us (0.17)
  blocking collectives: 188 us -> 0 us
  other arithmetic: 69.9 us -> 0 us
  local copies, waits for them, and re-layouts: 71.5 us -> 19.3 us
  starting transfers between devices: 47.9 us -> 21.2 us
  Pallas kernels: 0 us -> 21.6 us
  waiting for transfers between devices: 19.4 us -> 4.7 us
  between operations: 10.9 us -> 0.83 us
    psum x3 -> x0, blocking collectives: 188 us -> none  [device_totals(): return lax.psum((jnp.sum(first), jnp.sum(second)), ('by', 'bx'))]
    mul x7 -> x0, other arithmetic: 43.3 us -> none  [the longest x1 13.1 us: on_device(): updated = wet * (tracers + change + vertical(tracers, wet, vert_mix))]
    ppermute x19 -> x4, starting transfers between devices: 47.9 us -> 12.3 us  [the longest x2 7.69 us: swap_both(): lax.ppermute(second, axis, pairs(size, True, wrap))]
    slice x12 -> x0, local copies, waits for them, and re-layouts: 29.5 us -> none  [the longest x5 18.5 us: padded_2(): first = lax.slice_in_dim(shard, 0, width, axis=dim)]
    pallas_call x0 -> x5, Pallas kernels: none -> 21.6 us  [the longest x1 10.2 us: on_device(): pl.pallas_call(tracers_kernel, out_shape=(shape(LEV, ROWS, COLS),) * 2, i...]
    ppermute x19 -> x4, waiting for transfers between devices: 19.4 us -> 4.7 us  [the longest x2 4.69 us: swap_both(): lax.ppermute(second, axis, pairs(size, True, wrap))]
    ppermute x2 -> x0, local copies, waits for them, and re-layouts: 13.5 us -> none  [the longest x1 6.8 us: padded_2(): after = lax.ppermute(first, axis, down)]
    squeeze x1 -> x0, other arithmetic: 11.1 us -> none  [on_device(): east_cols = padded[2][:, 1:-1, :-1]]
  transfers between devices with their start and end apart: 19 -> 5, of which waited for: 9 -> 2; matrix products, arithmetic and copies ran while one was open for 28% -> 0% of each run, Pallas kernels for 0% -> 15%
where the time goes in v1:
time: 68.5 us; the launch traced here: 67.7 us
  Pallas kernels  21.6 us (32%)
  starting transfers between devices  21.2 us (31%)
  local copies, waits for them, and re-layouts  19.3 us (28%)
  waiting for transfers between devices  4.7 us (7%)
  between operations  0.83 us (1%)
    unnamed x62, local copies, waits for them, and re-layouts  19.3 us
    pallas_call x1, Pallas kernels, on_device(): pl.pallas_call(tracers_kernel, out_shape=(shape(LEV, ROWS, COLS),) * 2, i...  10.2 us
    all_to_all x1, starting transfers between devices, on_device(): sums = lax.all_to_all(sums[:n_by * n_bx], ('by', 'bx'), 0, 0, tiled=True)  8.87 us
    ppermute x2, starting transfers between devices, swap_both(): lax.ppermute(second, axis, pairs(size, True, wrap))  7.69 us
    pallas_call x1, Pallas kernels, on_device(): pl.pallas_call(forcing_kernel, out_shape=(column_message, column_message,...  7.4 us
    ppermute x2, waiting for transfers between devices, swap_both(): lax.ppermute(second, axis, pairs(size, True, wrap))  4.69 us
    ppermute x2, starting transfers between devices, swap_both(): lax.ppermute(first, axis, pairs(size, False, wrap))  4.65 us
    pallas_call x1, Pallas kernels, on_device(): pl.pallas_call(surface_kernel, out_shape=plane, in_specs=[VMEM] * 4, out_...  1.92 us
  transfers between devices with their start and end apart: 5, of which 2 were waited for; matrix products, arithmetic and copies ran while one was open for 0% of the time, Pallas kernels for 15%

profile of v1, /device:TPU:1, one launch (start us, length us, event | category | flops | bytes accessed | tf_op | source)
XLA Modules:
  0.0 67.7 jit_solution(8382028530614697199)
XLA Ops:
  0.6 0.0 copy-start
  0.6 1.3 %copy-done = f32[18,64,256]{2,1,0:T(8,128)S(1)} copy-done((f32[18,64,256]{2,1,0:T(8,128)S(1)}, f32[18,64,256]{2,1,0:T(8,128)}, u32[]{:S(2)}) %copy-start) | copy-done | bytes 1179672
  1.9 1.3 %copy-done.2 = f32[18,64,256]{2,1,0:T(8,128)S(1)} copy-done((f32[18,64,256]{2,1,0:T(8,128)S(1)}, f32[18,64,256]{2,1,0:T(8,128)}, u32[]{:S(2)}) %copy-start.2) | copy-done | bytes 1179672
  3.2 1.1 %copy-done.4 = bf16[18,64,256]{2,1,0:T(8,128)(2,1)S(1)} copy-done((bf16[18,64,256]{2,1,0:T(8,128)(2,1)S(1)}, bf16[18,64,256]{2,1,0:T(8,128)(2,1)}, u32[]{:S(2)}) %copy-start.4) | copy-done | bytes 589848
  4.2 1.1 %copy-done.6 = bf16[18,64,256]{2,1,0:T(8,128)(2,1)S(1)} copy-done((bf16[18,64,256]{2,1,0:T(8,128)(2,1)S(1)}, bf16[18,64,256]{2,1,0:T(8,128)(2,1)}, u32[]{:S(2)}) %copy-start.6) | copy-done | bytes 589848
  5.3 0.8 %copy-done.8 = s32[64,256]{1,0:T(8,128)S(1)} copy-done((s32[64,256]{1,0:T(8,128)S(1)}, s32[64,256]{1,0:T(8,128)}, u32[]{:S(2)}) %copy-start.8) | copy-done | bytes 65560
  6.1 0.8 %copy-done.10 = f32[64,256]{1,0:T(8,128)S(1)} copy-done((f32[64,256]{1,0:T(8,128)S(1)}, f32[64,256]{1,0:T(8,128)}, u32[]{:S(2)}) %copy-start.10) | copy-done | bytes 65560
  7.0 0.8 %copy-done.11 = f32[64,256]{1,0:T(8,128)S(1)} copy-done((f32[64,256]{1,0:T(8,128)S(1)}, f32[64,256]{1,0:T(8,128)}, u32[]{:S(2)}) %copy-start.11) | copy-done | bytes 65560
  7.8 0.7 copy-done.25
  8.5 0.7 copy-done.27
  9.1 0.7 copy-done.29
  9.8 7.4 %forcing.1 = (f32[88,128]{1,0:T(8,128)S(1)}, f32[88,128]{1,0:T(8,128)S(1)}, f32[64,256]{1,0:T(8,128)S(1)}, f32[120,256]{1,0:T(8,128)S(1)}) custom-call(f32[18]{0:T(128)S(1)} %copy-done.25, f32[18]{0:T(128)S(1)} %copy-done.29, f32[18]{0:T(128)S(1)} %copy-done.27, f32[18,64,256]{2,1,0:T(8,128)S(1)} %copy-done, f32[18,64,256]{2,1,0:T(8,128)S(1)} %copy-done.2, ...), custom_call_target="tpu_custom_call" | custom-call | flops 8847360 | bytes 3538944 | tf_op jit(solution)/shard_map/forcing/pallas_call | solution.py:396
  17.2 0.0 copy-start.1
  17.2 0.0 copy-start.30
  17.2 2.5 %collective-permute-start = (f32[88,128]{1,0:T(8,128)S(1)}, f32[88,128]{1,0:T(8,128)S(1)}, u32[]{:S(2)}, u32[]{:S(2)}) collective-permute-start(f32[88,128]{1,0:T(8,128)S(1)} %get-tuple-element.21.first), channel_id=1, source_target_pairs={{0,1},{1,0},{2,3},{3,2},{4,5},{5,4},{6,7},{7,6},{8,9},{9,8},{10,11... | collective-permute-start | bytes 135176 | tf_op jit(solution)/shard_map/ppermute | solution.py:41
  19.8 4.7 %collective-permute-start.1 = (f32[88,128]{1,0:T(8,128)S(1)}, f32[88,128]{1,0:T(8,128)S(1)}, u32[]{:S(2)}, u32[]{:S(2)}) collective-permute-start(f32[88,128]{1,0:T(8,128)S(1)} %get-tuple-element.22.second), channel_id=1, source_target_pairs={{1,2},{2,1},{3,4},{4,3},{5,6},{6,5},{7,8},{8,7},{9,10},{10,9},{11,... | collective-permute-start | bytes 135176 | tf_op jit(solution)/shard_map/ppermute | solution.py:42
  24.5 0.0 collective-permute-done.first_in
  24.5 1.5 %collective-permute-done.1.second_in = f32[88,128]{1,0:T(8,128)S(1)} collective-permute-done((f32[88,128]{1,0:T(8,128)S(1)}, f32[88,128]{1,0:T(8,128)S(1)}, u32[]{:S(2)}, u32[]{:S(2)}) %collective-permute-start.1) | collective-permute-done | bytes 45088 | tf_op jit(solution)/shard_map/ppermute | solution.py:42
  26.0 0.0 copy-done.28
  26.0 0.8 %columns.1 = (f32[80,384]{1,0:T(8,128)S(1)}, f32[80,384]{1,0:T(8,128)S(1)}, f32[64,384]{1,0:T(8,128)S(1)}, f32[64,384]{1,0:T(8,128)S(1)}, f32[64,384]{1,0:T(8,12...) custom-call(f32[18]{0:T(128)S(1)} %copy-done.26, f32[18]{0:T(128)S(1)} %copy-done.28, ...), custom_call_target="tpu_custom_call" | custom-call | flops 1000000 | bytes 1000000 | tf_op jit(solution)/shard_map/columns/pallas_call | solution.py:405
  26.9 0.0 copy-start.21
  26.9 0.6 copy-done.21
  27.5 0.6 copy-done.23
  28.1 2.1 %collective-permute-start.2 = (f32[80,384]{1,0:T(8,128)S(1)}, f32[80,384]{1,0:T(8,128)S(1)}, u32[]{:S(2)}, u32[]{:S(2)}) collective-permute-start(f32[80,384]{1,0:T(8,128)S(1)} %get-tuple-element.27.first), channel_id=1, source_target_pairs={{0,16},{16,0},{32,48},{48,32},{64,80},{80,64},{96,112},{112,96},{1... | collective-permute-start | bytes 368648 | tf_op jit(solution)/shard_map/ppermute | solution.py:41
  30.2 3.0 %collective-permute-start.3 = (f32[80,384]{1,0:T(8,128)S(1)}, f32[80,384]{1,0:T(8,128)S(1)}, u32[]{:S(2)}, u32[]{:S(2)}) collective-permute-start(f32[80,384]{1,0:T(8,128)S(1)} %get-tuple-element.28.second), channel_id=1, source_target_pairs={{16,32},{32,16},{48,64},{64,48},{80,96},{96,80},{17,33},{33,17},{4... | collective-permute-start | bytes 368648 | tf_op jit(solution)/shard_map/ppermute | solution.py:42
  33.2 0.0 collective-permute-done.2.first_in
  33.2 3.2 %collective-permute-done.3.second_in = f32[80,384]{1,0:T(8,128)S(1)} collective-permute-done((f32[80,384]{1,0:T(8,128)S(1)}, f32[80,384]{1,0:T(8,128)S(1)}, u32[]{:S(2)}, u32[]{:S(2)}) %collective-permute-start.3) | collective-permute-done | bytes 122912 | tf_op jit(solution)/shard_map/ppermute | solution.py:42
  36.4 1.3 %solver.1 = (f32[64,256]{1,0:T(8,128)S(1)}, f32[64,256]{1,0:T(8,128)S(1)}, f32[64,256]{1,0:T(8,128)S(1)}, f32[128,128]{1,0:T(8,128)S(1)}, f32[96,256]{1,0:T(8,128)S(1)}) custom-call(f32[18]{0:T(128)S(1)} %copy-done.26, f32[18]{0:T(128)S(1)} %copy-done.28, f32[80,384]{1,0:T(8,128)S(1)} %get-tuple-element.27.first, f32[80,384]{1,0:T(8,128)S(1)} %get-tuple-element.28.second, ...), custom_call_target="tpu_custom_call" | custom-call | flops 4000000 | bytes 1000000 | tf_op jit(solution)/shard_map/solver/pallas_call | solution.py:413
  37.7 0.0 copy-start.12
  37.7 0.6 copy-done.12
  38.3 0.6 copy-done.14
  38.9 0.6 copy-done.16
  39.6 0.6 copy-done.18
  40.2 0.6 copy-done.20
  40.8 8.9 %all-to-all-start = ((f32[128,1,128]{2,1,0:T(1,128)}), f32[128,1,128]{2,1,0:T(1,128)}, u32[]{:S(2)}, u32[]{:S(2)}) async-start(f32[128,1,128]{2,1,0:T(1,128)} %bitcast.4), calls=%async_computation | async-start | bytes 131072 | tf_op jit(solution)/shard_map/all_to_all | solution.py:429
  49.7 0.0 copy-done.3
  49.7 0.0 copy-done.5
  49.7 0.0 copy-start.9
  49.8 0.8 %copy-done.9 = s32[64,256]{1,0:T(8,128)S(1)} copy-done((s32[64,256]{1,0:T(8,128)S(1)}, s32[64,256]{1,0:T(8,128)}, u32[]{:S(2)}) %copy-start.9) | copy-done | bytes 65560
  50.6 0.9 %copy-done.13 = f32[96,256]{1,0:T(8,128)S(1)} copy-done((f32[96,256]{1,0:T(8,128)S(1)}, f32[96,256]{1,0:T(8,128)}, u32[]{:S(2)}) %copy-start.13) | copy-done | bytes 98328
  51.5 0.8 %copy-done.22 = f32[64,128]{1,0:T(8,128)S(1)} copy-done((f32[64,128]{1,0:T(8,128)S(1)}, f32[64,128]{1,0:T(8,128)}, u32[]{:S(2)}) %copy-start.22) | copy-done | bytes 32792
  52.2 0.8 %copy-done.24 = f32[64,128]{1,0:T(8,128)S(1)} copy-done((f32[64,128]{1,0:T(8,128)S(1)}, f32[64,128]{1,0:T(8,128)}, u32[]{:S(2)}) %copy-start.24) | copy-done | bytes 32792
  53.0 10.2 %tracers.1 = (f32[18,64,256]{2,1,0:T(8,128)}, f32[18,64,256]{2,1,0:T(8,128)}) custom-call(f32[18]{0:T(128)S(1)} %copy-done.26, f32[18]{0:T(128)S(1)} %copy-done.30, f32[18,64,256]{2,1,0:T(8,128)S(1)} %copy-done.1, f32[18,64,256]{2,1,0:T(8,128)S(1)} %copy-done.3, bf16[18,64,256]{2,1,0:T(8,128)(2,1)S(1)} %copy-done.5, bf16[18,64,256]{2,1,0:T(8,128)(2,1)S(1)} %copy-done.7, ...), custom_call_target="tpu_custom_call" | custom-call | flops 17694720 | bytes 5898240 | tf_op jit(solution)/shard_map/tracers/pallas_call | solution.py:420
  63.2 0.0 all-to-all-done
  63.2 0.8 %copy-done.15 = f32[64,256]{1,0:T(8,128)S(1)} copy-done((f32[64,256]{1,0:T(8,128)S(1)}, f32[64,256]{1,0:T(8,128)}, u32[]{:S(2)}) %copy-start.15) | copy-done | bytes 65560
  64.1 0.8 %copy-done.17 = f32[64,256]{1,0:T(8,128)S(1)} copy-done((f32[64,256]{1,0:T(8,128)S(1)}, f32[64,256]{1,0:T(8,128)}, u32[]{:S(2)}) %copy-start.17) | copy-done | bytes 65560
  64.9 0.8 %copy-done.19 = f32[64,256]{1,0:T(8,128)S(1)} copy-done((f32[64,256]{1,0:T(8,128)S(1)}, f32[64,256]{1,0:T(8,128)}, u32[]{:S(2)}) %copy-start.19) | copy-done | bytes 65560
  65.7 1.9 %surface.1 = f32[64,256]{1,0:T(8,128)} custom-call(f32[128,128]{1,0:T(8,128)} %bitcast.2.sums, f32[64,256]{1,0:T(8,128)S(1)} %copy-done.15, f32[64,256]{1,0:T(8,128)S(1)} %copy-done.17, f32[64,256]{1,0:T(8,128)S(1)} %copy-done.19), custom_call_target="tpu_custom_call" | custom-call | flops 100000 | bytes 100000 | tf_op jit(solution)/shard_map/surface/pallas_call | solution.py:430
  (29 shorter events, 0.0 us)
Async XLA Ops:
  0.6 1.3 %copy-start = (f32[18,64,256]{2,1,0:T(8,128)S(1)}, f32[18,64,256]{2,1,0:T(8,128)}, u32[]{:S(2)}) copy-start(f32[18,64,256]{2,1,0:T(8,128)} %one_hbm.3) | copy-start | bytes 3538948
  1.9 1.3 %copy-start.2 = (f32[18,64,256]{2,1,0:T(8,128)S(1)}, f32[18,64,256]{2,1,0:T(8,128)}, u32[]{:S(2)}) copy-start(f32[18,64,256]{2,1,0:T(8,128)} %two_hbm.3) | copy-start | bytes 3538948
  3.2 1.1 %copy-start.4 = (bf16[18,64,256]{2,1,0:T(8,128)(2,1)S(1)}, bf16[18,64,256]{2,1,0:T(8,128)(2,1)}, u32[]{:S(2)}) copy-start(bf16[18,64,256]{2,1,0:T(8,128)(2,1)} %east_hbm.3) | copy-start | bytes 1769476
  4.2 1.1 %copy-start.6 = (bf16[18,64,256]{2,1,0:T(8,128)(2,1)S(1)}, bf16[18,64,256]{2,1,0:T(8,128)(2,1)}, u32[]{:S(2)}) copy-start(bf16[18,64,256]{2,1,0:T(8,128)(2,1)} %north_hbm.3) | copy-start | bytes 1769476
  5.3 0.8 %copy-start.8 = (s32[64,256]{1,0:T(8,128)S(1)}, s32[64,256]{1,0:T(8,128)}, u32[]{:S(2)}) copy-start(s32[64,256]{1,0:T(8,128)} %levels.5) | copy-start | bytes 196612
  6.1 0.8 %copy-start.10 = (f32[64,256]{1,0:T(8,128)S(1)}, f32[64,256]{1,0:T(8,128)}, u32[]{:S(2)}) copy-start(f32[64,256]{1,0:T(8,128)} %corner.3) | copy-start | bytes 196612
  7.0 0.8 %copy-start.11 = (f32[64,256]{1,0:T(8,128)S(1)}, f32[64,256]{1,0:T(8,128)}, u32[]{:S(2)}) copy-start(f32[64,256]{1,0:T(8,128)} %diag.3) | copy-start | bytes 196612
  7.8 0.7 copy-start.25
  8.5 0.7 copy-start.27
  9.1 0.7 copy-start.29
  9.8 16.2 %copy-start.26 = (f32[18]{0:T(128)S(1)}, f32[18]{0:T(128)}, u32[]{:S(2)}) copy-start(f32[18]{0:T(128)} %side.7) | copy-start | bytes 220
  9.8 16.2 %copy-start.28 = (f32[18]{0:T(128)S(1)}, f32[18]{0:T(128)}, u32[]{:S(2)}) copy-start(f32[18]{0:T(128)} %thick.5) | copy-start | bytes 220
  9.8 39.9 %copy-start.3 = (f32[18,64,256]{2,1,0:T(8,128)S(1)}, f32[18,64,256]{2,1,0:T(8,128)}, u32[]{:S(2)}) copy-start(f32[18,64,256]{2,1,0:T(8,128)} %two_hbm.3) | copy-start | bytes 3538948
  9.8 39.9 %copy-start.5 = (bf16[18,64,256]{2,1,0:T(8,128)(2,1)S(1)}, bf16[18,64,256]{2,1,0:T(8,128)(2,1)}, u32[]{:S(2)}) copy-start(bf16[18,64,256]{2,1,0:T(8,128)(2,1)} %east_hbm.3) | copy-start | bytes 1769476
  9.8 39.9 %copy-start.7 = (bf16[18,64,256]{2,1,0:T(8,128)(2,1)S(1)}, bf16[18,64,256]{2,1,0:T(8,128)(2,1)}, u32[]{:S(2)}) copy-start(bf16[18,64,256]{2,1,0:T(8,128)(2,1)} %north_hbm.3) | copy-start | bytes 1769476
  17.2 32.5 %copy-start.1 = (f32[18,64,256]{2,1,0:T(8,128)S(1)}, f32[18,64,256]{2,1,0:T(8,128)}, u32[]{:S(2)}) copy-start(f32[18,64,256]{2,1,0:T(8,128)} %one_hbm.3) | copy-start | bytes 3538948
  17.2 32.5 %copy-start.30 = (f32[18]{0:T(128)S(1)}, f32[18]{0:T(128)}, u32[]{:S(2)}) copy-start(f32[18]{0:T(128)} %vert.3) | copy-start | bytes 220
  17.2 7.2 %collective-permute-start = (f32[88,128]{1,0:T(8,128)S(1)}, f32[88,128]{1,0:T(8,128)S(1)}, u32[]{:S(2)}, u32[]{:S(2)}) collective-permute-start(f32[88,128]{1,0:T(8,128)S(1)} %get-tuple-element.21.first), channel_id=1, source_target_pairs={{0,1},{1,0},{2,3},{3,2},{4,5},{5,4},{6,7},{7,6},{8,9},{9,8},{10,11... | collective-permute-start | bytes 135176 | tf_op jit(solution)/shard_map/ppermute | solution.py:41
  19.8 6.2 %collective-permute-start.1 = (f32[88,128]{1,0:T(8,128)S(1)}, f32[88,128]{1,0:T(8,128)S(1)}, u32[]{:S(2)}, u32[]{:S(2)}) collective-permute-start(f32[88,128]{1,0:T(8,128)S(1)} %get-tuple-element.22.second), channel_id=1, source_target_pairs={{1,2},{2,1},{3,4},{4,3},{5,6},{6,5},{7,8},{8,7},{9,10},{10,9},{11,... | collective-permute-start | bytes 135176 | tf_op jit(solution)/shard_map/ppermute | solution.py:42
  26.9 0.6 copy-start.21
  27.5 0.6 copy-start.23
  28.1 5.1 %collective-permute-start.2 = (f32[80,384]{1,0:T(8,128)S(1)}, f32[80,384]{1,0:T(8,128)S(1)}, u32[]{:S(2)}, u32[]{:S(2)}) collective-permute-start(f32[80,384]{1,0:T(8,128)S(1)} %get-tuple-element.27.first), channel_id=1, source_target_pairs={{0,16},{16,0},{32,48},{48,32},{64,80},{80,64},{96,112},{112,96},{1... | collective-permute-start | bytes 368648 | tf_op jit(solution)/shard_map/ppermute | solution.py:41
  30.2 6.2 %collective-permute-start.3 = (f32[80,384]{1,0:T(8,128)S(1)}, f32[80,384]{1,0:T(8,128)S(1)}, u32[]{:S(2)}, u32[]{:S(2)}) collective-permute-start(f32[80,384]{1,0:T(8,128)S(1)} %get-tuple-element.28.second), channel_id=1, source_target_pairs={{16,32},{32,16},{48,64},{64,48},{80,96},{96,80},{17,33},{33,17},{4... | collective-permute-start | bytes 368648 | tf_op jit(solution)/shard_map/ppermute | solution.py:42
  37.7 0.6 copy-start.12
  38.3 0.6 copy-start.14
  38.9 0.6 copy-start.16
  39.6 0.6 copy-start.18
  40.2 0.6 copy-start.20
  40.8 22.4 %all-to-all-start = ((f32[128,1,128]{2,1,0:T(1,128)}), f32[128,1,128]{2,1,0:T(1,128)}, u32[]{:S(2)}, u32[]{:S(2)}) async-start(f32[128,1,128]{2,1,0:T(1,128)} %bitcast.4), calls=%async_computation | async-start | bytes 131072 | tf_op jit(solution)/shard_map/all_to_all | solution.py:429
  49.7 0.8 %copy-start.9 = (s32[64,256]{1,0:T(8,128)S(1)}, s32[64,256]{1,0:T(8,128)}, u32[]{:S(2)}) copy-start(s32[64,256]{1,0:T(8,128)} %levels.5) | copy-start | bytes 196612
  50.6 0.9 %copy-start.13 = (f32[96,256]{1,0:T(8,128)S(1)}, f32[96,256]{1,0:T(8,128)}, u32[]{:S(2)}) copy-start(f32[96,256]{1,0:T(8,128)} %copy-done.12) | copy-start | bytes 294916
  51.5 0.8 %copy-start.22 = (f32[64,128]{1,0:T(8,128)S(1)}, f32[64,128]{1,0:T(8,128)}, u32[]{:S(2)}) copy-start(f32[64,128]{1,0:T(8,128)} %copy-done.21) | copy-start | bytes 98308
  52.2 0.8 %copy-start.24 = (f32[64,128]{1,0:T(8,128)S(1)}, f32[64,128]{1,0:T(8,128)}, u32[]{:S(2)}) copy-start(f32[64,128]{1,0:T(8,128)} %copy-done.23) | copy-start | bytes 98308
  63.2 0.8 %copy-start.15 = (f32[64,256]{1,0:T(8,128)S(1)}, f32[64,256]{1,0:T(8,128)}, u32[]{:S(2)}) copy-start(f32[64,256]{1,0:T(8,128)} %copy-done.14) | copy-start | bytes 196612
  64.1 0.8 %copy-start.17 = (f32[64,256]{1,0:T(8,128)S(1)}, f32[64,256]{1,0:T(8,128)}, u32[]{:S(2)}) copy-start(f32[64,256]{1,0:T(8,128)} %copy-done.16) | copy-start | bytes 196612
  64.9 0.8 %copy-start.19 = (f32[64,256]{1,0:T(8,128)S(1)}, f32[64,256]{1,0:T(8,128)}, u32[]{:S(2)}) copy-start(f32[64,256]{1,0:T(8,128)} %copy-done.18) | copy-start | bytes 196612

commit v2 on v1

v2 whole, which is shorter than its diff:
```python
import jax
import jax.numpy as jnp
from jax import lax
from jax.experimental import pallas as pl
from jax.experimental.pallas import tpu as pltpu
from jax.sharding import PartitionSpec as P

LEV = 18
CHUNK = 16
SLOT = 24
ROWS, COLS = 64, 256
WIDE = COLS + 128
TALL = ROWS + 16
F32 = jnp.float32
VMEM = pl.BlockSpec(memory_space=pltpu.VMEM)
SMEM = pl.BlockSpec(memory_space=pltpu.SMEM)
HBM = pl.BlockSpec(memory_space=pl.ANY)
PARAMS = pltpu.CompilerParams(vmem_limit_bytes=16 * 1024 * 1024)


def iota(shape, axis):
    return lax.broadcasted_iota(jnp.int32, shape, axis)


def shape(*dims):
    return jax.ShapeDtypeStruct(dims, F32)


def pairs(size, odd, wrap):
    swaps = []
    for low in range(1 if odd else 0, size, 2):
        high = low + 1
        if high == size and not wrap:
            continue
        swaps += [(low, high % size), (high % size, low)]
    return swaps


def swap_both(first, second, axis, size, wrap):
    return (
        lax.ppermute(first, axis, pairs(size, False, wrap)),
        lax.ppermute(second, axis, pairs(size, True, wrap)),
    )


def by_side(axis, first, second):
    even = lax.axis_index(axis) % 2 == 0
    return jnp.where(even, first, second), jnp.where(even, second, first)


def load_chunks(sources, targets, sems):
    def copy(array, chunk):
        part = pl.ds(pl.multiple_of(chunk * CHUNK, CHUNK), CHUNK)
        return pltpu.make_async_copy(sources[array].at[:, part], targets[array].at[:, part], sems.at[array, chunk])

    return copy


def start_all(copies):
    for copy in copies:
        copy.start()


def wait_all(copies):
    for copy in copies:
        copy.wait()


def forcing_kernel(side_hbm, vert_hbm, thick_hbm, one_hbm, two_hbm, east_hbm, north_hbm, levels_hbm, corner_hbm, diag_hbm,
                   first_out, second_out, forcing_out, deep_out, depth_out, diag_out, edge_rows, weights,
                   side, vert, thick, one, two, east, north,
                   levels, corner, diag, east_deep, north_deep, east_sum, north_sum, column, right, left, sems, small):
    copy = load_chunks((one_hbm, two_hbm, east_hbm, north_hbm), (one, two, east, north), sems)
    chunks = ROWS // CHUNK
    pairs_of = ((levels_hbm, levels), (side_hbm, side), (vert_hbm, vert), (thick_hbm, thick), (corner_hbm, corner), (diag_hbm, diag))
    singles = [pltpu.make_async_copy(a, b, small.at[i]) for i, (a, b) in enumerate(pairs_of)]
    start_all(singles[:4])
    for chunk in range(chunks):
        start_all(copy(array, chunk) for array in range(4))
    start_all(singles[4:])
    wait_all(singles[:4])
    deep = levels[...]
    at_row, at_col = iota((ROWS, COLS), 0), iota((ROWS, COLS), 1)
    east_deep[...] = jnp.where(at_col < COLS - 1, jnp.minimum(deep, pltpu.roll(deep, COLS - 1, 1)), 0)
    north_deep[...] = jnp.where(at_row < ROWS - 1, jnp.minimum(deep, pltpu.roll(deep, ROWS - 1, 0)), 0)
    edge_rows[...] = jnp.zeros(edge_rows.shape, F32)
    row, lane = iota((CHUNK, COLS), 0), iota((CHUNK, 128), 1)
    wait_all(copy(array, 0) for array in range(4))

    @pl.loop(0, chunks)
    def _(chunk):
        @pl.when(chunk + 1 < chunks)
        def _():
            wait_all(copy(array, chunk + 1) for array in range(4))

        start = pl.multiple_of(chunk * CHUNK, CHUNK)
        part = pl.ds(start, CHUNK)
        here, to_east, to_north = levels[part], east_deep[part], north_deep[part]

        def level(k, carry):
            e_sum, n_sum, total, to_right, to_left = carry
            c_one, c_two = one[k, part], two[k, part]
            flow_e, flow_n = east[k, part].astype(F32), north[k, part].astype(F32)
            both = c_one - 0.5 * c_two
            beyond = one[k, pl.ds(start + CHUNK, 1)] - 0.5 * two[k, pl.ds(start + CHUNK, 1)]
            weight, mix = thick[k], side[k]
            below, above = jnp.minimum(k + 1, LEV - 1), jnp.maximum(k - 1, 0)
            fall = (weight - thick[below]) * vert[k]
            fall_above = (thick[above] - weight) * vert[above]
            total = total + both * jnp.where(
                here > k + 1, weight + fall_above - fall, jnp.where(here > k, weight + fall_above, 0.0))
            nxt = pltpu.roll(both, COLS - 1, 1)
            e_sum = e_sum + jnp.where(
                to_east > k, (0.5 * weight) * (flow_e * (both + nxt)) - (weight * mix) * (nxt - both), 0.0)
            nxt = jnp.where(row == CHUNK - 1, beyond, pltpu.roll(both, CHUNK - 1, 0))
            n_sum = n_sum + jnp.where(
                to_north > k, (0.5 * weight) * (flow_n * (both + nxt)) - (weight * mix) * (nxt - both), 0.0)
            to_right = jnp.where(lane == k, c_one[:, COLS - 1:], to_right)
            to_right = jnp.where(lane == k + LEV, c_two[:, COLS - 1:], to_right)
            to_right = jnp.where((lane == k + 2 * LEV) | (lane == k + 3 * LEV), flow_e[:, COLS - 1:], to_right)
            to_left = jnp.where(lane == k + 64, c_one[:, :1], to_left)
            to_left = jnp.where(lane == k + 64 + LEV, c_two[:, :1], to_left)
            return e_sum, n_sum, total, to_right, to_left

        flat, tile = jnp.zeros((CHUNK, COLS), F32), jnp.zeros((CHUNK, 128), F32)
        result = lax.fori_loop(0, LEV, level, (flat, flat, flat, tile, tile), unroll=3)
        for target, value in zip((east_sum, north_sum, column, right, left), result):
            target[part] = value

    @pl.loop(0, LEV)
    def _(k):
        edge_rows[pl.ds(k, 1)] = one[k, 0:1]
        edge_rows[pl.ds(SLOT + k, 1)] = two[k, 0:1]
        edge_rows[pl.ds(2 * SLOT + k, 1)] = one[k, ROWS - 1:ROWS]
        edge_rows[pl.ds(3 * SLOT + k, 1)] = two[k, ROWS - 1:ROWS]
        edge_rows[pl.ds(4 * SLOT + k, 1)] = north[k, ROWS - CHUNK:ROWS].astype(F32)[CHUNK - 1:]

    at, level = iota((8, 128), 1), iota((SLOT, 128), 0)
    lane_mix = lane_weight = jnp.zeros((8, 128), F32)
    row_mix = row_weight = jnp.zeros((SLOT, 128), F32)
    for k in range(LEV):
        lane_mix = jnp.where((at == k) | (at == k + LEV), side[k], lane_mix)
        lane_weight = jnp.where(at == k, thick[k], jnp.where(at == k + LEV, -0.5 * thick[k], lane_weight))
        row_mix = jnp.where(level == k, side[k], row_mix)
        row_weight = jnp.where(level == k, thick[k], row_weight)
    weights[...] = jnp.concatenate([lane_mix, lane_weight, row_mix, row_weight], axis=0)
    e_sum, n_sum = east_sum[...], north_sum[...]
    forcing = column[...] - (e_sum - pltpu.roll(e_sum, 1, 1)) - (n_sum - pltpu.roll(n_sum, 1, 0))
    forcing_out[...] = forcing
    wait_all(singles[4:])
    depth = jnp.where(deep > 0, corner[...], 0.0)
    fields = (forcing, depth, diag[...], deep.astype(F32))
    deep_out[...], depth_out[...], diag_out[...] = fields[3], fields[1], fields[2]
    to_right, to_left = right[...], left[...]
    lane = iota((ROWS, 128), 1)
    for i, field in enumerate(fields):
        tile = field[:, COLS - 128:]
        tile = pltpu.roll(tile, 128 - 2 * i, 1) if i else tile
        to_right = jnp.where((lane >= 126 - 2 * i) & (lane < 128 - 2 * i), tile, to_right)
        tile = field[:, :128]
        tile = pltpu.roll(tile, 3 * i, 1) if i else tile
        to_left = jnp.where((lane >= 3 * i) & (lane < 3 * i + 3), tile, to_left)
    rows_0 = edge_rows[0:SLOT] - 0.5 * edge_rows[SLOT:2 * SLOT]
    rows_1 = edge_rows[2 * SLOT:3 * SLOT] - 0.5 * edge_rows[3 * SLOT:4 * SLOT]
    rows_2 = edge_rows[4 * SLOT:5 * SLOT]
    lane = iota((SLOT, 128), 1)
    corner_right = corner_left = jnp.zeros((SLOT, 128), F32)
    for i, rows in enumerate((rows_0, rows_1, rows_2)):
        tile = rows[:, COLS - 128:]
        tile = pltpu.roll(tile, 128 - 2 * i, 1) if i else tile
        corner_right = jnp.where((lane >= 126 - 2 * i) & (lane < 128 - 2 * i), tile, corner_right)
        tile = rows[:, :128]
        tile = pltpu.roll(tile, 3 * i, 1) if i else tile
        corner_left = jnp.where((lane >= 3 * i) & (lane < 3 * i + 3), tile, corner_left)
    even = lax.axis_index("bx") % 2 == 0
    first_out[:ROWS] = jnp.where(even, to_right, to_left)
    second_out[:ROWS] = jnp.where(even, to_left, to_right)
    first_out[ROWS:] = jnp.where(even, corner_right, corner_left)
    second_out[ROWS:] = jnp.where(even, corner_left, corner_right)


def lane_tile(from_right, from_left, i):
    lane = iota(from_right.shape, 1)
    if i:
        from_right, from_left = pltpu.roll(from_right, 128 - 3 * i, 1), pltpu.roll(from_left, 2 * i, 1)
    return jnp.where(lane < 3, from_right, jnp.where(lane >= 126, from_left, 0.0))


def columns_kernel(weights, first, second, first_in, second_in, forcing, deep_in, depth_in, diag, edge_rows,
                   first_out, second_out, forcing_wide, depth_wide, diag_wide, flux_left, flux_right):
    own_right, own_left = by_side("bx", first[...], second[...])
    from_right, from_left = by_side("bx", first_in[...], second_in[...])
    deep_f, depth = deep_in[...], depth_in[...]
    lane = iota((ROWS, 128), 1)
    at = iota((8, 128), 1)
    mix, weight = weights[0:1], weights[8:9]
    of_lane = jnp.where(at < LEV, at, jnp.where(at < 2 * LEV, at - LEV, 100))[:1].astype(F32)

    def face(west, east, flow, west_deep, east_deep):
        flux = 0.5 * flow * (west + east) - mix * (east - west)
        flux = jnp.where(of_lane < jnp.minimum(west_deep, east_deep), flux, 0.0)
        return flux, jnp.sum(flux * weight, axis=1, keepdims=True)

    own, seen = own_left[:ROWS], from_left[:ROWS]
    flux, west_sum = face(seen, pltpu.roll(own, 64, 1), pltpu.roll(seen, 128 - 2 * LEV, 1), seen[:, 121:122], deep_f[:, :1])
    flux_left[...] = flux
    own, seen = own_right[:ROWS], from_right[:ROWS]
    flux, east_sum = face(own, pltpu.roll(seen, 64, 1), pltpu.roll(own, 128 - 2 * LEV, 1), deep_f[:, COLS - 1:], seen[:, 9:10])
    flux_right[...] = flux

    mine = forcing[...]
    tiles = (
        mine[:, :128] + jnp.where(lane == 0, west_sum, 0.0),
        mine[:, 128:] - jnp.where(lane == 127, east_sum, 0.0),
        lane_tile(from_right[:ROWS], from_left[:ROWS], 0)
        + jnp.where(lane == 0, east_sum, jnp.where(lane == 127, -west_sum, 0.0)),
    )
    wide = jnp.concatenate(tiles, axis=1)
    forcing_wide[...] = wide
    depth_w = jnp.concatenate([depth, lane_tile(from_right[:ROWS], from_left[:ROWS], 1)], axis=1)
    diag_w = jnp.concatenate([diag[...], lane_tile(from_right[:ROWS], from_left[:ROWS], 2)], axis=1)
    deep_w = jnp.concatenate([deep_f, lane_tile(from_right[:ROWS], from_left[:ROWS], 3)], axis=1)
    depth_wide[...] = depth_w
    diag_wide[...] = diag_w

    def rows(value, i):
        return jnp.concatenate([value, lane_tile(from_right[ROWS:], from_left[ROWS:], i)], axis=1)

    nothing = jnp.zeros((SLOT, 128), F32)
    two_0, two_1 = edge_rows[SLOT:2 * SLOT], edge_rows[3 * SLOT:4 * SLOT]
    both_0 = rows(edge_rows[0:SLOT] - 0.5 * two_0, 0)
    both_1 = rows(edge_rows[2 * SLOT:3 * SLOT] - 0.5 * two_1, 1)
    north_1 = rows(edge_rows[4 * SLOT:5 * SLOT], 2)
    even = lax.axis_index("by") % 2 == 0
    up = (both_1, jnp.concatenate([two_1, nothing], axis=1), north_1, jnp.concatenate(
        [wide[62:64], deep_w[63:64], depth_w[62:64], diag_w[63:64], jnp.zeros((2, WIDE), F32)], axis=0))
    down = (both_0, jnp.concatenate([two_0, nothing], axis=1), jnp.zeros((SLOT, WIDE), F32), jnp.concatenate(
        [wide[0:3], deep_w[0:1], depth_w[0:2], diag_w[0:2]], axis=0))
    for i in range(4):
        place = slice(i * SLOT, i * SLOT + (SLOT if i < 3 else 8))
        first_out[place] = jnp.where(even, up[i], down[i])
        second_out[place] = jnp.where(even, down[i], up[i])


def operate(field, half_depth, diag):
    east = pltpu.roll(field, WIDE - 1, 1)
    north = pltpu.roll(field, TALL - 1, 0)
    corner = pltpu.roll(north, WIDE - 1, 1)
    plus = half_depth * (corner - field)
    minus = half_depth * (east - north)
    return (diag * field - plus + pltpu.roll(minus, 1, 1)
            + pltpu.roll(pltpu.roll(plus, 1, 1) - minus, 1, 0)), plus, minus


def solver_kernel(weights, first, second, first_in, second_in, forcing, depth, diag,
                  low_one, low_two, high_one, high_two, tracer_one, tracer_two,
                  zero_out, one_out, two_out, sums_out, full_one, full_two, strips, sems):
    own_up, own_down = by_side("by", first[...], second[...])
    above, beneath = by_side("by", first_in[...], second_in[...])
    level = iota((SLOT, WIDE), 0)
    mix, weight = (jnp.concatenate([weights[i:i + SLOT]] * (WIDE // 128), axis=1) for i in (16, 16 + SLOT))
    level_f = level.astype(F32)

    def face(south, north, south_deep, north_deep):
        flow = south[2 * SLOT:3 * SLOT]
        wet = level_f < jnp.minimum(south_deep, north_deep)

        def flux(low, high):
            columns = low.shape[1]
            value = 0.5 * flow[:, :columns] * (low + high) - mix[:, :columns] * (high - low)
            return jnp.where(wet[:, :columns], value, 0.0)

        both = flux(south[:SLOT], north[:SLOT])
        two = flux(south[SLOT:2 * SLOT, :COLS], north[SLOT:2 * SLOT, :COLS])
        return jnp.sum(both * weight, axis=0, keepdims=True), both[:, :COLS] + 0.5 * two, two

    top, top_one, top_two = face(own_up, above, own_up[74:75], above[75:76])
    bottom, bottom_one, bottom_two = face(beneath, own_down, beneath[74:75], own_down[75:76])

    strip_row = iota((8, COLS), 0)
    stores = []
    for i, (strip, flux, at, target) in enumerate((
            (low_one, bottom_one, 0, full_one), (low_two, bottom_two, 0, full_two),
            (high_one, -top_one, 7, full_one), (high_two, -top_two, 7, full_two))):
        for k in range(LEV):
            strips[i, k] = strip[k] + jnp.where(strip_row == at, flux[k:k + 1], 0.0)
        place = pl.ds(0 if at == 0 else ROWS - 8, 8)
        stores.append(pltpu.make_async_copy(strips.at[i], target.at[:, place], sems.at[i]))
        stores[-1].start()

    def blank(count):
        return jnp.zeros((count, WIDE), F32)

    own_row = iota((ROWS, WIDE), 0)
    mine = forcing[...] + jnp.where(own_row == 0, bottom, jnp.where(own_row == ROWS - 1, -top, 0.0))
    field = jnp.concatenate([
        jnp.concatenate([blank(6), beneath[72:73], beneath[73:74] - bottom], axis=0), mine,
        jnp.concatenate([above[72:73] + top, above[73:75], blank(5)], axis=0)], axis=0)
    half_depth = 0.5 * jnp.concatenate([
        jnp.concatenate([blank(6), beneath[75:77]], axis=0), depth[...],
        jnp.concatenate([above[76:78], blank(6)], axis=0)], axis=0)
    diag_all = jnp.concatenate([
        jnp.concatenate([blank(7), beneath[77:78]], axis=0), diag[...],
        jnp.concatenate([above[78:80], blank(6)], axis=0)], axis=0)
    last = lax.axis_index("by") == lax.axis_size("by") - 1
    inside = iota((TALL, WIDE), 0) < jnp.where(last, ROWS + 8, TALL)

    image, _, _ = operate(field, half_depth, diag_all)
    image = jnp.where(inside, image, 0.0)
    twice, _, _ = operate(image, half_depth, diag_all)
    twice = jnp.where(inside, twice, 0.0)
    _, plus, minus = operate(twice, half_depth, diag_all)
    east = pltpu.roll(twice, WIDE - 1, 1)
    north = pltpu.roll(twice, TALL - 1, 0)
    corner = pltpu.roll(north, WIDE - 1, 1)
    energy = diag_all * twice * twice + plus * (corner - twice) + minus * (east - north)

    def own(value):
        return value[8:8 + ROWS, :COLS]

    v_0, v_1, v_2 = own(field), own(image), own(twice)
    zero_out[...], one_out[...], two_out[...] = v_0, v_1, v_2
    lane = iota((128, 128), 1)
    sums = jnp.zeros((128, 128), F32)
    for i, product in enumerate((v_0 * v_0, v_0 * v_1, v_1 * v_1, v_1 * v_2, v_2 * v_2, own(energy))):
        sums = jnp.where(lane == i, jnp.sum(product, keepdims=True), sums)
    sums_out[...] = sums
    wait_all(stores)


def surface_kernel(sums, zero, one, two, surface):
    total = jnp.sum(sums[...], axis=0, keepdims=True)
    m = [total[:, i:i + 1] for i in range(6)]
    a_0 = m[0] / m[1]
    rr_1 = m[0] - 2.0 * a_0 * m[1] + a_0 * a_0 * m[2]
    rar_1 = m[1] - 2.0 * a_0 * m[2] + a_0 * a_0 * m[3]
    b_1 = rr_1 / m[0]
    a_1 = rr_1 / (rar_1 - b_1 * rr_1 / a_0)
    grow = 1.0 + b_1
    p_1 = -(a_0 + a_1 * grow)
    p_2 = a_1 * a_0
    rr_2 = m[0] + p_1 * p_1 * m[2] + p_2 * p_2 * m[4] + 2.0 * (p_1 * m[1] + p_2 * m[2] + p_1 * p_2 * m[3])
    rar_2 = m[1] + p_1 * p_1 * m[3] + p_2 * p_2 * m[5] + 2.0 * (p_1 * m[2] + p_2 * m[3] + p_1 * p_2 * m[4])
    b_2 = rr_2 / rr_1
    a_2 = rr_2 / (rar_2 - b_2 * rr_2 / a_1)
    w_0 = a_0 + a_1 * grow + a_2 * (1.0 + b_2 * grow)
    w_1 = -a_1 * a_0 + a_2 * (p_1 - b_2 * a_0)
    w_2 = a_2 * p_2
    surface[...] = w_0 * zero[...] + w_1 * one[...] + w_2 * two[...]


def tracers_kernel(side_hbm, vert_hbm, one_hbm, two_hbm, east_hbm, north_hbm, deep_in, flux_left, flux_right,
                   one_out, two_out, low_one, low_two, high_one, high_two,
                   side, vert, one, two, east, north, east_deep, north_deep, new_one, new_two, edge, sems, small, out_sems):
    copy = load_chunks((one_hbm, two_hbm, east_hbm, north_hbm), (one, two, east, north), sems)
    chunks = ROWS // CHUNK
    singles = [pltpu.make_async_copy(a, b, small.at[i]) for i, (a, b) in enumerate(((side_hbm, side), (vert_hbm, vert)))]
    start_all(singles)
    for chunk in range(chunks):
        start_all(copy(array, chunk) for array in range(4))

    kept = ((0, 8, 8), (1, CHUNK, CHUNK), (2, 2 * CHUNK, CHUNK), (3, 3 * CHUNK, 8))

    def store(array, which):
        chunk, start, count = kept[which]
        source, target = ((new_one, one_out), (new_two, two_out))[array]
        return pltpu.make_async_copy(
            source.at[:, pl.ds(start, count)], target.at[:, pl.ds(start, count)], out_sems.at[array, which])

    deep = deep_in[...].astype(jnp.int32)
    at_row = iota((ROWS, COLS), 0)
    east_deep[...] = jnp.minimum(deep, pltpu.roll(deep, COLS - 1, 1))
    north_deep[...] = jnp.where(at_row < ROWS - 1, jnp.minimum(deep, pltpu.roll(deep, ROWS - 1, 0)), 0)
    edge[...] = jnp.zeros(edge.shape, F32)
    row, lane = iota((CHUNK, COLS), 0), iota((CHUNK, 128), 1)
    wait_all(singles)
    wait_all(copy(array, 0) for array in range(4))

    @pl.loop(0, chunks)
    def _(chunk):
        @pl.when(chunk + 1 < chunks)
        def _():
            wait_all(copy(array, chunk + 1) for array in range(4))

        start = pl.multiple_of(chunk * CHUNK, CHUNK)
        part = pl.ds(start, CHUNK)
        here = deep_in[part].astype(jnp.int32)
        to_east, to_north = east_deep[part], north_deep[part]
        west_flux, east_flux = flux_left[part], flux_right[part]

        def level(k, falls):
            flow_e, flow_n = 0.5 * east[k, part].astype(F32), 0.5 * north[k, part].astype(F32)
            mix, fall_w = side[k], vert[k]
            below = jnp.minimum(k + 1, LEV - 1)
            wet, wet_below = here > k, here > k + 1
            wet_east, wet_north = to_east > k, to_north > k
            kept_falls = []
            for i, (source, target) in enumerate(((one, new_one), (two, new_two))):
                c = source[k, part]
                nxt = pltpu.roll(c, COLS - 1, 1)
                e = jnp.where(wet_east, flow_e * (c + nxt) - mix * (nxt - c), 0.0)
                seam = pltpu.roll(east_flux, 127 - k - i * LEV, 1)
                e = jnp.concatenate([e[:, :128], jnp.where(lane == 127, seam, e[:, 128:])], axis=1)
                e_west = pltpu.roll(e, 1, 1)
                seam = pltpu.roll(west_flux, lax.rem(256 - k - i * LEV, 128), 1)
                e_west = jnp.concatenate([jnp.where(lane == 0, seam, e_west[:, :128]), e_west[:, 128:]], axis=1)
                nxt = jnp.where(row == CHUNK - 1, source[k, pl.ds(start + CHUNK, 1)], pltpu.roll(c, CHUNK - 1, 0))
                n = jnp.where(wet_north, flow_n * (c + nxt) - mix * (nxt - c), 0.0)
                place = pl.ds(i * SLOT + k, 1)
                n_south = jnp.where(row == 0, edge[place], pltpu.roll(n, 1, 0))
                edge[place] = n[CHUNK - 1:]
                fall = jnp.where(wet_below, fall_w * (source[below, part] - c), 0.0)
                target[k, part] = jnp.where(wet, c - (e - e_west) - (n - n_south) + (fall - falls[i]), 0.0)
                kept_falls.append(fall)
            return tuple(kept_falls)

        nothing = jnp.zeros((CHUNK, COLS), F32)
        lax.fori_loop(0, LEV, level, (nothing, nothing), unroll=2)
        for which in range(chunks):
            @pl.when(chunk == which)
            def _():
                store(0, which).start()
                store(1, which).start()

    low_one[...], low_two[...] = new_one[:, :8], new_two[:, :8]
    high_one[...], high_two[...] = new_one[:, ROWS - 8:], new_two[:, ROWS - 8:]
    wait_all(store(array, which) for array in range(2) for which in range(chunks))


def level_scratch():
    block, taller = (LEV, ROWS, COLS), (LEV, ROWS + 8, COLS)
    return [pltpu.VMEM(taller, F32), pltpu.VMEM(taller, F32), pltpu.VMEM(block, jnp.bfloat16), pltpu.VMEM(block, jnp.bfloat16)]


def cost(flops, moved):
    return pl.CostEstimate(flops=flops, bytes_accessed=moved, transcendentals=0)


def on_device(*arrays):
    (tracer_one, tracer_two, east_flow, north_flow, depth_levels, side_mix, vert_mix, thickness,
     corner_depth, diagonal) = (pltpu.with_memory_space_constraint(array, pltpu.HBM) for array in arrays)
    n_by, n_bx = lax.axis_size("by"), lax.axis_size("bx")
    cells = LEV * ROWS * COLS
    plane, wide, tile = shape(ROWS, COLS), shape(ROWS, WIDE), shape(ROWS, 128)
    block, strip = shape(LEV, ROWS, COLS), shape(LEV, 8, COLS)
    column_message, row_message = shape(ROWS + SLOT, 128), shape(3 * SLOT + 8, WIDE)
    flat, flat_int = pltpu.VMEM((ROWS, COLS), F32), pltpu.VMEM((ROWS, COLS), jnp.int32)
    level_list = pltpu.SMEM((LEV,), F32)
    transfers = pltpu.SemaphoreType.DMA((4, ROWS // CHUNK))
    first, second, forcing, deep, depth, diag, edge_rows, weights = pl.pallas_call(
        forcing_kernel,
        out_shape=(column_message, column_message, plane, plane, plane, plane, shape(5 * SLOT, COLS), tile),
        in_specs=[HBM] * 10,
        out_specs=(VMEM,) * 8,
        scratch_shapes=[level_list] * 3 + level_scratch() + [flat_int, flat, flat] + [flat_int] * 2 + [flat] * 3
        + [pltpu.VMEM((ROWS, 128), F32)] * 2 + [transfers, pltpu.SemaphoreType.DMA((6,))],
        compiler_params=PARAMS, cost_estimate=cost(30 * cells, 12 * cells), name="forcing",
    )(side_mix, vert_mix, thickness, tracer_one, tracer_two, east_flow, north_flow, depth_levels, corner_depth, diagonal)
    first_in, second_in = swap_both(first, second, "bx", n_bx, True)
    row_first, row_second, forcing, depth, diag, flux_left, flux_right = pl.pallas_call(
        columns_kernel,
        out_shape=(row_message, row_message, wide, wide, wide, tile, tile),
        in_specs=[VMEM] * 10,
        out_specs=(VMEM,) * 7,
        compiler_params=PARAMS, cost_estimate=cost(10**6, 10**6), name="columns",
    )(weights, first, second, first_in, second_in, forcing, deep, depth, diag, edge_rows)
    row_first_in, row_second_in = swap_both(row_first, row_second, "by", n_by, False)
    part_one, part_two, low_one, low_two, high_one, high_two = pl.pallas_call(
        tracers_kernel,
        out_shape=(block, block, strip, strip, strip, strip),
        in_specs=[HBM] * 6 + [VMEM] * 3,
        out_specs=(HBM,) * 2 + (VMEM,) * 4,
        scratch_shapes=[level_list] * 2 + level_scratch() + [flat_int] * 2 + [pltpu.VMEM((LEV, ROWS, COLS), F32)] * 2
        + [pltpu.VMEM((2 * SLOT, COLS), F32), transfers, pltpu.SemaphoreType.DMA((2,)),
           pltpu.SemaphoreType.DMA((2, ROWS // CHUNK))],
        compiler_params=PARAMS, cost_estimate=cost(60 * cells, 20 * cells), name="tracers",
    )(side_mix, vert_mix, tracer_one, tracer_two, east_flow, north_flow, deep, flux_left, flux_right)
    zero, one, two, sums, new_one, new_two = pl.pallas_call(
        solver_kernel,
        out_shape=(plane, plane, plane, shape(128, 128), block, block),
        in_specs=[VMEM] * 12 + [HBM] * 2,
        out_specs=(VMEM,) * 4 + (HBM,) * 2,
        input_output_aliases={12: 4, 13: 5},
        scratch_shapes=[pltpu.VMEM((4, LEV, 8, COLS), F32), pltpu.SemaphoreType.DMA((4,))],
        compiler_params=PARAMS, cost_estimate=cost(4 * 10**6, 10**6), name="solver",
    )(weights, row_first, row_second, row_first_in, row_second_in, forcing, depth, diag,
      low_one, low_two, high_one, high_two, part_one, part_two)
    sums = lax.all_to_all(sums[:n_by * n_bx], ("by", "bx"), 0, 0, tiled=True)
    surface = pl.pallas_call(
        surface_kernel, out_shape=plane, in_specs=[VMEM] * 4, out_specs=VMEM,
        compiler_params=PARAMS, cost_estimate=cost(10**5, 10**5), name="surface",
    )(sums, zero, one, two)
    return new_one, new_two, surface


def solution(mesh):
    block, field = P(None, "by", "bx"), P("by", "bx")
    return jax.shard_map(
        on_device, mesh=mesh,
        in_specs=(block, block, block, block, field, P(), P(), P(), field, field),
        out_specs=(block, block, field), check_vma=False,
    )
```

time: 68.5 us -> 49.7 us (0.73)
  local copies, waits for them, and re-layouts: 19.3 us -> 0 us
  blocking collectives: 0 us -> 17.5 us
  starting transfers between devices: 21.2 us -> 12.4 us
  Pallas kernels: 21.6 us -> 17.3 us
  waiting for transfers between devices: 4.7 us -> 1.53 us
    unnamed x62 -> x0, local copies, waits for them, and re-layouts: 19.3 us -> none
    all_to_all x0 -> x1, blocking collectives: none -> 17.5 us  [on_device(): sums = lax.all_to_all(sums[:n_by * n_bx], ('by', 'bx'), 0, 0, tiled=True)]
    all_to_all x1 -> x0, starting transfers between devices: 8.87 us -> none  [on_device(): sums = lax.all_to_all(sums[:n_by * n_bx], ('by', 'bx'), 0, 0, tiled=True)]
    ppermute x2, waiting for transfers between devices: 4.69 us -> 1.52 us  [swap_both(): lax.ppermute(second, axis, pairs(size, True, wrap))]
    pallas_call x1, Pallas kernels: 7.4 us -> 5.54 us  [on_device(): pl.pallas_call(forcing_kernel, out_shape=(column_message, column_message,...]
    pallas_call x1, Pallas kernels: 10.2 us -> 8.94 us  [on_device(): pl.pallas_call(tracers_kernel, out_shape=(block, block, strip, strip, str...]
    pallas_call x1, Pallas kernels: 1.92 us -> 1.08 us  [on_device(): pl.pallas_call(surface_kernel, out_shape=plane, in_specs=[VMEM] * 4, out_...]
  transfers between devices with their start and end apart: 5 -> 4, of which waited for: 2 -> 1; matrix products, arithmetic and copies ran while one was open for 0% -> 0% of each run, Pallas kernels for 15% -> 18%
where the time goes in v2:
time: 49.7 us; the launch traced here: 49.5 us
  blocking collectives  17.5 us (35%)
  Pallas kernels  17.3 us (35%)
  starting transfers between devices  12.4 us (25%)
  waiting for transfers between devices  1.53 us (3%)
  between operations  0.69 us (1%)
    all_to_all x1, blocking collectives, on_device(): sums = lax.all_to_all(sums[:n_by * n_bx], ('by', 'bx'), 0, 0, tiled=True)  17.5 us
    pallas_call x1, Pallas kernels, on_device(): pl.pallas_call(tracers_kernel, out_shape=(block, block, strip, strip, str...  8.94 us
    ppermute x2, starting transfers between devices, swap_both(): lax.ppermute(second, axis, pairs(size, True, wrap))  7.71 us
    pallas_call x1, Pallas kernels, on_device(): pl.pallas_call(forcing_kernel, out_shape=(column_message, column_message,...  5.54 us
    ppermute x2, starting transfers between devices, swap_both(): lax.ppermute(first, axis, pairs(size, False, wrap))  4.73 us
    ppermute x2, waiting for transfers between devices, swap_both(): lax.ppermute(second, axis, pairs(size, True, wrap))  1.52 us
    pallas_call x1, Pallas kernels, on_device(): pl.pallas_call(solver_kernel, out_shape=(plane, plane, plane, shape(128,...  1.5 us
    pallas_call x1, Pallas kernels, on_device(): pl.pallas_call(surface_kernel, out_shape=plane, in_specs=[VMEM] * 4, out_...  1.08 us
  transfers between devices with their start and end apart: 4, of which 1 were waited for; matrix products, arithmetic and copies ran while one was open for 0% of the time, Pallas kernels for 18%

profile of v2, /device:TPU:1, one launch (start us, length us, event | category | flops | bytes accessed | tf_op | source)
XLA Modules:
  0.0 49.5 jit_solution(18409102674376027377)
XLA Ops:
  0.6 5.5 %forcing.1 = (f32[88,128]{1,0:T(8,128)S(1)}, f32[88,128]{1,0:T(8,128)S(1)}, f32[64,256]{1,0:T(8,128)S(1)}, f32[64,256]{1,0:T(8,128)S(1)}, f32[64,256]{1,0:T(8,12...) custom-call(f32[18]{0:T(128)} %side_hbm.3, f32[18]{0:T(128)} %vert_hbm.3, ...), custom_call_target="tpu_custom_call" | custom-call | flops 8847360 | bytes 3538944 | tf_op jit(solution)/shard_map/forcing/pallas_call | solution.py:450
  6.2 2.5 %collective-permute-start = (f32[88,128]{1,0:T(8,128)S(1)}, f32[88,128]{1,0:T(8,128)S(1)}, u32[]{:S(2)}, u32[]{:S(2)}) collective-permute-start(f32[88,128]{1,0:T(8,128)S(1)} %get-tuple-element.31.first), channel_id=1, source_target_pairs={{0,1},{1,0},{2,3},{3,2},{4,5},{5,4},{6,7},{7,6},{8,9},{9,8},{10,11... | collective-permute-start | bytes 135176 | tf_op jit(solution)/shard_map/ppermute | solution.py:41
  8.7 4.7 %collective-permute-start.1 = (f32[88,128]{1,0:T(8,128)S(1)}, f32[88,128]{1,0:T(8,128)S(1)}, u32[]{:S(2)}, u32[]{:S(2)}) collective-permute-start(f32[88,128]{1,0:T(8,128)S(1)} %get-tuple-element.32.second), channel_id=1, source_target_pairs={{1,2},{2,1},{3,4},{4,3},{5,6},{6,5},{7,8},{8,7},{9,10},{10,9},{11,... | collective-permute-start | bytes 135176 | tf_op jit(solution)/shard_map/ppermute | solution.py:42
  13.4 0.0 collective-permute-done.first_in
  13.4 1.5 %collective-permute-done.1.second_in = f32[88,128]{1,0:T(8,128)S(1)} collective-permute-done((f32[88,128]{1,0:T(8,128)S(1)}, f32[88,128]{1,0:T(8,128)S(1)}, u32[]{:S(2)}, u32[]{:S(2)}) %collective-permute-start.1) | collective-permute-done | bytes 45088 | tf_op jit(solution)/shard_map/ppermute | solution.py:42
  14.9 0.3 columns.1
  15.2 2.2 %collective-permute-start.2 = (f32[80,384]{1,0:T(8,128)S(1)}, f32[80,384]{1,0:T(8,128)S(1)}, u32[]{:S(2)}, u32[]{:S(2)}) collective-permute-start(f32[80,384]{1,0:T(8,128)S(1)} %get-tuple-element.38.first), channel_id=1, source_target_pairs={{0,16},{16,0},{32,48},{48,32},{64,80},{80,64},{96,112},{112,96},{1... | collective-permute-start | bytes 368648 | tf_op jit(solution)/shard_map/ppermute | solution.py:41
  17.4 3.0 %collective-permute-start.3 = (f32[80,384]{1,0:T(8,128)S(1)}, f32[80,384]{1,0:T(8,128)S(1)}, u32[]{:S(2)}, u32[]{:S(2)}) collective-permute-start(f32[80,384]{1,0:T(8,128)S(1)} %get-tuple-element.39.second), channel_id=1, source_target_pairs={{16,32},{32,16},{48,64},{64,48},{80,96},{96,80},{17,33},{33,17},{4... | collective-permute-start | bytes 368648 | tf_op jit(solution)/shard_map/ppermute | solution.py:42
  20.4 8.9 %tracers.1 = (f32[18,64,256]{2,1,0:T(8,128)}, f32[18,64,256]{2,1,0:T(8,128)}, f32[18,8,256]{2,1,0:T(8,128)S(1)}, f32[18,8,256]{2,1,0:T(8,128)S(1)}, f32[18,8,256...) custom-call(f32[18]{0:T(128)} %side_hbm.3, f32[18]{0:T(128)} %vert_hbm.3, f32[18,64,256]{2,1,0:T(8,128)} %one_hbm.3, ...), custom_call_target="tpu_custom_call" | custom-call | flops 17694720 | bytes 5898240 | tf_op jit(solution)/shard_map/tracers/pallas_call | solution.py:468
  29.4 0.0 collective-permute-done.2.first_in
  29.4 0.0 collective-permute-done.3.second_in
  29.4 1.5 %solver.1 = (f32[64,256]{1,0:T(8,128)S(1)}, f32[64,256]{1,0:T(8,128)S(1)}, f32[64,256]{1,0:T(8,128)S(1)}, f32[128,128]{1,0:T(8,128)S(1)}, f32[18,64,256]{2,1,0:T(8,128)}, /*index=5*/f32[18,64,256]{2,1,0:T(8,128)}) custom-call(f32[64,128]{1,0:T(8,128)S(1)} %get-tuple-element.30.weights, ...), custom_call_target="tpu_custom_call", output_to_operand_aliasing={{4}: (12, {}), {5}: (13, {})} | custom-call | flops 4000000 | bytes 1000000 | tf_op jit(solution)/shard_map/solver/pallas_call | solution.py:478
  30.9 17.5 %all_to_all.11 = f32[128,1,128]{2,1,0:T(1,128)S(1)} all-to-all(f32[128,1,128]{2,1,0:T(1,128)S(1)} %bitcast.5), channel_id=1, replica_groups=mesh['by'=8,'bx'=16] {'by','bx'}, dimensions={0} | all-to-all | bytes 131072 | tf_op jit(solution)/shard_map/all_to_all | solution.py:488
  48.4 1.1 %surface.1 = f32[64,256]{1,0:T(8,128)} custom-call(f32[128,128]{1,0:T(8,128)S(1)} %bitcast.4, f32[64,256]{1,0:T(8,128)S(1)} %get-tuple-element.54.zero, f32[64,256]{1,0:T(8,128)S(1)} %get-tuple-element.55.one, f32[64,256]{1,0:T(8,128)S(1)} %get-tuple-element.56.two), custom_call_target="tpu_custom_call" | custom-call | flops 100000 | bytes 100000 | tf_op jit(solution)/shard_map/surface/pallas_call | solution.py:489
Async XLA Ops:
  6.2 7.2 %collective-permute-start = (f32[88,128]{1,0:T(8,128)S(1)}, f32[88,128]{1,0:T(8,128)S(1)}, u32[]{:S(2)}, u32[]{:S(2)}) collective-permute-start(f32[88,128]{1,0:T(8,128)S(1)} %get-tuple-element.31.first), channel_id=1, source_target_pairs={{0,1},{1,0},{2,3},{3,2},{4,5},{5,4},{6,7},{7,6},{8,9},{9,8},{10,11... | collective-permute-start | bytes 135176 | tf_op jit(solution)/shard_map/ppermute | solution.py:41
  8.7 6.2 %collective-permute-start.1 = (f32[88,128]{1,0:T(8,128)S(1)}, f32[88,128]{1,0:T(8,128)S(1)}, u32[]{:S(2)}, u32[]{:S(2)}) collective-permute-start(f32[88,128]{1,0:T(8,128)S(1)} %get-tuple-element.32.second), channel_id=1, source_target_pairs={{1,2},{2,1},{3,4},{4,3},{5,6},{6,5},{7,8},{8,7},{9,10},{10,9},{11,... | collective-permute-start | bytes 135176 | tf_op jit(solution)/shard_map/ppermute | solution.py:42
  15.2 14.2 %collective-permute-start.2 = (f32[80,384]{1,0:T(8,128)S(1)}, f32[80,384]{1,0:T(8,128)S(1)}, u32[]{:S(2)}, u32[]{:S(2)}) collective-permute-start(f32[80,384]{1,0:T(8,128)S(1)} %get-tuple-element.38.first), channel_id=1, source_target_pairs={{0,16},{16,0},{32,48},{48,32},{64,80},{80,64},{96,112},{112,96},{1... | collective-permute-start | bytes 368648 | tf_op jit(solution)/shard_map/ppermute | solution.py:41
  17.4 12.0 %collective-permute-start.3 = (f32[80,384]{1,0:T(8,128)S(1)}, f32[80,384]{1,0:T(8,128)S(1)}, u32[]{:S(2)}, u32[]{:S(2)}) collective-permute-start(f32[80,384]{1,0:T(8,128)S(1)} %get-tuple-element.39.second), channel_id=1, source_target_pairs={{16,32},{32,16},{48,64},{64,48},{80,96},{96,80},{17,33},{33,17},{4... | collective-permute-start | bytes 368648 | tf_op jit(solution)/shard_map/ppermute | solution.py:42

commit v3 on v2

--- a/solution.py
+++ b/solution.py
@@ -6,11 +6,14 @@
 from jax.sharding import PartitionSpec as P
 
 LEV = 18
+AHEAD = 4
 CHUNK = 16
 SLOT = 24
 ROWS, COLS = 64, 256
 WIDE = COLS + 128
 TALL = ROWS + 16
+FORCING_UNROLL = 18
+TRACERS_UNROLL = 6
 F32 = jnp.float32
 VMEM = pl.BlockSpec(memory_space=pltpu.VMEM)
 SMEM = pl.BlockSpec(memory_space=pltpu.SMEM)
@@ -68,16 +71,17 @@
 
 def forcing_kernel(side_hbm, vert_hbm, thick_hbm, one_hbm, two_hbm, east_hbm, north_hbm, levels_hbm, corner_hbm, diag_hbm,
                    first_out, second_out, forcing_out, deep_out, depth_out, diag_out, edge_rows, weights,
-                   side, vert, thick, one, two, east, north,
-                   levels, corner, diag, east_deep, north_deep, east_sum, north_sum, column, right, left, sems, small):
+                   one, two, east, north, side, vert, thick, levels, corner, diag, east_deep, north_deep, east_sum, north_sum, column, right, left, sems, small):
     copy = load_chunks((one_hbm, two_hbm, east_hbm, north_hbm), (one, two, east, north), sems)
     chunks = ROWS // CHUNK
     pairs_of = ((levels_hbm, levels), (side_hbm, side), (vert_hbm, vert), (thick_hbm, thick), (corner_hbm, corner), (diag_hbm, diag))
     singles = [pltpu.make_async_copy(a, b, small.at[i]) for i, (a, b) in enumerate(pairs_of)]
     start_all(singles[:4])
-    for chunk in range(chunks):
+    for chunk in range(AHEAD):
         start_all(copy(array, chunk) for array in range(4))
     start_all(singles[4:])
+    for array in (one, two):
+        array[:, ROWS:] = jnp.zeros((LEV, 8, COLS), F32)
     wait_all(singles[:4])
     deep = levels[...]
     at_row, at_col = iota((ROWS, COLS), 0), iota((ROWS, COLS), 1)
@@ -93,6 +97,10 @@
         def _():
             wait_all(copy(array, chunk + 1) for array in range(4))
 
+        @pl.when(chunk + AHEAD < chunks)
+        def _():
+            start_all(copy(array, chunk + AHEAD) for array in range(4))
+
         start = pl.multiple_of(chunk * CHUNK, CHUNK)
         part = pl.ds(start, CHUNK)
         here, to_east, to_north = levels[part], east_deep[part], north_deep[part]
@@ -103,18 +111,17 @@
             flow_e, flow_n = east[k, part].astype(F32), north[k, part].astype(F32)
             both = c_one - 0.5 * c_two
             beyond = one[k, pl.ds(start + CHUNK, 1)] - 0.5 * two[k, pl.ds(start + CHUNK, 1)]
-            weight, mix = thick[k], side[k]
+            weight, mix = thick[k], 2.0 * side[k]
             below, above = jnp.minimum(k + 1, LEV - 1), jnp.maximum(k - 1, 0)
             fall = (weight - thick[below]) * vert[k]
             fall_above = (thick[above] - weight) * vert[above]
             total = total + both * jnp.where(
                 here > k + 1, weight + fall_above - fall, jnp.where(here > k, weight + fall_above, 0.0))
+            both, beyond = (0.5 * weight) * both, (0.5 * weight) * beyond
             nxt = pltpu.roll(both, COLS - 1, 1)
-            e_sum = e_sum + jnp.where(
-                to_east > k, (0.5 * weight) * (flow_e * (both + nxt)) - (weight * mix) * (nxt - both), 0.0)
+            e_sum = e_sum + jnp.where(to_east > k, flow_e * (both + nxt) - mix * (nxt - both), 0.0)
             nxt = jnp.where(row == CHUNK - 1, beyond, pltpu.roll(both, CHUNK - 1, 0))
-            n_sum = n_sum + jnp.where(
-                to_north > k, (0.5 * weight) * (flow_n * (both + nxt)) - (weight * mix) * (nxt - both), 0.0)
+            n_sum = n_sum + jnp.where(to_north > k, flow_n * (both + nxt) - mix * (nxt - both), 0.0)
             to_right = jnp.where(lane == k, c_one[:, COLS - 1:], to_right)
             to_right = jnp.where(lane == k + LEV, c_two[:, COLS - 1:], to_right)
             to_right = jnp.where((lane == k + 2 * LEV) | (lane == k + 3 * LEV), flow_e[:, COLS - 1:], to_right)
@@ -123,27 +130,26 @@
             return e_sum, n_sum, total, to_right, to_left
 
         flat, tile = jnp.zeros((CHUNK, COLS), F32), jnp.zeros((CHUNK, 128), F32)
-        result = lax.fori_loop(0, LEV, level, (flat, flat, flat, tile, tile), unroll=3)
+        result = lax.fori_loop(0, LEV, level, (flat, flat, flat, tile, tile), unroll=FORCING_UNROLL)
         for target, value in zip((east_sum, north_sum, column, right, left), result):
             target[part] = value
 
-    @pl.loop(0, LEV)
-    def _(k):
-        edge_rows[pl.ds(k, 1)] = one[k, 0:1]
-        edge_rows[pl.ds(SLOT + k, 1)] = two[k, 0:1]
-        edge_rows[pl.ds(2 * SLOT + k, 1)] = one[k, ROWS - 1:ROWS]
-        edge_rows[pl.ds(3 * SLOT + k, 1)] = two[k, ROWS - 1:ROWS]
-        edge_rows[pl.ds(4 * SLOT + k, 1)] = north[k, ROWS - CHUNK:ROWS].astype(F32)[CHUNK - 1:]
-
-    at, level = iota((8, 128), 1), iota((SLOT, 128), 0)
-    lane_mix = lane_weight = jnp.zeros((8, 128), F32)
-    row_mix = row_weight = jnp.zeros((SLOT, 128), F32)
+    for k in range(LEV):
+        rows = (one[k, 0:1], two[k, 0:1], one[k, ROWS - 1:ROWS], two[k, ROWS - 1:ROWS],
+                north[k, ROWS - 16:ROWS].astype(F32)[15:])
+        for i, value in enumerate(rows):
+            edge_rows[i * SLOT + k:i * SLOT + k + 1] = value
+
+    at, level = iota((8, COLS), 1), iota((SLOT, COLS), 0)
+    lane_mix = lane_weight = jnp.zeros((8, COLS), F32)
+    row_mix = row_weight = row_vert = jnp.zeros((SLOT, COLS), F32)
     for k in range(LEV):
         lane_mix = jnp.where((at == k) | (at == k + LEV), side[k], lane_mix)
         lane_weight = jnp.where(at == k, thick[k], jnp.where(at == k + LEV, -0.5 * thick[k], lane_weight))
         row_mix = jnp.where(level == k, side[k], row_mix)
         row_weight = jnp.where(level == k, thick[k], row_weight)
-    weights[...] = jnp.concatenate([lane_mix, lane_weight, row_mix, row_weight], axis=0)
+        row_vert = jnp.where(level == k, vert[k], row_vert)
+    weights[...] = jnp.concatenate([lane_mix, lane_weight, row_mix, row_weight, row_vert], axis=0)
     e_sum, n_sum = east_sum[...], north_sum[...]
     forcing = column[...] - (e_sum - pltpu.roll(e_sum, 1, 1)) - (n_sum - pltpu.roll(n_sum, 1, 0))
     forcing_out[...] = forcing
@@ -193,7 +199,7 @@
     deep_f, depth = deep_in[...], depth_in[...]
     lane = iota((ROWS, 128), 1)
     at = iota((8, 128), 1)
-    mix, weight = weights[0:1], weights[8:9]
+    mix, weight = weights[0:1, :128], weights[8:9, :128]
     of_lane = jnp.where(at < LEV, at, jnp.where(at < 2 * LEV, at - LEV, 100))[:1].astype(F32)
 
     def face(west, east, flow, west_deep, east_deep):
@@ -203,10 +209,10 @@
 
     own, seen = own_left[:ROWS], from_left[:ROWS]
     flux, west_sum = face(seen, pltpu.roll(own, 64, 1), pltpu.roll(seen, 128 - 2 * LEV, 1), seen[:, 121:122], deep_f[:, :1])
-    flux_left[...] = flux
+    flux_left[...] = 2.0 * flux
     own, seen = own_right[:ROWS], from_right[:ROWS]
     flux, east_sum = face(own, pltpu.roll(seen, 64, 1), pltpu.roll(own, 128 - 2 * LEV, 1), deep_f[:, COLS - 1:], seen[:, 9:10])
-    flux_right[...] = flux
+    flux_right[...] = 2.0 * flux
 
     mine = forcing[...]
     tiles = (
@@ -253,12 +259,15 @@
 
 
 def solver_kernel(weights, first, second, first_in, second_in, forcing, depth, diag,
-                  low_one, low_two, high_one, high_two, tracer_one, tracer_two,
-                  zero_out, one_out, two_out, sums_out, full_one, full_two, strips, sems):
+                  part_one, part_two, zero_out, one_out, two_out, sums_out, full_one, full_two, strips, sems):
+    inner = pl.ds(8, ROWS - 16)
+    stores = [pltpu.make_async_copy(source.at[:, inner], target.at[:, inner], sems.at[4 + i])
+              for i, (source, target) in enumerate(((part_one, full_one), (part_two, full_two)))]
+    start_all(stores)
     own_up, own_down = by_side("by", first[...], second[...])
     above, beneath = by_side("by", first_in[...], second_in[...])
     level = iota((SLOT, WIDE), 0)
-    mix, weight = (jnp.concatenate([weights[i:i + SLOT]] * (WIDE // 128), axis=1) for i in (16, 16 + SLOT))
+    mix, weight = (jnp.concatenate([weights[i:i + SLOT], weights[i:i + SLOT, :128]], axis=1) for i in (16, 16 + SLOT))
     level_f = level.astype(F32)
 
     def face(south, north, south_deep, north_deep):
@@ -278,14 +287,13 @@
     bottom, bottom_one, bottom_two = face(beneath, own_down, beneath[74:75], own_down[75:76])
 
     strip_row = iota((8, COLS), 0)
-    stores = []
-    for i, (strip, flux, at, target) in enumerate((
-            (low_one, bottom_one, 0, full_one), (low_two, bottom_two, 0, full_two),
-            (high_one, -top_one, 7, full_one), (high_two, -top_two, 7, full_two))):
+    for i, (source, flux, at, target) in enumerate((
+            (part_one, bottom_one, 0, full_one), (part_two, bottom_two, 0, full_two),
+            (part_one, -top_one, 7, full_one), (part_two, -top_two, 7, full_two))):
+        start = 0 if at == 0 else ROWS - 8
         for k in range(LEV):
-            strips[i, k] = strip[k] + jnp.where(strip_row == at, flux[k:k + 1], 0.0)
-        place = pl.ds(0 if at == 0 else ROWS - 8, 8)
-        stores.append(pltpu.make_async_copy(strips.at[i], target.at[:, place], sems.at[i]))
+            strips[i, k] = source[k, start:start + 8] + jnp.where(strip_row == at, flux[k:k + 1], 0.0)
+        stores.append(pltpu.make_async_copy(strips.at[i], target.at[:, pl.ds(start, 8)], sems.at[i]))
         stores[-1].start()
 
     def blank(count):
@@ -349,39 +357,17 @@
     surface[...] = w_0 * zero[...] + w_1 * one[...] + w_2 * two[...]
 
 
-def tracers_kernel(side_hbm, vert_hbm, one_hbm, two_hbm, east_hbm, north_hbm, deep_in, flux_left, flux_right,
-                   one_out, two_out, low_one, low_two, high_one, high_two,
-                   side, vert, one, two, east, north, east_deep, north_deep, new_one, new_two, edge, sems, small, out_sems):
-    copy = load_chunks((one_hbm, two_hbm, east_hbm, north_hbm), (one, two, east, north), sems)
-    chunks = ROWS // CHUNK
-    singles = [pltpu.make_async_copy(a, b, small.at[i]) for i, (a, b) in enumerate(((side_hbm, side), (vert_hbm, vert)))]
-    start_all(singles)
-    for chunk in range(chunks):
-        start_all(copy(array, chunk) for array in range(4))
-
-    kept = ((0, 8, 8), (1, CHUNK, CHUNK), (2, 2 * CHUNK, CHUNK), (3, 3 * CHUNK, 8))
-
-    def store(array, which):
-        chunk, start, count = kept[which]
-        source, target = ((new_one, one_out), (new_two, two_out))[array]
-        return pltpu.make_async_copy(
-            source.at[:, pl.ds(start, count)], target.at[:, pl.ds(start, count)], out_sems.at[array, which])
-
+def tracers_kernel(weights, one, two, east, north, deep_in, flux_left, flux_right, new_one, new_two,
+                   east_deep, north_deep, edge):
     deep = deep_in[...].astype(jnp.int32)
     at_row = iota((ROWS, COLS), 0)
     east_deep[...] = jnp.minimum(deep, pltpu.roll(deep, COLS - 1, 1))
     north_deep[...] = jnp.where(at_row < ROWS - 1, jnp.minimum(deep, pltpu.roll(deep, ROWS - 1, 0)), 0)
     edge[...] = jnp.zeros(edge.shape, F32)
     row, lane = iota((CHUNK, COLS), 0), iota((CHUNK, 128), 1)
-    wait_all(singles)
-    wait_all(copy(array, 0) for array in range(4))
-
-    @pl.loop(0, chunks)
+
+    @pl.loop(0, ROWS // CHUNK)
     def _(chunk):
-        @pl.when(chunk + 1 < chunks)
-        def _():
-            wait_all(copy(array, chunk + 1) for array in range(4))
-
         start = pl.multiple_of(chunk * CHUNK, CHUNK)
         part = pl.ds(start, CHUNK)
         here = deep_in[part].astype(jnp.int32)
@@ -389,48 +375,35 @@
         west_flux, east_flux = flux_left[part], flux_right[part]
 
         def level(k, falls):
-            flow_e, flow_n = 0.5 * east[k, part].astype(F32), 0.5 * north[k, part].astype(F32)
-            mix, fall_w = side[k], vert[k]
+            flow_e, flow_n = east[k, part].astype(F32), north[k, part].astype(F32)
+            mix = 2.0 * weights[pl.ds(16 + k, 1)]
             below = jnp.minimum(k + 1, LEV - 1)
-            wet, wet_below = here > k, here > k + 1
-            wet_east, wet_north = to_east > k, to_north > k
+            wet, wet_east, wet_north = here > k, to_east > k, to_north > k
+            east_own, east_next = jnp.where(wet_east, flow_e + mix, 0.0), jnp.where(wet_east, flow_e - mix, 0.0)
+            north_own, north_next = jnp.where(wet_north, flow_n + mix, 0.0), jnp.where(wet_north, flow_n - mix, 0.0)
+            fall_w = jnp.where(here > k + 1, weights[pl.ds(16 + 2 * SLOT + k, 1)], 0.0)
             kept_falls = []
             for i, (source, target) in enumerate(((one, new_one), (two, new_two))):
                 c = source[k, part]
-                nxt = pltpu.roll(c, COLS - 1, 1)
-                e = jnp.where(wet_east, flow_e * (c + nxt) - mix * (nxt - c), 0.0)
+                e = east_own * c + east_next * pltpu.roll(c, COLS - 1, 1)
                 seam = pltpu.roll(east_flux, 127 - k - i * LEV, 1)
                 e = jnp.concatenate([e[:, :128], jnp.where(lane == 127, seam, e[:, 128:])], axis=1)
                 e_west = pltpu.roll(e, 1, 1)
                 seam = pltpu.roll(west_flux, lax.rem(256 - k - i * LEV, 128), 1)
                 e_west = jnp.concatenate([jnp.where(lane == 0, seam, e_west[:, :128]), e_west[:, 128:]], axis=1)
                 nxt = jnp.where(row == CHUNK - 1, source[k, pl.ds(start + CHUNK, 1)], pltpu.roll(c, CHUNK - 1, 0))
-                n = jnp.where(wet_north, flow_n * (c + nxt) - mix * (nxt - c), 0.0)
+                n = north_own * c + north_next * nxt
                 place = pl.ds(i * SLOT + k, 1)
                 n_south = jnp.where(row == 0, edge[place], pltpu.roll(n, 1, 0))
                 edge[place] = n[CHUNK - 1:]
-                fall = jnp.where(wet_below, fall_w * (source[below, part] - c), 0.0)
-                target[k, part] = jnp.where(wet, c - (e - e_west) - (n - n_south) + (fall - falls[i]), 0.0)
+                fall = fall_w * (source[below, part] - c)
+                target[k, part] = jnp.where(
+                    wet, c + (fall - falls[i]) - 0.5 * ((e - e_west) + (n - n_south)), 0.0)
                 kept_falls.append(fall)
             return tuple(kept_falls)
 
         nothing = jnp.zeros((CHUNK, COLS), F32)
-        lax.fori_loop(0, LEV, level, (nothing, nothing), unroll=2)
-        for which in range(chunks):
-            @pl.when(chunk == which)
-            def _():
-                store(0, which).start()
-                store(1, which).start()
-
-    low_one[...], low_two[...] = new_one[:, :8], new_two[:, :8]
-    high_one[...], high_two[...] = new_one[:, ROWS - 8:], new_two[:, ROWS - 8:]
-    wait_all(store(array, which) for array in range(2) for which in range(chunks))
-
-
-def level_scratch():
-    block, taller = (LEV, ROWS, COLS), (LEV, ROWS + 8, COLS)
-    return [pltpu.VMEM(taller, F32), pltpu.VMEM(taller, F32), pltpu.VMEM(block, jnp.bfloat16), pltpu.VMEM(block, jnp.bfloat16)]
-
+        lax.fori_loop(0, LEV, level, (nothing, nothing), unroll=TRACERS_UNROLL)
 
 def cost(flops, moved):
     return pl.CostEstimate(flops=flops, bytes_accessed=moved, transcendentals=0)
@@ -442,17 +415,19 @@
     n_by, n_bx = lax.axis_size("by"), lax.axis_size("bx")
     cells = LEV * ROWS * COLS
     plane, wide, tile = shape(ROWS, COLS), shape(ROWS, WIDE), shape(ROWS, 128)
-    block, strip = shape(LEV, ROWS, COLS), shape(LEV, 8, COLS)
+    block, taller = shape(LEV, ROWS, COLS), shape(LEV, ROWS + 8, COLS)
+    half = jax.ShapeDtypeStruct((LEV, ROWS, COLS), jnp.bfloat16)
     column_message, row_message = shape(ROWS + SLOT, 128), shape(3 * SLOT + 8, WIDE)
     flat, flat_int = pltpu.VMEM((ROWS, COLS), F32), pltpu.VMEM((ROWS, COLS), jnp.int32)
     level_list = pltpu.SMEM((LEV,), F32)
     transfers = pltpu.SemaphoreType.DMA((4, ROWS // CHUNK))
-    first, second, forcing, deep, depth, diag, edge_rows, weights = pl.pallas_call(
+    first, second, forcing, deep, depth, diag, edge_rows, weights, one, two, east, north = pl.pallas_call(
         forcing_kernel,
-        out_shape=(column_message, column_message, plane, plane, plane, plane, shape(5 * SLOT, COLS), tile),
+        out_shape=(column_message, column_message, plane, plane, plane, plane, shape(5 * SLOT, COLS),
+                   shape(16 + 3 * SLOT, COLS), taller, taller, half, half),
         in_specs=[HBM] * 10,
-        out_specs=(VMEM,) * 8,
-        scratch_shapes=[level_list] * 3 + level_scratch() + [flat_int, flat, flat] + [flat_int] * 2 + [flat] * 3
+        out_specs=(VMEM,) * 12,
+        scratch_shapes=[level_list] * 3 + [flat_int, flat, flat] + [flat_int] * 2 + [flat] * 3
         + [pltpu.VMEM((ROWS, 128), F32)] * 2 + [transfers, pltpu.SemaphoreType.DMA((6,))],
         compiler_params=PARAMS, cost_estimate=cost(30 * cells, 12 * cells), name="forcing",
     )(side_mix, vert_mix, thickness, tracer_one, tracer_two, east_flow, north_flow, depth_levels, corner_depth, diagonal)
@@ -465,26 +440,22 @@
         compiler_params=PARAMS, cost_estimate=cost(10**6, 10**6), name="columns",
     )(weights, first, second, first_in, second_in, forcing, deep, depth, diag, edge_rows)
     row_first_in, row_second_in = swap_both(row_first, row_second, "by", n_by, False)
-    part_one, part_two, low_one, low_two, high_one, high_two = pl.pallas_call(
+    part_one, part_two = pl.pallas_call(
         tracers_kernel,
-        out_shape=(block, block, strip, strip, strip, strip),
-        in_specs=[HBM] * 6 + [VMEM] * 3,
-        out_specs=(HBM,) * 2 + (VMEM,) * 4,
-        scratch_shapes=[level_list] * 2 + level_scratch() + [flat_int] * 2 + [pltpu.VMEM((LEV, ROWS, COLS), F32)] * 2
-        + [pltpu.VMEM((2 * SLOT, COLS), F32), transfers, pltpu.SemaphoreType.DMA((2,)),
-           pltpu.SemaphoreType.DMA((2, ROWS // CHUNK))],
+        out_shape=(block, block),
+        in_specs=[VMEM] * 8,
+        out_specs=(VMEM,) * 2,
+        scratch_shapes=[flat_int] * 2 + [pltpu.VMEM((2 * SLOT, COLS), F32)],
         compiler_params=PARAMS, cost_estimate=cost(60 * cells, 20 * cells), name="tracers",
-    )(side_mix, vert_mix, tracer_one, tracer_two, east_flow, north_flow, deep, flux_left, flux_right)
+    )(weights, one, two, east, north, deep, flux_left, flux_right)
     zero, one, two, sums, new_one, new_two = pl.pallas_call(
         solver_kernel,
         out_shape=(plane, plane, plane, shape(128, 128), block, block),
-        in_specs=[VMEM] * 12 + [HBM] * 2,
+        in_specs=[VMEM] * 10,
         out_specs=(VMEM,) * 4 + (HBM,) * 2,
-        input_output_aliases={12: 4, 13: 5},
-        scratch_shapes=[pltpu.VMEM((4, LEV, 8, COLS), F32), pltpu.SemaphoreType.DMA((4,))],
+        scratch_shapes=[pltpu.VMEM((4, LEV, 8, COLS), F32), pltpu.SemaphoreType.DMA((6,))],
         compiler_params=PARAMS, cost_estimate=cost(4 * 10**6, 10**6), name="solver",
-    )(weights, row_first, row_second, row_first_in, row_second_in, forcing, depth, diag,
-      low_one, low_two, high_one, high_two, part_one, part_two)
+    )(weights, row_first, row_second, row_first_in, row_second_in, forcing, depth, diag, part_one, part_two)
     sums = lax.all_to_all(sums[:n_by * n_bx], ("by", "bx"), 0, 0, tiled=True)
     surface = pl.pallas_call(
         surface_kernel, out_shape=plane, in_specs=[VMEM] * 4, out_specs=VMEM,

time: 49.7 us -> 44.1 us (0.89)
  Pallas kernels: 17.3 us -> 11.8 us
    pallas_call x1, Pallas kernels: 8.94 us -> 4.39 us  [on_device(): pl.pallas_call(tracers_kernel, out_shape=(block, block), in_specs=[VMEM]...]
    pallas_call x1, Pallas kernels: 5.54 us -> 4.02 us  [on_device(): pl.pallas_call(forcing_kernel, out_shape=(column_message, column_message,...]
    pallas_call x1, Pallas kernels: 1.5 us -> 2 us  [on_device(): pl.pallas_call(solver_kernel, out_shape=(plane, plane, plane, shape(128,...]
  transfers between devices with their start and end apart: 4 -> 4, of which waited for: 1 -> 1; matrix products, arithmetic and copies ran while one was open for 0% -> 0% of each run, Pallas kernels for 18% -> 10%
where the time goes in v3:
time: 44.1 us; the launch traced here: 43.9 us
  blocking collectives  17.5 us (40%)
  starting transfers between devices  12.4 us (28%)
  Pallas kernels  11.8 us (27%)
  waiting for transfers between devices  1.53 us (3%)
  between operations  0.69 us (2%)
    all_to_all x1, blocking collectives, on_device(): sums = lax.all_to_all(sums[:n_by * n_bx], ('by', 'bx'), 0, 0, tiled=True)  17.5 us
    ppermute x2, starting transfers between devices, swap_both(): lax.ppermute(second, axis, pairs(size, True, wrap))  7.71 us
    ppermute x2, starting transfers between devices, swap_both(): lax.ppermute(first, axis, pairs(size, False, wrap))  4.73 us
    pallas_call x1, Pallas kernels, on_device(): pl.pallas_call(tracers_kernel, out_shape=(block, block), in_specs=[VMEM]...  4.39 us
    pallas_call x1, Pallas kernels, on_device(): pl.pallas_call(forcing_kernel, out_shape=(column_message, column_message,...  4.02 us
    pallas_call x1, Pallas kernels, on_device(): pl.pallas_call(solver_kernel, out_shape=(plane, plane, plane, shape(128,...  2 us
    ppermute x2, waiting for transfers between devices, swap_both(): lax.ppermute(second, axis, pairs(size, True, wrap))  1.52 us
    pallas_call x1, Pallas kernels, on_device(): pl.pallas_call(surface_kernel, out_shape=plane, in_specs=[VMEM] * 4, out_...  1.08 us
  transfers between devices with their start and end apart: 4, of which 1 were waited for; matrix products, arithmetic and copies ran while one was open for 0% of the time, Pallas kernels for 10%

profile of v3, /device:TPU:1, one launch (start us, length us, event | category | flops | bytes accessed | tf_op | source)
XLA Modules:
  0.0 43.9 jit_solution(6177246899074998313)
XLA Ops:
  0.6 4.0 %forcing.1 = (f32[88,128]{1,0:T(8,128)S(1)}, f32[88,128]{1,0:T(8,128)S(1)}, f32[64,256]{1,0:T(8,128)S(1)}, f32[64,256]{1,0:T(8,128)S(1)}, f32[64,256]{1,0:T(8,12...) custom-call(f32[18]{0:T(128)} %side_hbm.1, ...), custom_call_target="tpu_custom_call" | custom-call | flops 8847360 | bytes 3538944 | tf_op jit(solution)/shard_map/forcing/pallas_call | solution.py:424
  4.7 2.5 %collective-permute-start = (f32[88,128]{1,0:T(8,128)S(1)}, f32[88,128]{1,0:T(8,128)S(1)}, u32[]{:S(2)}, u32[]{:S(2)}) collective-permute-start(f32[88,128]{1,0:T(8,128)S(1)} %get-tuple-element.31.first), channel_id=1, source_target_pairs={{0,1},{1,0},{2,3},{3,2},{4,5},{5,4},{6,7},{7,6},{8,9},{9,8},{10,11... | collective-permute-start | bytes 135176 | tf_op jit(solution)/shard_map/ppermute | solution.py:44
  7.2 4.7 %collective-permute-start.1 = (f32[88,128]{1,0:T(8,128)S(1)}, f32[88,128]{1,0:T(8,128)S(1)}, u32[]{:S(2)}, u32[]{:S(2)}) collective-permute-start(f32[88,128]{1,0:T(8,128)S(1)} %get-tuple-element.32.second), channel_id=1, source_target_pairs={{1,2},{2,1},{3,4},{4,3},{5,6},{6,5},{7,8},{8,7},{9,10},{10,9},{11,... | collective-permute-start | bytes 135176 | tf_op jit(solution)/shard_map/ppermute | solution.py:45
  11.9 0.0 collective-permute-done.first_in
  11.9 1.5 %collective-permute-done.1.second_in = f32[88,128]{1,0:T(8,128)S(1)} collective-permute-done((f32[88,128]{1,0:T(8,128)S(1)}, f32[88,128]{1,0:T(8,128)S(1)}, u32[]{:S(2)}, u32[]{:S(2)}) %collective-permute-start.1) | collective-permute-done | bytes 45088 | tf_op jit(solution)/shard_map/ppermute | solution.py:45
  13.4 0.3 columns.1
  13.7 2.2 %collective-permute-start.2 = (f32[80,384]{1,0:T(8,128)S(1)}, f32[80,384]{1,0:T(8,128)S(1)}, u32[]{:S(2)}, u32[]{:S(2)}) collective-permute-start(f32[80,384]{1,0:T(8,128)S(1)} %get-tuple-element.38.first), channel_id=1, source_target_pairs={{0,16},{16,0},{32,48},{48,32},{64,80},{80,64},{96,112},{112,96},{1... | collective-permute-start | bytes 368648 | tf_op jit(solution)/shard_map/ppermute | solution.py:44
  15.9 3.0 %collective-permute-start.3 = (f32[80,384]{1,0:T(8,128)S(1)}, f32[80,384]{1,0:T(8,128)S(1)}, u32[]{:S(2)}, u32[]{:S(2)}) collective-permute-start(f32[80,384]{1,0:T(8,128)S(1)} %get-tuple-element.39.second), channel_id=1, source_target_pairs={{16,32},{32,16},{48,64},{64,48},{80,96},{96,80},{17,33},{33,17},{4... | collective-permute-start | bytes 368648 | tf_op jit(solution)/shard_map/ppermute | solution.py:45
  18.9 4.4 %tracers.1 = (f32[18,64,256]{2,1,0:T(8,128)S(1)}, f32[18,64,256]{2,1,0:T(8,128)S(1)}) custom-call(f32[88,256]{1,0:T(8,128)S(1)} %get-tuple-element.30.weights, f32[18,72,256]{2,1,0:T(8,128)S(1)} %get-tuple-element.43.one, f32[18,72,256]{2,1,0:T(8,128)S(1)} %get-tuple-element.44.two, bf16[18,64,256]{2,1,0:T(8,128)(2,1)S(1)} %get-tuple-element.45.east, ...), custom_call_target="tpu_custom_call" | custom-call | flops 17694720 | bytes 5898240 | tf_op jit(solution)/shard_map/tracers/pallas_call | solution.py:443
  23.3 0.0 collective-permute-done.2.first_in
  23.3 0.0 collective-permute-done.3.second_in
  23.3 2.0 %solver.1 = (f32[64,256]{1,0:T(8,128)S(1)}, f32[64,256]{1,0:T(8,128)S(1)}, f32[64,256]{1,0:T(8,128)S(1)}, f32[128,128]{1,0:T(8,128)S(1)}, f32[18,64,256]{2,1,0:T(8,128)}, /*index=5*/f32[18,64,256]{2,1,0:T(8,128)}) custom-call(f32[88,256]{1,0:T(8,128)S(1)} %get-tuple-element.30.weights, f32[80,384]{1,0:T(8,128)S(1)} %get-tuple-element.38.first, ...), custom_call_target="tpu_custom_call" | custom-call | flops 4000000 | bytes 1000000 | tf_op jit(solution)/shard_map/solver/pallas_call | solution.py:451
  25.4 17.5 %all_to_all.11 = f32[128,1,128]{2,1,0:T(1,128)S(1)} all-to-all(f32[128,1,128]{2,1,0:T(1,128)S(1)} %bitcast.5), channel_id=1, replica_groups=mesh['by'=8,'bx'=16] {'by','bx'}, dimensions={0} | all-to-all | bytes 131072 | tf_op jit(solution)/shard_map/all_to_all | solution.py:459
  42.9 1.1 %surface.1 = f32[64,256]{1,0:T(8,128)} custom-call(f32[128,128]{1,0:T(8,128)S(1)} %bitcast.4, f32[64,256]{1,0:T(8,128)S(1)} %get-tuple-element.54.zero, f32[64,256]{1,0:T(8,128)S(1)} %get-tuple-element.55.one, f32[64,256]{1,0:T(8,128)S(1)} %get-tuple-element.56.two), custom_call_target="tpu_custom_call" | custom-call | flops 100000 | bytes 100000 | tf_op jit(solution)/shard_map/surface/pallas_call | solution.py:460
Async XLA Ops:
  4.7 7.2 %collective-permute-start = (f32[88,128]{1,0:T(8,128)S(1)}, f32[88,128]{1,0:T(8,128)S(1)}, u32[]{:S(2)}, u32[]{:S(2)}) collective-permute-start(f32[88,128]{1,0:T(8,128)S(1)} %get-tuple-element.31.first), channel_id=1, source_target_pairs={{0,1},{1,0},{2,3},{3,2},{4,5},{5,4},{6,7},{7,6},{8,9},{9,8},{10,11... | collective-permute-start | bytes 135176 | tf_op jit(solution)/shard_map/ppermute | solution.py:44
  7.2 6.2 %collective-permute-start.1 = (f32[88,128]{1,0:T(8,128)S(1)}, f32[88,128]{1,0:T(8,128)S(1)}, u32[]{:S(2)}, u32[]{:S(2)}) collective-permute-start(f32[88,128]{1,0:T(8,128)S(1)} %get-tuple-element.32.second), channel_id=1, source_target_pairs={{1,2},{2,1},{3,4},{4,3},{5,6},{6,5},{7,8},{8,7},{9,10},{10,9},{11,... | collective-permute-start | bytes 135176 | tf_op jit(solution)/shard_map/ppermute | solution.py:45
  13.7 9.6 %collective-permute-start.2 = (f32[80,384]{1,0:T(8,128)S(1)}, f32[80,384]{1,0:T(8,128)S(1)}, u32[]{:S(2)}, u32[]{:S(2)}) collective-permute-start(f32[80,384]{1,0:T(8,128)S(1)} %get-tuple-element.38.first), channel_id=1, source_target_pairs={{0,16},{16,0},{32,48},{48,32},{64,80},{80,64},{96,112},{112,96},{1... | collective-permute-start | bytes 368648 | tf_op jit(solution)/shard_map/ppermute | solution.py:44
  15.9 7.4 %collective-permute-start.3 = (f32[80,384]{1,0:T(8,128)S(1)}, f32[80,384]{1,0:T(8,128)S(1)}, u32[]{:S(2)}, u32[]{:S(2)}) collective-permute-start(f32[80,384]{1,0:T(8,128)S(1)} %get-tuple-element.39.second), channel_id=1, source_target_pairs={{16,32},{32,16},{48,64},{64,48},{80,96},{96,80},{17,33},{33,17},{4... | collective-permute-start | bytes 368648 | tf_op jit(solution)/shard_map/ppermute | solution.py:45

commit v4 on v3

--- a/solution.py
+++ b/solution.py
@@ -6,7 +6,6 @@
 from jax.sharding import PartitionSpec as P
 
 LEV = 18
-AHEAD = 4
 CHUNK = 16
 SLOT = 24
 ROWS, COLS = 64, 256
@@ -77,7 +76,7 @@
     pairs_of = ((levels_hbm, levels), (side_hbm, side), (vert_hbm, vert), (thick_hbm, thick), (corner_hbm, corner), (diag_hbm, diag))
     singles = [pltpu.make_async_copy(a, b, small.at[i]) for i, (a, b) in enumerate(pairs_of)]
     start_all(singles[:4])
-    for chunk in range(AHEAD):
+    for chunk in range(chunks):
         start_all(copy(array, chunk) for array in range(4))
     start_all(singles[4:])
     for array in (one, two):
@@ -96,10 +95,6 @@
         @pl.when(chunk + 1 < chunks)
         def _():
             wait_all(copy(array, chunk + 1) for array in range(4))
-
-        @pl.when(chunk + AHEAD < chunks)
-        def _():
-            start_all(copy(array, chunk + AHEAD) for array in range(4))
 
         start = pl.multiple_of(chunk * CHUNK, CHUNK)
         part = pl.ds(start, CHUNK)
@@ -192,7 +187,7 @@
     return jnp.where(lane < 3, from_right, jnp.where(lane >= 126, from_left, 0.0))
 
 
-def columns_kernel(weights, first, second, first_in, second_in, forcing, deep_in, depth_in, diag, edge_rows,
+def columns_kernel(weights, first, second, first_in, second_in, forcing, deep_in, depth_in, diag, edge_rows, after,
                    first_out, second_out, forcing_wide, depth_wide, diag_wide, flux_left, flux_right):
     own_right, own_left = by_side("bx", first[...], second[...])
     from_right, from_left = by_side("bx", first_in[...], second_in[...])
@@ -209,10 +204,10 @@
 
     own, seen = own_left[:ROWS], from_left[:ROWS]
     flux, west_sum = face(seen, pltpu.roll(own, 64, 1), pltpu.roll(seen, 128 - 2 * LEV, 1), seen[:, 121:122], deep_f[:, :1])
-    flux_left[...] = 2.0 * flux
+    flux_left[...] = flux
     own, seen = own_right[:ROWS], from_right[:ROWS]
     flux, east_sum = face(own, pltpu.roll(seen, 64, 1), pltpu.roll(own, 128 - 2 * LEV, 1), deep_f[:, COLS - 1:], seen[:, 9:10])
-    flux_right[...] = 2.0 * flux
+    flux_right[...] = flux
 
     mine = forcing[...]
     tiles = (
@@ -258,12 +253,8 @@
             + pltpu.roll(pltpu.roll(plus, 1, 1) - minus, 1, 0)), plus, minus
 
 
-def solver_kernel(weights, first, second, first_in, second_in, forcing, depth, diag,
-                  part_one, part_two, zero_out, one_out, two_out, sums_out, full_one, full_two, strips, sems):
-    inner = pl.ds(8, ROWS - 16)
-    stores = [pltpu.make_async_copy(source.at[:, inner], target.at[:, inner], sems.at[4 + i])
-              for i, (source, target) in enumerate(((part_one, full_one), (part_two, full_two)))]
-    start_all(stores)
+def solver_kernel(weights, first, second, first_in, second_in, forcing, depth, diag, after,
+                  zero_out, one_out, two_out, sums_out, flux_rows):
     own_up, own_down = by_side("by", first[...], second[...])
     above, beneath = by_side("by", first_in[...], second_in[...])
     level = iota((SLOT, WIDE), 0)
@@ -286,15 +277,8 @@
     top, top_one, top_two = face(own_up, above, own_up[74:75], above[75:76])
     bottom, bottom_one, bottom_two = face(beneath, own_down, beneath[74:75], own_down[75:76])
 
-    strip_row = iota((8, COLS), 0)
-    for i, (source, flux, at, target) in enumerate((
-            (part_one, bottom_one, 0, full_one), (part_two, bottom_two, 0, full_two),
-            (part_one, -top_one, 7, full_one), (part_two, -top_two, 7, full_two))):
-        start = 0 if at == 0 else ROWS - 8
-        for k in range(LEV):
-            strips[i, k] = source[k, start:start + 8] + jnp.where(strip_row == at, flux[k:k + 1], 0.0)
-        stores.append(pltpu.make_async_copy(strips.at[i], target.at[:, pl.ds(start, 8)], sems.at[i]))
-        stores[-1].start()
+    for i, flux in enumerate((bottom_one, bottom_two, top_one, top_two)):
+        flux_rows[i * SLOT:(i + 1) * SLOT] = flux
 
     def blank(count):
         return jnp.zeros((count, WIDE), F32)
@@ -333,10 +317,25 @@
     for i, product in enumerate((v_0 * v_0, v_0 * v_1, v_1 * v_1, v_1 * v_2, v_2 * v_2, own(energy))):
         sums = jnp.where(lane == i, jnp.sum(product, keepdims=True), sums)
     sums_out[...] = sums
-    wait_all(stores)
-
-
-def surface_kernel(sums, zero, one, two, surface):
+
+
+def surface_kernel(sums, zero, one, two, flux_rows, new_one, new_two, inner_one, inner_two,
+                   surface_out, full_one, full_two, surface, strips, sems):
+    row = iota((8, COLS), 0)
+    stores = []
+    for i, (source, target) in enumerate(((new_one, full_one), (new_two, full_two))):
+        part = pl.ds(ROWS - CHUNK, CHUNK - 8)
+        stores.append(pltpu.make_async_copy(source.at[:, part], target.at[:, part], sems.at[4 + i]))
+        stores[-1].start()
+    for i, (source, at, sign, target) in enumerate((
+            (new_one, 0, 1.0, full_one), (new_two, 0, 1.0, full_two),
+            (new_one, 7, -1.0, full_one), (new_two, 7, -1.0, full_two))):
+        start = 0 if at == 0 else ROWS - 8
+        for k in range(LEV):
+            place = i * SLOT + k
+            strips[i, k] = source[k, start:start + 8] + jnp.where(row == at, sign * flux_rows[place:place + 1], 0.0)
+        stores.append(pltpu.make_async_copy(strips.at[i], target.at[:, pl.ds(start, 8)], sems.at[i]))
+        stores[-1].start()
     total = jnp.sum(sums[...], axis=0, keepdims=True)
     m = [total[:, i:i + 1] for i in range(6)]
     a_0 = m[0] / m[1]
@@ -355,24 +354,24 @@
     w_1 = -a_1 * a_0 + a_2 * (p_1 - b_2 * a_0)
     w_2 = a_2 * p_2
     surface[...] = w_0 * zero[...] + w_1 * one[...] + w_2 * two[...]
-
-
-def tracers_kernel(weights, one, two, east, north, deep_in, flux_left, flux_right, new_one, new_two,
-                   east_deep, north_deep, edge):
+    stores.append(pltpu.make_async_copy(surface, surface_out, sems.at[6]))
+    stores[-1].start()
+    wait_all(stores)
+
+
+def tracers_kernel(weights, one, two, east, north, deep_in, part_one, part_two, east_deep, north_deep, edge):
     deep = deep_in[...].astype(jnp.int32)
-    at_row = iota((ROWS, COLS), 0)
-    east_deep[...] = jnp.minimum(deep, pltpu.roll(deep, COLS - 1, 1))
+    at_row, at_col = iota((ROWS, COLS), 0), iota((ROWS, COLS), 1)
+    east_deep[...] = jnp.where(at_col < COLS - 1, jnp.minimum(deep, pltpu.roll(deep, COLS - 1, 1)), 0)
     north_deep[...] = jnp.where(at_row < ROWS - 1, jnp.minimum(deep, pltpu.roll(deep, ROWS - 1, 0)), 0)
     edge[...] = jnp.zeros(edge.shape, F32)
-    row, lane = iota((CHUNK, COLS), 0), iota((CHUNK, 128), 1)
+    row = iota((CHUNK, COLS), 0)
 
     @pl.loop(0, ROWS // CHUNK)
     def _(chunk):
         start = pl.multiple_of(chunk * CHUNK, CHUNK)
         part = pl.ds(start, CHUNK)
-        here = deep_in[part].astype(jnp.int32)
-        to_east, to_north = east_deep[part], north_deep[part]
-        west_flux, east_flux = flux_left[part], flux_right[part]
+        here, to_east, to_north = deep_in[part].astype(jnp.int32), east_deep[part], north_deep[part]
 
         def level(k, falls):
             flow_e, flow_n = east[k, part].astype(F32), north[k, part].astype(F32)
@@ -383,14 +382,9 @@
             north_own, north_next = jnp.where(wet_north, flow_n + mix, 0.0), jnp.where(wet_north, flow_n - mix, 0.0)
             fall_w = jnp.where(here > k + 1, weights[pl.ds(16 + 2 * SLOT + k, 1)], 0.0)
             kept_falls = []
-            for i, (source, target) in enumerate(((one, new_one), (two, new_two))):
+            for i, (source, target) in enumerate(((one, part_one), (two, part_two))):
                 c = source[k, part]
                 e = east_own * c + east_next * pltpu.roll(c, COLS - 1, 1)
-                seam = pltpu.roll(east_flux, 127 - k - i * LEV, 1)
-                e = jnp.concatenate([e[:, :128], jnp.where(lane == 127, seam, e[:, 128:])], axis=1)
-                e_west = pltpu.roll(e, 1, 1)
-                seam = pltpu.roll(west_flux, lax.rem(256 - k - i * LEV, 128), 1)
-                e_west = jnp.concatenate([jnp.where(lane == 0, seam, e_west[:, :128]), e_west[:, 128:]], axis=1)
                 nxt = jnp.where(row == CHUNK - 1, source[k, pl.ds(start + CHUNK, 1)], pltpu.roll(c, CHUNK - 1, 0))
                 n = north_own * c + north_next * nxt
                 place = pl.ds(i * SLOT + k, 1)
@@ -398,12 +392,34 @@
                 edge[place] = n[CHUNK - 1:]
                 fall = fall_w * (source[below, part] - c)
                 target[k, part] = jnp.where(
-                    wet, c + (fall - falls[i]) - 0.5 * ((e - e_west) + (n - n_south)), 0.0)
+                    wet, c + (fall - falls[i]) - 0.5 * ((e - pltpu.roll(e, 1, 1)) + (n - n_south)), 0.0)
                 kept_falls.append(fall)
             return tuple(kept_falls)
 
         nothing = jnp.zeros((CHUNK, COLS), F32)
         lax.fori_loop(0, LEV, level, (nothing, nothing), unroll=TRACERS_UNROLL)
+
+
+def edges_kernel(flux_left, flux_right, part_one, part_two, one_out, two_out, new_one, new_two, sems):
+    kept = ((8, CHUNK - 8), (CHUNK, CHUNK), (2 * CHUNK, CHUNK))
+    stores = []
+    lane = iota((CHUNK, 128), 1)
+    for chunk in range(ROWS // CHUNK):
+        part = pl.ds(chunk * CHUNK, CHUNK)
+        west_flux, east_flux = flux_left[part], flux_right[part]
+        for i, (source, target, out) in enumerate(((part_one, new_one, one_out), (part_two, new_two, two_out))):
+            for k in range(LEV):
+                at = k + i * LEV
+                seam = pltpu.roll(west_flux, 128 - at, 1) if at else west_flux
+                target[k, part, :128] = source[k, part, :128] + jnp.where(lane == 0, seam, 0.0)
+                seam = pltpu.roll(east_flux, 127 - at, 1)
+                target[k, part, 128:] = source[k, part, 128:] - jnp.where(lane == 127, seam, 0.0)
+            if chunk < len(kept):
+                place = pl.ds(*kept[chunk])
+                stores.append(pltpu.make_async_copy(target.at[:, place], out.at[:, place], sems.at[i, chunk]))
+                stores[-1].start()
+    wait_all(stores)
+
 
 def cost(flops, moved):
     return pl.CostEstimate(flops=flops, bytes_accessed=moved, transcendentals=0)
@@ -431,36 +447,48 @@
         + [pltpu.VMEM((ROWS, 128), F32)] * 2 + [transfers, pltpu.SemaphoreType.DMA((6,))],
         compiler_params=PARAMS, cost_estimate=cost(30 * cells, 12 * cells), name="forcing",
     )(side_mix, vert_mix, thickness, tracer_one, tracer_two, east_flow, north_flow, depth_levels, corner_depth, diagonal)
+    part_one, part_two = pl.pallas_call(
+        tracers_kernel,
+        out_shape=(block, block),
+        in_specs=[VMEM] * 6,
+        out_specs=(VMEM,) * 2,
+        scratch_shapes=[flat_int] * 2 + [pltpu.VMEM((2 * SLOT, COLS), F32)],
+        compiler_params=PARAMS, cost_estimate=cost(60 * cells, 20 * cells), name="tracers",
+    )(weights, one, two, east, north, deep)
     first_in, second_in = swap_both(first, second, "bx", n_bx, True)
     row_first, row_second, forcing, depth, diag, flux_left, flux_right = pl.pallas_call(
         columns_kernel,
         out_shape=(row_message, row_message, wide, wide, wide, tile, tile),
-        in_specs=[VMEM] * 10,
+        in_specs=[VMEM] * 10 + [HBM],
         out_specs=(VMEM,) * 7,
         compiler_params=PARAMS, cost_estimate=cost(10**6, 10**6), name="columns",
-    )(weights, first, second, first_in, second_in, forcing, deep, depth, diag, edge_rows)
+    )(weights, first, second, first_in, second_in, forcing, deep, depth, diag, edge_rows, part_one)
     row_first_in, row_second_in = swap_both(row_first, row_second, "by", n_by, False)
-    part_one, part_two = pl.pallas_call(
-        tracers_kernel,
-        out_shape=(block, block),
-        in_specs=[VMEM] * 8,
-        out_specs=(VMEM,) * 2,
-        scratch_shapes=[flat_int] * 2 + [pltpu.VMEM((2 * SLOT, COLS), F32)],
-        compiler_params=PARAMS, cost_estimate=cost(60 * cells, 20 * cells), name="tracers",
-    )(weights, one, two, east, north, deep, flux_left, flux_right)
-    zero, one, two, sums, new_one, new_two = pl.pallas_call(
+    inner_one, inner_two, edge_one, edge_two = pl.pallas_call(
+        edges_kernel,
+        out_shape=(block, block, block, block),
+        in_specs=[VMEM] * 4,
+        out_specs=(HBM,) * 2 + (VMEM,) * 2,
+        scratch_shapes=[pltpu.SemaphoreType.DMA((2, ROWS // CHUNK))],
+        compiler_params=PARAMS, cost_estimate=cost(10 * cells, 10 * cells), name="edges",
+    )(flux_left, flux_right, part_one, part_two)
+    v_0, v_1, v_2, sums, flux_rows = pl.pallas_call(
         solver_kernel,
-        out_shape=(plane, plane, plane, shape(128, 128), block, block),
-        in_specs=[VMEM] * 10,
-        out_specs=(VMEM,) * 4 + (HBM,) * 2,
-        scratch_shapes=[pltpu.VMEM((4, LEV, 8, COLS), F32), pltpu.SemaphoreType.DMA((6,))],
+        out_shape=(plane, plane, plane, shape(128, 128), shape(4 * SLOT, COLS)),
+        in_specs=[VMEM] * 8 + [HBM],
+        out_specs=(VMEM,) * 5,
         compiler_params=PARAMS, cost_estimate=cost(4 * 10**6, 10**6), name="solver",
-    )(weights, row_first, row_second, row_first_in, row_second_in, forcing, depth, diag, part_one, part_two)
+    )(weights, row_first, row_second, row_first_in, row_second_in, forcing, depth, diag, edge_one)
     sums = lax.all_to_all(sums[:n_by * n_bx], ("by", "bx"), 0, 0, tiled=True)
-    surface = pl.pallas_call(
-        surface_kernel, out_shape=plane, in_specs=[VMEM] * 4, out_specs=VMEM,
+    surface, new_one, new_two = pl.pallas_call(
+        surface_kernel,
+        out_shape=(plane, block, block),
+        in_specs=[VMEM] * 7 + [HBM] * 2,
+        out_specs=(HBM,) * 3,
+        input_output_aliases={7: 1, 8: 2},
+        scratch_shapes=[flat, pltpu.VMEM((4, LEV, 8, COLS), F32), pltpu.SemaphoreType.DMA((7,))],
         compiler_params=PARAMS, cost_estimate=cost(10**5, 10**5), name="surface",
-    )(sums, zero, one, two)
+    )(sums, v_0, v_1, v_2, flux_rows, edge_one, edge_two, inner_one, inner_two)
     return new_one, new_two, surface
 
 

time: 44.1 us -> 42 us (0.952)
  blocking collectives: 17.5 us -> 16.7 us
  starting transfers between devices: 12.4 us -> 11.6 us
  Pallas kernels: 11.8 us -> 11.1 us
    pallas_call x1 -> x2, Pallas kernels: 1.08 us -> 2.62 us  [the longest x1 1.38 us: on_device(): pl.pallas_call(edges_kernel, out_shape=(block, block, block, block), in_s...]
    pallas_call x1, Pallas kernels: 2 us -> 0.72 us  [on_device(): pl.pallas_call(solver_kernel, out_shape=(plane, plane, plane, shape(128,...]
    pallas_call x1, Pallas kernels: 4.39 us -> 3.41 us  [on_device(): pl.pallas_call(tracers_kernel, out_shape=(block, block), in_specs=[VMEM]...]
    ppermute x2, starting transfers between devices: 4.73 us -> 3.86 us  [swap_both(): lax.ppermute(first, axis, pairs(size, False, wrap))]
    all_to_all x1, blocking collectives: 17.5 us -> 16.7 us  [on_device(): sums = lax.all_to_all(sums[:n_by * n_bx], ('by', 'bx'), 0, 0, tiled=True)]
  transfers between devices with their start and end apart: 4 -> 4, of which waited for: 1 -> 1; matrix products, arithmetic and copies ran while one was open for 0% -> 0% of each run, Pallas kernels for 10% -> 11%
where the time goes in v4:
time: 42 us; the launch traced here: 41.9 us
  blocking collectives  16.7 us (40%)
  starting transfers between devices  11.6 us (28%)
  Pallas kernels  11.1 us (26%)
  waiting for transfers between devices  1.77 us (4%)
  between operations  0.71 us (2%)
    all_to_all x1, blocking collectives, on_device(): sums = lax.all_to_all(sums[:n_by * n_bx], ('by', 'bx'), 0, 0, tiled=True)  16.7 us
    ppermute x2, starting transfers between devices, swap_both(): lax.ppermute(second, axis, pairs(size, True, wrap))  7.71 us
    pallas_call x1, Pallas kernels, on_device(): pl.pallas_call(forcing_kernel, out_shape=(column_message, column_message,...  4.02 us
    ppermute x2, starting transfers between devices, swap_both(): lax.ppermute(first, axis, pairs(size, False, wrap))  3.86 us
    pallas_call x1, Pallas kernels, on_device(): pl.pallas_call(tracers_kernel, out_shape=(block, block), in_specs=[VMEM]...  3.41 us
    ppermute x2, waiting for transfers between devices, swap_both(): lax.ppermute(second, axis, pairs(size, True, wrap))  1.77 us
    pallas_call x1, Pallas kernels, on_device(): pl.pallas_call(edges_kernel, out_shape=(block, block, block, block), in_s...  1.38 us
    pallas_call x1, Pallas kernels, on_device(): pl.pallas_call(surface_kernel, out_shape=(plane, block, block), in_specs=...  1.24 us
  transfers between devices with their start and end apart: 4, of which 1 were waited for; matrix products, arithmetic and copies ran while one was open for 0% of the time, Pallas kernels for 11%

profile of v4, /device:TPU:1, one launch (start us, length us, event | category | flops | bytes accessed | tf_op | source)
XLA Modules:
  0.0 41.9 jit_solution(10216654643020453047)
XLA Ops:
  0.6 4.0 %forcing.1 = (f32[88,128]{1,0:T(8,128)S(1)}, f32[88,128]{1,0:T(8,128)S(1)}, f32[64,256]{1,0:T(8,128)S(1)}, f32[64,256]{1,0:T(8,128)S(1)}, f32[64,256]{1,0:T(8,12...) custom-call(f32[18]{0:T(128)} %side_hbm.1, ...), custom_call_target="tpu_custom_call" | custom-call | flops 8847360 | bytes 3538944 | tf_op jit(solution)/shard_map/forcing/pallas_call | solution.py:440
  4.7 2.5 %collective-permute-start = (f32[88,128]{1,0:T(8,128)S(1)}, f32[88,128]{1,0:T(8,128)S(1)}, u32[]{:S(2)}, u32[]{:S(2)}) collective-permute-start(f32[88,128]{1,0:T(8,128)S(1)} %get-tuple-element.37.first), channel_id=1, source_target_pairs={{0,1},{1,0},{2,3},{3,2},{4,5},{5,4},{6,7},{7,6},{8,9},{9,8},{10,11... | collective-permute-start | bytes 135176 | tf_op jit(solution)/shard_map/ppermute | solution.py:43
  7.2 4.7 %collective-permute-start.1 = (f32[88,128]{1,0:T(8,128)S(1)}, f32[88,128]{1,0:T(8,128)S(1)}, u32[]{:S(2)}, u32[]{:S(2)}) collective-permute-start(f32[88,128]{1,0:T(8,128)S(1)} %get-tuple-element.38.second), channel_id=1, source_target_pairs={{1,2},{2,1},{3,4},{4,3},{5,6},{6,5},{7,8},{8,7},{9,10},{10,9},{11,... | collective-permute-start | bytes 135176 | tf_op jit(solution)/shard_map/ppermute | solution.py:44
  11.9 3.4 %tracers.1 = (f32[18,64,256]{2,1,0:T(8,128)S(1)}, f32[18,64,256]{2,1,0:T(8,128)S(1)}) custom-call(f32[88,256]{1,0:T(8,128)S(1)} %get-tuple-element.36.weights, f32[18,72,256]{2,1,0:T(8,128)S(1)} %get-tuple-element.44.one, f32[18,72,256]{2,1,0:T(8,128)S(1)} %get-tuple-element.45.two, bf16[18,64,256]{2,1,0:T(8,128)(2,1)S(1)} %get-tuple-element.46.east, ...), custom_call_target="tpu_custom_call" | custom-call | flops 17694720 | bytes 5898240 | tf_op jit(solution)/shard_map/tracers/pallas_call | solution.py:450
  15.3 0.0 collective-permute-done.first_in
  15.3 0.0 collective-permute-done.1.second_in
  15.3 0.3 columns.1
  15.6 1.3 %collective-permute-start.2 = (f32[80,384]{1,0:T(8,128)S(1)}, f32[80,384]{1,0:T(8,128)S(1)}, u32[]{:S(2)}, u32[]{:S(2)}) collective-permute-start(f32[80,384]{1,0:T(8,128)S(1)} %get-tuple-element.49.first), channel_id=1, source_target_pairs={{0,16},{16,0},{32,48},{48,32},{64,80},{80,64},{96,112},{112,96},{1... | collective-permute-start | bytes 368648 | tf_op jit(solution)/shard_map/ppermute | solution.py:43
  17.0 3.0 %collective-permute-start.3 = (f32[80,384]{1,0:T(8,128)S(1)}, f32[80,384]{1,0:T(8,128)S(1)}, u32[]{:S(2)}, u32[]{:S(2)}) collective-permute-start(f32[80,384]{1,0:T(8,128)S(1)} %get-tuple-element.50.second), channel_id=1, source_target_pairs={{16,32},{32,16},{48,64},{64,48},{80,96},{96,80},{17,33},{33,17},{4... | collective-permute-start | bytes 368648 | tf_op jit(solution)/shard_map/ppermute | solution.py:44
  20.0 1.4 %edges.1 = (f32[18,64,256]{2,1,0:T(8,128)}, f32[18,64,256]{2,1,0:T(8,128)}, f32[18,64,256]{2,1,0:T(8,128)S(1)}, f32[18,64,256]{2,1,0:T(8,128)S(1)}) custom-call(f32[64,128]{1,0:T(8,128)S(1)} %get-tuple-element.54.flux_left, f32[64,128]{1,0:T(8,128)S(1)} %get-tuple-element.55.flux_right, f32[18,64,256]{2,1,0:T(8,128)S(1)} %get-tuple-element.48.after.part_one, ...), custom_call_target="tpu_custom_call" | custom-call | flops 2949120 | bytes 2949120 | tf_op jit(solution)/shard_map/edges/pallas_call | solution.py:467
  21.4 0.0 collective-permute-done.2.first_in
  21.4 1.8 %collective-permute-done.3.second_in = f32[80,384]{1,0:T(8,128)S(1)} collective-permute-done((f32[80,384]{1,0:T(8,128)S(1)}, f32[80,384]{1,0:T(8,128)S(1)}, u32[]{:S(2)}, u32[]{:S(2)}) %collective-permute-start.3) | collective-permute-done | bytes 122912 | tf_op jit(solution)/shard_map/ppermute | solution.py:44
  23.1 0.7 %solver.1 = (f32[64,256]{1,0:T(8,128)S(1)}, f32[64,256]{1,0:T(8,128)S(1)}, f32[64,256]{1,0:T(8,128)S(1)}, f32[128,128]{1,0:T(8,128)S(1)}, f32[96,256]{1,0:T(8,128)S(1)}) custom-call(f32[88,256]{1,0:T(8,128)S(1)} %get-tuple-element.36.weights, f32[80,384]{1,0:T(8,128)S(1)} %get-tuple-element.49.first, f32[80,384]{1,0:T(8,128)S(1)} %get-tuple-element.50.second, ...), custom_call_target="tpu_custom_call" | custom-call | flops 4000000 | bytes 1000000 | tf_op jit(solution)/shard_map/solver/pallas_call | solution.py:475
  23.9 16.7 %all_to_all.11 = f32[128,1,128]{2,1,0:T(1,128)S(1)} all-to-all(f32[128,1,128]{2,1,0:T(1,128)S(1)} %bitcast.5), channel_id=1, replica_groups=mesh['by'=8,'bx'=16] {'by','bx'}, dimensions={0} | all-to-all | bytes 131072 | tf_op jit(solution)/shard_map/all_to_all | solution.py:482
  40.6 1.2 %surface.1 = (f32[64,256]{1,0:T(8,128)}, f32[18,64,256]{2,1,0:T(8,128)}, f32[18,64,256]{2,1,0:T(8,128)}) custom-call(f32[128,128]{1,0:T(8,128)S(1)} %bitcast.4, f32[64,256]{1,0:T(8,128)S(1)} %get-tuple-element.59.zero, f32[64,256]{1,0:T(8,128)S(1)} %get-tuple-element.60.one, ...), custom_call_target="tpu_custom_call", output_to_operand_aliasing={{1}: (7, {}), {2}: (8, {})} | custom-call | flops 100000 | bytes 100000 | tf_op jit(solution)/shard_map/surface/pallas_call | solution.py:483
Async XLA Ops:
  4.7 10.7 %collective-permute-start = (f32[88,128]{1,0:T(8,128)S(1)}, f32[88,128]{1,0:T(8,128)S(1)}, u32[]{:S(2)}, u32[]{:S(2)}) collective-permute-start(f32[88,128]{1,0:T(8,128)S(1)} %get-tuple-element.37.first), channel_id=1, source_target_pairs={{0,1},{1,0},{2,3},{3,2},{4,5},{5,4},{6,7},{7,6},{8,9},{9,8},{10,11... | collective-permute-start | bytes 135176 | tf_op jit(solution)/shard_map/ppermute | solution.py:43
  7.2 8.1 %collective-permute-start.1 = (f32[88,128]{1,0:T(8,128)S(1)}, f32[88,128]{1,0:T(8,128)S(1)}, u32[]{:S(2)}, u32[]{:S(2)}) collective-permute-start(f32[88,128]{1,0:T(8,128)S(1)} %get-tuple-element.38.second), channel_id=1, source_target_pairs={{1,2},{2,1},{3,4},{4,3},{5,6},{6,5},{7,8},{8,7},{9,10},{10,9},{11,... | collective-permute-start | bytes 135176 | tf_op jit(solution)/shard_map/ppermute | solution.py:44
  15.6 5.7 %collective-permute-start.2 = (f32[80,384]{1,0:T(8,128)S(1)}, f32[80,384]{1,0:T(8,128)S(1)}, u32[]{:S(2)}, u32[]{:S(2)}) collective-permute-start(f32[80,384]{1,0:T(8,128)S(1)} %get-tuple-element.49.first), channel_id=1, source_target_pairs={{0,16},{16,0},{32,48},{48,32},{64,80},{80,64},{96,112},{112,96},{1... | collective-permute-start | bytes 368648 | tf_op jit(solution)/shard_map/ppermute | solution.py:43
  17.0 6.2 %collective-permute-start.3 = (f32[80,384]{1,0:T(8,128)S(1)}, f32[80,384]{1,0:T(8,128)S(1)}, u32[]{:S(2)}, u32[]{:S(2)}) collective-permute-start(f32[80,384]{1,0:T(8,128)S(1)} %get-tuple-element.50.second), channel_id=1, source_target_pairs={{16,32},{32,16},{48,64},{64,48},{80,96},{96,80},{17,33},{33,17},{4... | collective-permute-start | bytes 368648 | tf_op jit(solution)/shard_map/ppermute | solution.py:44

commit v5 on v4

--- a/solution.py
+++ b/solution.py
@@ -117,11 +117,12 @@
             e_sum = e_sum + jnp.where(to_east > k, flow_e * (both + nxt) - mix * (nxt - both), 0.0)
             nxt = jnp.where(row == CHUNK - 1, beyond, pltpu.roll(both, CHUNK - 1, 0))
             n_sum = n_sum + jnp.where(to_north > k, flow_n * (both + nxt) - mix * (nxt - both), 0.0)
-            to_right = jnp.where(lane == k, c_one[:, COLS - 1:], to_right)
-            to_right = jnp.where(lane == k + LEV, c_two[:, COLS - 1:], to_right)
-            to_right = jnp.where((lane == k + 2 * LEV) | (lane == k + 3 * LEV), flow_e[:, COLS - 1:], to_right)
-            to_left = jnp.where(lane == k + 64, c_one[:, :1], to_left)
-            to_left = jnp.where(lane == k + 64 + LEV, c_two[:, :1], to_left)
+            for i, value in enumerate((c_one, c_two, flow_e)):
+                at = k + i * LEV
+                to_right = jnp.where(lane == at, pltpu.roll(value[:, COLS - 128:], at + 1, 1), to_right)
+            for i, value in enumerate((c_one, c_two)):
+                at = k + i * LEV + 64
+                to_left = jnp.where(lane == at, pltpu.roll(value[:, :128], at, 1), to_left)
             return e_sum, n_sum, total, to_right, to_left
 
         flat, tile = jnp.zeros((CHUNK, COLS), F32), jnp.zeros((CHUNK, 128), F32)
@@ -154,6 +155,7 @@
     deep_out[...], depth_out[...], diag_out[...] = fields[3], fields[1], fields[2]
     to_right, to_left = right[...], left[...]
     lane = iota((ROWS, 128), 1)
+    to_right = jnp.where((lane >= 3 * LEV) & (lane < 4 * LEV), pltpu.roll(to_right, LEV, 1), to_right)
     for i, field in enumerate(fields):
         tile = field[:, COLS - 128:]
         tile = pltpu.roll(tile, 128 - 2 * i, 1) if i else tile

time: 42 us -> 41.7 us (level)
  transfers between devices with their start and end apart: 4 -> 4, of which waited for: 1 -> 1; matrix products, arithmetic and copies ran while one was open for 0% -> 0% of each run, Pallas kernels for 11% -> 12%
where the time goes in v5:
time: 41.7 us; the launch traced here: 41.6 us
  blocking collectives  16.7 us (40%)
  starting transfers between devices  11.6 us (28%)
  Pallas kernels  10.8 us (26%)
  waiting for transfers between devices  1.77 us (4%)
  between operations  0.71 us (2%)
    all_to_all x1, blocking collectives, on_device(): sums = lax.all_to_all(sums[:n_by * n_bx], ('by', 'bx'), 0, 0, tiled=True)  16.7 us
    ppermute x2, starting transfers between devices, swap_both(): lax.ppermute(second, axis, pairs(size, True, wrap))  7.71 us
    ppermute x2, starting transfers between devices, swap_both(): lax.ppermute(first, axis, pairs(size, False, wrap))  3.86 us
    pallas_call x1, Pallas kernels, on_device(): pl.pallas_call(forcing_kernel, out_shape=(column_message, column_message,...  3.74 us
    pallas_call x1, Pallas kernels, on_device(): pl.pallas_call(tracers_kernel, out_shape=(block, block), in_specs=[VMEM]...  3.41 us
    ppermute x2, waiting for transfers between devices, swap_both(): lax.ppermute(second, axis, pairs(size, True, wrap))  1.77 us
    pallas_call x1, Pallas kernels, on_device(): pl.pallas_call(edges_kernel, out_shape=(block, block, block, block), in_s...  1.38 us
    pallas_call x1, Pallas kernels, on_device(): pl.pallas_call(surface_kernel, out_shape=(plane, block, block), in_specs=...  1.24 us
  transfers between devices with their start and end apart: 4, of which 1 were waited for; matrix products, arithmetic and copies ran while one was open for 0% of the time, Pallas kernels for 12%

profile of v5, /device:TPU:1, one launch (start us, length us, event | category | flops | bytes accessed | tf_op | source)
XLA Modules:
  0.0 41.6 jit_solution(2401573194523986703)
XLA Ops:
  0.6 3.7 %forcing.1 = (f32[88,128]{1,0:T(8,128)S(1)}, f32[88,128]{1,0:T(8,128)S(1)}, f32[64,256]{1,0:T(8,128)S(1)}, f32[64,256]{1,0:T(8,128)S(1)}, f32[64,256]{1,0:T(8,12...) custom-call(f32[18]{0:T(128)} %side_hbm.1, ...), custom_call_target="tpu_custom_call" | custom-call | flops 8847360 | bytes 3538944 | tf_op jit(solution)/shard_map/forcing/pallas_call | solution.py:442
  4.4 2.5 %collective-permute-start = (f32[88,128]{1,0:T(8,128)S(1)}, f32[88,128]{1,0:T(8,128)S(1)}, u32[]{:S(2)}, u32[]{:S(2)}) collective-permute-start(f32[88,128]{1,0:T(8,128)S(1)} %get-tuple-element.37.first), channel_id=1, source_target_pairs={{0,1},{1,0},{2,3},{3,2},{4,5},{5,4},{6,7},{7,6},{8,9},{9,8},{10,11... | collective-permute-start | bytes 135176 | tf_op jit(solution)/shard_map/ppermute | solution.py:43
  6.9 4.7 %collective-permute-start.1 = (f32[88,128]{1,0:T(8,128)S(1)}, f32[88,128]{1,0:T(8,128)S(1)}, u32[]{:S(2)}, u32[]{:S(2)}) collective-permute-start(f32[88,128]{1,0:T(8,128)S(1)} %get-tuple-element.38.second), channel_id=1, source_target_pairs={{1,2},{2,1},{3,4},{4,3},{5,6},{6,5},{7,8},{8,7},{9,10},{10,9},{11,... | collective-permute-start | bytes 135176 | tf_op jit(solution)/shard_map/ppermute | solution.py:44
  11.6 3.4 %tracers.1 = (f32[18,64,256]{2,1,0:T(8,128)S(1)}, f32[18,64,256]{2,1,0:T(8,128)S(1)}) custom-call(f32[88,256]{1,0:T(8,128)S(1)} %get-tuple-element.36.weights, f32[18,72,256]{2,1,0:T(8,128)S(1)} %get-tuple-element.44.one, f32[18,72,256]{2,1,0:T(8,128)S(1)} %get-tuple-element.45.two, bf16[18,64,256]{2,1,0:T(8,128)(2,1)S(1)} %get-tuple-element.46.east, ...), custom_call_target="tpu_custom_call" | custom-call | flops 17694720 | bytes 5898240 | tf_op jit(solution)/shard_map/tracers/pallas_call | solution.py:452
  15.0 0.0 collective-permute-done.first_in
  15.0 0.0 collective-permute-done.1.second_in
  15.1 0.3 columns.1
  15.4 1.3 %collective-permute-start.2 = (f32[80,384]{1,0:T(8,128)S(1)}, f32[80,384]{1,0:T(8,128)S(1)}, u32[]{:S(2)}, u32[]{:S(2)}) collective-permute-start(f32[80,384]{1,0:T(8,128)S(1)} %get-tuple-element.49.first), channel_id=1, source_target_pairs={{0,16},{16,0},{32,48},{48,32},{64,80},{80,64},{96,112},{112,96},{1... | collective-permute-start | bytes 368648 | tf_op jit(solution)/shard_map/ppermute | solution.py:43
  16.7 3.0 %collective-permute-start.3 = (f32[80,384]{1,0:T(8,128)S(1)}, f32[80,384]{1,0:T(8,128)S(1)}, u32[]{:S(2)}, u32[]{:S(2)}) collective-permute-start(f32[80,384]{1,0:T(8,128)S(1)} %get-tuple-element.50.second), channel_id=1, source_target_pairs={{16,32},{32,16},{48,64},{64,48},{80,96},{96,80},{17,33},{33,17},{4... | collective-permute-start | bytes 368648 | tf_op jit(solution)/shard_map/ppermute | solution.py:44
  19.7 1.4 %edges.1 = (f32[18,64,256]{2,1,0:T(8,128)}, f32[18,64,256]{2,1,0:T(8,128)}, f32[18,64,256]{2,1,0:T(8,128)S(1)}, f32[18,64,256]{2,1,0:T(8,128)S(1)}) custom-call(f32[64,128]{1,0:T(8,128)S(1)} %get-tuple-element.54.flux_left, f32[64,128]{1,0:T(8,128)S(1)} %get-tuple-element.55.flux_right, f32[18,64,256]{2,1,0:T(8,128)S(1)} %get-tuple-element.48.after.part_one, ...), custom_call_target="tpu_custom_call" | custom-call | flops 2949120 | bytes 2949120 | tf_op jit(solution)/shard_map/edges/pallas_call | solution.py:469
  21.1 0.0 collective-permute-done.2.first_in
  21.1 1.8 %collective-permute-done.3.second_in = f32[80,384]{1,0:T(8,128)S(1)} collective-permute-done((f32[80,384]{1,0:T(8,128)S(1)}, f32[80,384]{1,0:T(8,128)S(1)}, u32[]{:S(2)}, u32[]{:S(2)}) %collective-permute-start.3) | collective-permute-done | bytes 122912 | tf_op jit(solution)/shard_map/ppermute | solution.py:44
  22.9 0.7 %solver.1 = (f32[64,256]{1,0:T(8,128)S(1)}, f32[64,256]{1,0:T(8,128)S(1)}, f32[64,256]{1,0:T(8,128)S(1)}, f32[128,128]{1,0:T(8,128)S(1)}, f32[96,256]{1,0:T(8,128)S(1)}) custom-call(f32[88,256]{1,0:T(8,128)S(1)} %get-tuple-element.36.weights, f32[80,384]{1,0:T(8,128)S(1)} %get-tuple-element.49.first, f32[80,384]{1,0:T(8,128)S(1)} %get-tuple-element.50.second, ...), custom_call_target="tpu_custom_call" | custom-call | flops 4000000 | bytes 1000000 | tf_op jit(solution)/shard_map/solver/pallas_call | solution.py:477
  23.6 16.7 %all_to_all.11 = f32[128,1,128]{2,1,0:T(1,128)S(1)} all-to-all(f32[128,1,128]{2,1,0:T(1,128)S(1)} %bitcast.5), channel_id=1, replica_groups=mesh['by'=8,'bx'=16] {'by','bx'}, dimensions={0} | all-to-all | bytes 131072 | tf_op jit(solution)/shard_map/all_to_all | solution.py:484
  40.3 1.2 %surface.1 = (f32[64,256]{1,0:T(8,128)}, f32[18,64,256]{2,1,0:T(8,128)}, f32[18,64,256]{2,1,0:T(8,128)}) custom-call(f32[128,128]{1,0:T(8,128)S(1)} %bitcast.4, f32[64,256]{1,0:T(8,128)S(1)} %get-tuple-element.59.zero, f32[64,256]{1,0:T(8,128)S(1)} %get-tuple-element.60.one, ...), custom_call_target="tpu_custom_call", output_to_operand_aliasing={{1}: (7, {}), {2}: (8, {})} | custom-call | flops 100000 | bytes 100000 | tf_op jit(solution)/shard_map/surface/pallas_call | solution.py:485
Async XLA Ops:
  4.4 10.7 %collective-permute-start = (f32[88,128]{1,0:T(8,128)S(1)}, f32[88,128]{1,0:T(8,128)S(1)}, u32[]{:S(2)}, u32[]{:S(2)}) collective-permute-start(f32[88,128]{1,0:T(8,128)S(1)} %get-tuple-element.37.first), channel_id=1, source_target_pairs={{0,1},{1,0},{2,3},{3,2},{4,5},{5,4},{6,7},{7,6},{8,9},{9,8},{10,11... | collective-permute-start | bytes 135176 | tf_op jit(solution)/shard_map/ppermute | solution.py:43
  6.9 8.1 %collective-permute-start.1 = (f32[88,128]{1,0:T(8,128)S(1)}, f32[88,128]{1,0:T(8,128)S(1)}, u32[]{:S(2)}, u32[]{:S(2)}) collective-permute-start(f32[88,128]{1,0:T(8,128)S(1)} %get-tuple-element.38.second), channel_id=1, source_target_pairs={{1,2},{2,1},{3,4},{4,3},{5,6},{6,5},{7,8},{8,7},{9,10},{10,9},{11,... | collective-permute-start | bytes 135176 | tf_op jit(solution)/shard_map/ppermute | solution.py:44
  15.4 5.7 %collective-permute-start.2 = (f32[80,384]{1,0:T(8,128)S(1)}, f32[80,384]{1,0:T(8,128)S(1)}, u32[]{:S(2)}, u32[]{:S(2)}) collective-permute-start(f32[80,384]{1,0:T(8,128)S(1)} %get-tuple-element.49.first), channel_id=1, source_target_pairs={{0,16},{16,0},{32,48},{48,32},{64,80},{80,64},{96,112},{112,96},{1... | collective-permute-start | bytes 368648 | tf_op jit(solution)/shard_map/ppermute | solution.py:43
  16.7 6.2 %collective-permute-start.3 = (f32[80,384]{1,0:T(8,128)S(1)}, f32[80,384]{1,0:T(8,128)S(1)}, u32[]{:S(2)}, u32[]{:S(2)}) collective-permute-start(f32[80,384]{1,0:T(8,128)S(1)} %get-tuple-element.50.second), channel_id=1, source_target_pairs={{16,32},{32,16},{48,64},{64,48},{80,96},{96,80},{17,33},{33,17},{4... | collective-permute-start | bytes 368648 | tf_op jit(solution)/shard_map/ppermute | solution.py:44

commit v6 on v5

--- a/solution.py
+++ b/solution.py
@@ -7,7 +7,8 @@
 
 LEV = 18
 CHUNK = 16
-SLOT = 24
+SLOT = LEV
+BASE = 3 * SLOT
 ROWS, COLS = 64, 256
 WIDE = COLS + 128
 TALL = ROWS + 16
@@ -276,8 +277,8 @@
         two = flux(south[SLOT:2 * SLOT, :COLS], north[SLOT:2 * SLOT, :COLS])
         return jnp.sum(both * weight, axis=0, keepdims=True), both[:, :COLS] + 0.5 * two, two
 
-    top, top_one, top_two = face(own_up, above, own_up[74:75], above[75:76])
-    bottom, bottom_one, bottom_two = face(beneath, own_down, beneath[74:75], own_down[75:76])
+    top, top_one, top_two = face(own_up, above, own_up[BASE + 2:BASE + 3], above[BASE + 3:BASE + 4])
+    bottom, bottom_one, bottom_two = face(beneath, own_down, beneath[BASE + 2:BASE + 3], own_down[BASE + 3:BASE + 4])
 
     for i, flux in enumerate((bottom_one, bottom_two, top_one, top_two)):
         flux_rows[i * SLOT:(i + 1) * SLOT] = flux
@@ -288,14 +289,14 @@
     own_row = iota((ROWS, WIDE), 0)
     mine = forcing[...] + jnp.where(own_row == 0, bottom, jnp.where(own_row == ROWS - 1, -top, 0.0))
     field = jnp.concatenate([
-        jnp.concatenate([blank(6), beneath[72:73], beneath[73:74] - bottom], axis=0), mine,
-        jnp.concatenate([above[72:73] + top, above[73:75], blank(5)], axis=0)], axis=0)
+        jnp.concatenate([blank(6), beneath[BASE:BASE + 1], beneath[BASE + 1:BASE + 2] - bottom], axis=0), mine,
+        jnp.concatenate([above[BASE:BASE + 1] + top, above[BASE + 1:BASE + 3], blank(5)], axis=0)], axis=0)
     half_depth = 0.5 * jnp.concatenate([
-        jnp.concatenate([blank(6), beneath[75:77]], axis=0), depth[...],
-        jnp.concatenate([above[76:78], blank(6)], axis=0)], axis=0)
+        jnp.concatenate([blank(6), beneath[BASE + 3:BASE + 5]], axis=0), depth[...],
+        jnp.concatenate([above[BASE + 4:BASE + 6], blank(6)], axis=0)], axis=0)
     diag_all = jnp.concatenate([
-        jnp.concatenate([blank(7), beneath[77:78]], axis=0), diag[...],
-        jnp.concatenate([above[78:80], blank(6)], axis=0)], axis=0)
+        jnp.concatenate([blank(7), beneath[BASE + 5:BASE + 6]], axis=0), diag[...],
+        jnp.concatenate([above[BASE + 6:BASE + 8], blank(6)], axis=0)], axis=0)
     last = lax.axis_index("by") == lax.axis_size("by") - 1
     inside = iota((TALL, WIDE), 0) < jnp.where(last, ROWS + 8, TALL)
 
@@ -435,7 +436,7 @@
     plane, wide, tile = shape(ROWS, COLS), shape(ROWS, WIDE), shape(ROWS, 128)
     block, taller = shape(LEV, ROWS, COLS), shape(LEV, ROWS + 8, COLS)
     half = jax.ShapeDtypeStruct((LEV, ROWS, COLS), jnp.bfloat16)
-    column_message, row_message = shape(ROWS + SLOT, 128), shape(3 * SLOT + 8, WIDE)
+    column_message, row_message = shape(ROWS + SLOT, 128), shape(BASE + 8, WIDE)
     flat, flat_int = pltpu.VMEM((ROWS, COLS), F32), pltpu.VMEM((ROWS, COLS), jnp.int32)
     level_list = pltpu.SMEM((LEV,), F32)
     transfers = pltpu.SemaphoreType.DMA((4, ROWS // CHUNK))

time: 41.7 us -> 41.5 us (level)
  no operation moved by 1% of the time
where the time goes in v6:
time: 41.5 us; the launch traced here: 41.3 us
  blocking collectives  16.8 us (40%)
  starting transfers between devices  11.6 us (28%)
  Pallas kernels  10.8 us (26%)
  waiting for transfers between devices  1.51 us (4%)
  between operations  0.7 us (2%)
    all_to_all x1, blocking collectives, on_device(): sums = lax.all_to_all(sums[:n_by * n_bx], ('by', 'bx'), 0, 0, tiled=True)  16.8 us
    ppermute x2, starting transfers between devices, swap_both(): lax.ppermute(second, axis, pairs(size, True, wrap))  7.71 us
    ppermute x2, starting transfers between devices, swap_both(): lax.ppermute(first, axis, pairs(size, False, wrap))  3.86 us
    pallas_call x1, Pallas kernels, on_device(): pl.pallas_call(forcing_kernel, out_shape=(column_message, column_message,...  3.73 us
    pallas_call x1, Pallas kernels, on_device(): pl.pallas_call(tracers_kernel, out_shape=(block, block), in_specs=[VMEM]...  3.39 us
    ppermute x2, waiting for transfers between devices, swap_both(): lax.ppermute(second, axis, pairs(size, True, wrap))  1.5 us
    pallas_call x1, Pallas kernels, on_device(): pl.pallas_call(edges_kernel, out_shape=(block, block, block, block), in_s...  1.38 us
    pallas_call x1, Pallas kernels, on_device(): pl.pallas_call(surface_kernel, out_shape=(plane, block, block), in_specs=...  1.24 us
  transfers between devices with their start and end apart: 4, of which 1 were waited for; matrix products, arithmetic and copies ran while one was open for 0% of the time, Pallas kernels for 12%

profile of v6, /device:TPU:1, one launch (start us, length us, event | category | flops | bytes accessed | tf_op | source)
XLA Modules:
  0.0 41.3 jit_solution(7185553062861882340)
XLA Ops:
  0.6 3.7 %forcing.1 = (f32[82,128]{1,0:T(8,128)S(1)}, f32[82,128]{1,0:T(8,128)S(1)}, f32[64,256]{1,0:T(8,128)S(1)}, f32[64,256]{1,0:T(8,128)S(1)}, f32[64,256]{1,0:T(8,12...) custom-call(f32[18]{0:T(128)} %side_hbm.1, ...), custom_call_target="tpu_custom_call" | custom-call | flops 8847360 | bytes 3538944 | tf_op jit(solution)/shard_map/forcing/pallas_call | solution.py:443
  4.4 2.5 %collective-permute-start = (f32[82,128]{1,0:T(8,128)S(1)}, f32[82,128]{1,0:T(8,128)S(1)}, u32[]{:S(2)}, u32[]{:S(2)}) collective-permute-start(f32[82,128]{1,0:T(8,128)S(1)} %get-tuple-element.37.first), channel_id=1, source_target_pairs={{0,1},{1,0},{2,3},{3,2},{4,5},{5,4},{6,7},{7,6},{8,9},{9,8},{10,11... | collective-permute-start | bytes 125960 | tf_op jit(solution)/shard_map/ppermute | solution.py:44
  6.9 4.7 %collective-permute-start.1 = (f32[82,128]{1,0:T(8,128)S(1)}, f32[82,128]{1,0:T(8,128)S(1)}, u32[]{:S(2)}, u32[]{:S(2)}) collective-permute-start(f32[82,128]{1,0:T(8,128)S(1)} %get-tuple-element.38.second), channel_id=1, source_target_pairs={{1,2},{2,1},{3,4},{4,3},{5,6},{6,5},{7,8},{8,7},{9,10},{10,9},{11,... | collective-permute-start | bytes 125960 | tf_op jit(solution)/shard_map/ppermute | solution.py:45
  11.6 3.4 %tracers.1 = (f32[18,64,256]{2,1,0:T(8,128)S(1)}, f32[18,64,256]{2,1,0:T(8,128)S(1)}) custom-call(f32[70,256]{1,0:T(8,128)S(1)} %get-tuple-element.36.weights, f32[18,72,256]{2,1,0:T(8,128)S(1)} %get-tuple-element.44.one, f32[18,72,256]{2,1,0:T(8,128)S(1)} %get-tuple-element.45.two, bf16[18,64,256]{2,1,0:T(8,128)(2,1)S(1)} %get-tuple-element.46.east, ...), custom_call_target="tpu_custom_call" | custom-call | flops 17694720 | bytes 5898240 | tf_op jit(solution)/shard_map/tracers/pallas_call | solution.py:453
  15.0 0.0 collective-permute-done.first_in
  15.0 0.0 collective-permute-done.1.second_in
  15.0 0.3 columns.1
  15.3 1.3 %collective-permute-start.2 = (f32[62,384]{1,0:T(8,128)S(1)}, f32[62,384]{1,0:T(8,128)S(1)}, u32[]{:S(2)}, u32[]{:S(2)}) collective-permute-start(f32[62,384]{1,0:T(8,128)S(1)} %get-tuple-element.49.first), channel_id=1, source_target_pairs={{0,16},{16,0},{32,48},{48,32},{64,80},{80,64},{96,112},{112,96},{1... | collective-permute-start | bytes 285704 | tf_op jit(solution)/shard_map/ppermute | solution.py:44
  16.6 3.0 %collective-permute-start.3 = (f32[62,384]{1,0:T(8,128)S(1)}, f32[62,384]{1,0:T(8,128)S(1)}, u32[]{:S(2)}, u32[]{:S(2)}) collective-permute-start(f32[62,384]{1,0:T(8,128)S(1)} %get-tuple-element.50.second), channel_id=1, source_target_pairs={{16,32},{32,16},{48,64},{64,48},{80,96},{96,80},{17,33},{33,17},{4... | collective-permute-start | bytes 285704 | tf_op jit(solution)/shard_map/ppermute | solution.py:45
  19.7 1.4 %edges.1 = (f32[18,64,256]{2,1,0:T(8,128)}, f32[18,64,256]{2,1,0:T(8,128)}, f32[18,64,256]{2,1,0:T(8,128)S(1)}, f32[18,64,256]{2,1,0:T(8,128)S(1)}) custom-call(f32[64,128]{1,0:T(8,128)S(1)} %get-tuple-element.54.flux_left, f32[64,128]{1,0:T(8,128)S(1)} %get-tuple-element.55.flux_right, f32[18,64,256]{2,1,0:T(8,128)S(1)} %get-tuple-element.48.after.part_one, ...), custom_call_target="tpu_custom_call" | custom-call | flops 2949120 | bytes 2949120 | tf_op jit(solution)/shard_map/edges/pallas_call | solution.py:470
  21.1 0.0 collective-permute-done.2.first_in
  21.1 1.5 %collective-permute-done.3.second_in = f32[62,384]{1,0:T(8,128)S(1)} collective-permute-done((f32[62,384]{1,0:T(8,128)S(1)}, f32[62,384]{1,0:T(8,128)S(1)}, u32[]{:S(2)}, u32[]{:S(2)}) %collective-permute-start.3) | collective-permute-done | bytes 95264 | tf_op jit(solution)/shard_map/ppermute | solution.py:45
  22.6 0.7 %solver.1 = (f32[64,256]{1,0:T(8,128)S(1)}, f32[64,256]{1,0:T(8,128)S(1)}, f32[64,256]{1,0:T(8,128)S(1)}, f32[128,128]{1,0:T(8,128)S(1)}, f32[72,256]{1,0:T(8,128)S(1)}) custom-call(f32[70,256]{1,0:T(8,128)S(1)} %get-tuple-element.36.weights, f32[62,384]{1,0:T(8,128)S(1)} %get-tuple-element.49.first, f32[62,384]{1,0:T(8,128)S(1)} %get-tuple-element.50.second, ...), custom_call_target="tpu_custom_call" | custom-call | flops 4000000 | bytes 1000000 | tf_op jit(solution)/shard_map/solver/pallas_call | solution.py:478
  23.3 16.8 %all_to_all.11 = f32[128,1,128]{2,1,0:T(1,128)S(1)} all-to-all(f32[128,1,128]{2,1,0:T(1,128)S(1)} %bitcast.5), channel_id=1, replica_groups=mesh['by'=8,'bx'=16] {'by','bx'}, dimensions={0} | all-to-all | bytes 131072 | tf_op jit(solution)/shard_map/all_to_all | solution.py:485
  40.1 1.2 %surface.1 = (f32[64,256]{1,0:T(8,128)}, f32[18,64,256]{2,1,0:T(8,128)}, f32[18,64,256]{2,1,0:T(8,128)}) custom-call(f32[128,128]{1,0:T(8,128)S(1)} %bitcast.4, f32[64,256]{1,0:T(8,128)S(1)} %get-tuple-element.59.zero, f32[64,256]{1,0:T(8,128)S(1)} %get-tuple-element.60.one, ...), custom_call_target="tpu_custom_call", output_to_operand_aliasing={{1}: (7, {}), {2}: (8, {})} | custom-call | flops 100000 | bytes 100000 | tf_op jit(solution)/shard_map/surface/pallas_call | solution.py:486
Async XLA Ops:
  4.4 10.6 %collective-permute-start = (f32[82,128]{1,0:T(8,128)S(1)}, f32[82,128]{1,0:T(8,128)S(1)}, u32[]{:S(2)}, u32[]{:S(2)}) collective-permute-start(f32[82,128]{1,0:T(8,128)S(1)} %get-tuple-element.37.first), channel_id=1, source_target_pairs={{0,1},{1,0},{2,3},{3,2},{4,5},{5,4},{6,7},{7,6},{8,9},{9,8},{10,11... | collective-permute-start | bytes 125960 | tf_op jit(solution)/shard_map/ppermute | solution.py:44
  6.9 8.1 %collective-permute-start.1 = (f32[82,128]{1,0:T(8,128)S(1)}, f32[82,128]{1,0:T(8,128)S(1)}, u32[]{:S(2)}, u32[]{:S(2)}) collective-permute-start(f32[82,128]{1,0:T(8,128)S(1)} %get-tuple-element.38.second), channel_id=1, source_target_pairs={{1,2},{2,1},{3,4},{4,3},{5,6},{6,5},{7,8},{8,7},{9,10},{10,9},{11,... | collective-permute-start | bytes 125960 | tf_op jit(solution)/shard_map/ppermute | solution.py:45
  15.3 5.7 %collective-permute-start.2 = (f32[62,384]{1,0:T(8,128)S(1)}, f32[62,384]{1,0:T(8,128)S(1)}, u32[]{:S(2)}, u32[]{:S(2)}) collective-permute-start(f32[62,384]{1,0:T(8,128)S(1)} %get-tuple-element.49.first), channel_id=1, source_target_pairs={{0,16},{16,0},{32,48},{48,32},{64,80},{80,64},{96,112},{112,96},{1... | collective-permute-start | bytes 285704 | tf_op jit(solution)/shard_map/ppermute | solution.py:44
  16.6 5.9 %collective-permute-start.3 = (f32[62,384]{1,0:T(8,128)S(1)}, f32[62,384]{1,0:T(8,128)S(1)}, u32[]{:S(2)}, u32[]{:S(2)}) collective-permute-start(f32[62,384]{1,0:T(8,128)S(1)} %get-tuple-element.50.second), channel_id=1, source_target_pairs={{16,32},{32,16},{48,64},{64,48},{80,96},{96,80},{17,33},{33,17},{4... | collective-permute-start | bytes 285704 | tf_op jit(solution)/shard_map/ppermute | solution.py:45
